TPU v7x, 32 devices: a whole 2x2x4 slice. The times are simulated.
32 devices in a mesh: wide: 8 (over z, x), narrow: 4 (over y, core).
Axes of the slice: x: 2, y: 2, z: 4, core: 2. Of those that a mesh axis runs over, the one named last changes fastest.
Arguments:
- tokens: bfloat16 [4096, 960], P('wide'), may hold values from -6 to 6
- attn_in: bfloat16 [5, 960, 320], replicated, may hold values from -0.1875 to 0.1875
- attn_out: bfloat16 [5, 192, 960], replicated, may hold values from -0.5 to 0.5
- gate_weight: bfloat16 [960, 2560], P(None, 'narrow'), may hold values from -0.1875 to 0.1875
- up_weight: bfloat16 [960, 2560], P(None, 'narrow'), may hold values from -0.1875 to 0.1875
- down_weight: bfloat16 [2560, 960], P('narrow'), may hold values from -0.125 to 0.125
- attn_gain: float32 [960], replicated, may hold values from 0.5 to 1.5
- ffn_gain: float32 [960], replicated, may hold values from 0.5 to 1.5
- cotangent: bfloat16 [4096, 960], P('wide'), may hold values from -6 to 6
- seq_ids: int32 [4096], P('wide'), may hold values from 0 to 4, as said below
- positions: int32 [4096], P('wide'), may hold values from 0 to 2046, as said below
- valid_mask: int32 [4096], P('wide'), may hold values from 0 to 1, as said below
- group_owner: int32 [5], replicated, may hold values from 0 to 3, as said below
Outputs:
- layer_out: bfloat16 [4096, 960], P('wide')
- grad_tokens: bfloat16 [4096, 960], P('wide')
- grad_attn_in: float32 [8, 960, 320], P('narrow')
- grad_attn_out: float32 [8, 192, 960], P('narrow')
- grad_gate: float32 [960, 2560], P(None, 'narrow')
- grad_up: float32 [960, 2560], P(None, 'narrow')
- grad_down: float32 [2560, 960], P('narrow')
- grad_attn_gain: float32 [960], replicated
- grad_ffn_gain: float32 [960], replicated
Inputs may be any that keep to these rules, and one draw needn't show every extreme that they name: `seq_ids`: on each wide member's 512 tokens the id never falls; tokens with equal id on one member form one sequence; id 4 marks padding at the end of a member's tokens, at most 64 of them; in every draw some member holds a single sequence of 512 tokens. Within a sequence the positions rise by one from token to token, from that sequence's own offset. `valid_mask`: padding tokens are 0; about one in ten of the other tokens is 0. `group_owner`: each of the 4 narrow members holds one or two groups; exactly one holds two.
All inputs are finite; a program needn't handle non-finite values.
Results may differ from a plain program's by a relative error of at most 0.019.
Values sent between devices are 32-bit elements; how exact they have to be, the bound alone decides.
No kernel may reach another device: no remote copies, remote signals or barrier semaphores. Data moves between devices by JAX's collectives and lax.ppermute only.
A program may use at most 128 MiB of HBM per device.

v0:
```python
import math

import jax
import jax.numpy as jnp
from jax import lax
from jax.sharding import PartitionSpec as P

HEAD = 64
Q_PER = 3
SLOTS = 2
LAYERS = 2


EPS = 1e-05
THETA = 10000.0
block_limit = 512


def rope_tables(positions, half_width):
    powers = -jnp.arange(half_width, dtype=jnp.float32) / half_width
    frequency = THETA**powers
    angles = positions.astype(jnp.float32)[:, None] * frequency[None, :]
    return (jnp.cos(angles), jnp.sin(angles))


def rotate(vector, cosine, sine):
    half_width = vector.shape[-1] // 2
    first_half = vector[..., :half_width]
    second_half = vector[..., half_width:]
    return jnp.concatenate(
        [first_half * cosine - second_half * sine, second_half * cosine + first_half * sine],
        axis=-1,
    )


def unrotate(grad_vec, cosine, sine):
    half_width = grad_vec.shape[-1] // 2
    first_half = grad_vec[..., :half_width]
    second_half = grad_vec[..., half_width:]
    return jnp.concatenate(
        [first_half * cosine + second_half * sine, second_half * cosine - first_half * sine],
        axis=-1,
    )


def norm_forward(stream, gain):
    factor = lax.rsqrt(jnp.mean(stream * stream, axis=-1, keepdims=True) + EPS)
    scaled = stream * factor
    return ((scaled * gain).astype(jnp.bfloat16), scaled, factor)


def norm_backward(grad_normed, scaled, factor, gain):
    grad_gain = jnp.sum(grad_normed * scaled, axis=0)
    grad_scaled = grad_normed * gain
    inner_mean = jnp.mean(grad_scaled * scaled, axis=-1, keepdims=True)
    return (factor * (grad_scaled - scaled * inner_mean), grad_gain)


def allowed_block(row_start, row_count, seq_ids, valid_mask):
    key_count = seq_ids.shape[0]
    query_pos = row_start + jnp.arange(row_count, dtype=jnp.int32)
    key_pos = jnp.arange(key_count, dtype=jnp.int32)
    same_seq = seq_ids[:, None] == seq_ids[None, :]
    causal = key_pos[None, :] <= query_pos[:, None]
    readable = valid_mask[None, :] == 1
    return same_seq & causal & readable | (key_pos[None, :] == query_pos[:, None])


def per_device(
    tokens,
    attn_in,
    attn_out,
    gate_weight,
    up_weight,
    down_weight,
    attn_gain,
    ffn_gain,
    cotangent,
    seq_ids,
    positions,
    valid_mask,
    group_owner,
):
    rows_total = tokens.shape[0]
    groups = group_owner.shape[0]
    query_width = Q_PER * HEAD
    block_rows = min(block_limit, rows_total)
    blocks = rows_total // block_rows
    score_scale = 1.0 / math.sqrt(HEAD)
    member = lax.axis_index("narrow")
    group_order = jnp.arange(groups, dtype=jnp.int32)
    sharing = (group_owner[:, None] == group_owner[None, :]) & (
        group_order[None, :] < group_order[:, None]
    )
    group_rank = jnp.sum(sharing.astype(jnp.int32), axis=1)
    slot_pick = (group_owner[None, :] == member) & (
        group_rank[None, :] == jnp.arange(SLOTS, dtype=jnp.int32)[:, None]
    )
    slot_live = jnp.any(slot_pick, axis=1)
    chosen = jnp.sum(jnp.where(slot_pick, group_order[None, :], 0), axis=1)
    slot_in = jnp.where(
        slot_live[:, None, None], jnp.take(attn_in, chosen, axis=0), jnp.zeros((), jnp.bfloat16)
    )
    slot_out = jnp.where(
        slot_live[:, None, None], jnp.take(attn_out, chosen, axis=0), jnp.zeros((), jnp.bfloat16)
    )
    cosine, sine_table = rope_tables(positions, HEAD // 2)
    cosine_query = cosine[:, None, :]
    sine_query = sine_table[:, None, :]

    def attend_backward(query_rot, key_rot, value_low, logsum, grad_mixed):

        def one_block(carry, block_index):
            grad_key, grad_value = carry
            row_start = block_index * block_rows
            scores = (
                jnp.einsum("sqjh,skh->sjqk", query_rot, key_rot, preferred_element_type=jnp.float32)
                * score_scale
            )
            allowed = allowed_block(row_start, block_rows, seq_ids, valid_mask)
            attn_prob = jnp.where(allowed, jnp.exp(scores - logsum[..., None]), 0.0)
            grad_value = grad_value + jnp.einsum(
                "sjqk,sqjh->skh",
                attn_prob.astype(jnp.bfloat16),
                grad_mixed,
                preferred_element_type=jnp.float32,
            )
            grad_prob = jnp.einsum(
                "sqjh,skh->sjqk", grad_mixed, value_low, preferred_element_type=jnp.float32
            )
            row_delta = jnp.sum(attn_prob * grad_prob, axis=-1, keepdims=True)
            grad_scores = (attn_prob * (grad_prob - row_delta)).astype(jnp.bfloat16)
            grad_query = (
                jnp.einsum(
                    "sjqk,skh->sqjh", grad_scores, key_rot, preferred_element_type=jnp.float32
                )
                * score_scale
            )
            grad_key = (
                grad_key
                + jnp.einsum(
                    "sjqk,sqjh->skh", grad_scores, query_rot, preferred_element_type=jnp.float32
                )
                * score_scale
            )
            return ((grad_key, grad_value), grad_query)

        zero_keys = jnp.zeros((SLOTS, rows_total, HEAD), jnp.float32)
        (grad_key, grad_value), grad_query = lax.scan(
            one_block, (zero_keys, zero_keys), jnp.arange(blocks, dtype=jnp.int32)
        )
        grad_query = jnp.moveaxis(grad_query, 0, 1).reshape(SLOTS, rows_total, Q_PER, HEAD)
        return (grad_query, grad_key, grad_value)

    def layer_backward(grad_stream, saved_state):
        (
            normed_one,
            scaled_one,
            factor_one,
            query_rot,
            key_rot,
            value_low,
            mixed_flat,
            logsum,
            normed_two,
            scaled_two,
            factor_two,
            ffn_saved,
        ) = saved_state
        gate_pre, upper, inner_act = ffn_saved
        grad_branch = grad_stream.astype(jnp.bfloat16)
        grad_down_w = jnp.einsum(
            "tf,td->fd", inner_act, grad_branch, preferred_element_type=jnp.float32
        )
        grad_inner = jnp.einsum(
            "td,fd->tf", grad_branch, down_weight, preferred_element_type=jnp.float32
        )
        sigmoid_gate = jax.nn.sigmoid(gate_pre)
        grad_gate_pre = (
            grad_inner * upper * sigmoid_gate * (1.0 + gate_pre * (1.0 - sigmoid_gate))
        ).astype(jnp.bfloat16)
        grad_upper = (grad_inner * gate_pre * sigmoid_gate).astype(jnp.bfloat16)
        grad_gate_w = jnp.einsum(
            "td,tf->df", normed_two, grad_gate_pre, preferred_element_type=jnp.float32
        )
        grad_up_w = jnp.einsum(
            "td,tf->df", normed_two, grad_upper, preferred_element_type=jnp.float32
        )
        grad_normed_two = jnp.einsum(
            "tf,df->td", grad_gate_pre, gate_weight, preferred_element_type=jnp.float32
        ) + jnp.einsum("tf,df->td", grad_upper, up_weight, preferred_element_type=jnp.float32)
        grad_normed_two = lax.psum(grad_normed_two, "narrow")
        grad_hidden, grad_gain_two = norm_backward(
            grad_normed_two, scaled_two, factor_two, ffn_gain
        )
        grad_hidden = grad_hidden + grad_stream
        grad_attn = grad_hidden.astype(jnp.bfloat16)
        grad_out_w = jnp.einsum(
            "sth,td->shd", mixed_flat, grad_attn, preferred_element_type=jnp.float32
        )
        grad_mixed = jnp.einsum(
            "td,shd->sth", grad_attn, slot_out, preferred_element_type=jnp.float32
        )
        grad_mixed = grad_mixed.astype(jnp.bfloat16).reshape(SLOTS, rows_total, Q_PER, HEAD)
        grad_query, grad_key, grad_value = attend_backward(
            query_rot, key_rot, value_low, logsum, grad_mixed
        )
        grad_query_raw = unrotate(grad_query, cosine_query, sine_query).reshape(
            SLOTS, rows_total, query_width
        )
        grad_key_raw = unrotate(grad_key, cosine, sine_table)
        grad_proj = jnp.concatenate([grad_query_raw, grad_key_raw, grad_value], axis=-1).astype(
            jnp.bfloat16
        )
        grad_in_w = jnp.einsum(
            "td,stc->sdc", normed_one, grad_proj, preferred_element_type=jnp.float32
        )
        grad_normed_one = jnp.einsum(
            "stc,sdc->td", grad_proj, slot_in, preferred_element_type=jnp.float32
        )
        grad_normed_one = lax.psum(grad_normed_one, "narrow")
        grad_lower, grad_gain_one = norm_backward(
            grad_normed_one, scaled_one, factor_one, attn_gain
        )
        grad_lower = grad_lower + grad_hidden
        return (
            grad_lower,
            (
                grad_in_w,
                grad_out_w,
                grad_gate_w,
                grad_up_w,
                grad_down_w,
                grad_gain_one,
                grad_gain_two,
            ),
        )

    stream = tokens.astype(jnp.float32)
    stashed = []
    for layer_index in range(LAYERS):
        layer_normed_one, layer_scaled_one, layer_factor_one = norm_forward(stream, attn_gain)
        projected = jnp.einsum(
            "td,sdc->stc", layer_normed_one, slot_in, preferred_element_type=jnp.float32
        )
        query_raw = projected[..., :query_width].reshape(SLOTS, rows_total, Q_PER, HEAD)
        layer_query_rot = rotate(query_raw, cosine_query, sine_query).astype(jnp.bfloat16)
        layer_key_rot = rotate(
            projected[..., query_width : query_width + HEAD], cosine, sine_table
        ).astype(jnp.bfloat16)
        layer_value_low = projected[..., query_width + HEAD :].astype(jnp.bfloat16)
        attend_query_rot = layer_query_rot
        attend_key_rot = layer_key_rot
        attend_value_low = layer_value_low

        def attend_one_block(block_index):
            row_start = block_index * block_rows
            scores = (
                jnp.einsum(
                    "sqjh,skh->sjqk",
                    attend_query_rot,
                    attend_key_rot,
                    preferred_element_type=jnp.float32,
                )
                * score_scale
            )
            allowed = allowed_block(row_start, block_rows, seq_ids, valid_mask)
            masked = jnp.where(allowed, scores, -jnp.inf)
            row_peak = jnp.max(masked, axis=-1, keepdims=True)
            exponent = jnp.exp(masked - row_peak)
            row_total = jnp.sum(exponent, axis=-1, keepdims=True)
            weights = (exponent / row_total).astype(jnp.bfloat16)
            mixed_heads = jnp.einsum(
                "sjqk,skh->sqjh", weights, attend_value_low, preferred_element_type=jnp.float32
            )
            return (mixed_heads.astype(jnp.bfloat16), (row_peak + jnp.log(row_total))[..., 0])

        mixed_heads, attend_logsum = lax.map(attend_one_block, jnp.arange(blocks, dtype=jnp.int32))
        mixed_heads = jnp.moveaxis(mixed_heads, 0, 1).reshape(SLOTS, rows_total, Q_PER, HEAD)
        attend_logsum = jnp.moveaxis(attend_logsum, 0, 2).reshape(SLOTS, Q_PER, rows_total)
        layer_mixed_flat = mixed_heads.reshape(SLOTS, rows_total, query_width)
        partial_attn = jnp.einsum(
            "sth,shd->td", layer_mixed_flat, slot_out, preferred_element_type=jnp.float32
        )
        hidden_stream = stream + lax.psum(partial_attn, "narrow")
        layer_normed_two, layer_scaled_two, layer_factor_two = norm_forward(hidden_stream, ffn_gain)
        layer_gate_pre = jnp.dot(layer_normed_two, gate_weight, preferred_element_type=jnp.float32)
        layer_upper = jnp.dot(layer_normed_two, up_weight, preferred_element_type=jnp.float32)
        layer_inner_act = (jax.nn.silu(layer_gate_pre) * layer_upper).astype(jnp.bfloat16)
        partial_ffn = jnp.dot(layer_inner_act, down_weight, preferred_element_type=jnp.float32)
        result = hidden_stream + lax.psum(partial_ffn, "narrow")
        layer_ffn_saved = (layer_gate_pre, layer_upper, layer_inner_act)
        layer_saved_state = (
            layer_normed_one,
            layer_scaled_one,
            layer_factor_one,
            layer_query_rot,
            layer_key_rot,
            layer_value_low,
            layer_mixed_flat,
            attend_logsum,
            layer_normed_two,
            layer_scaled_two,
            layer_factor_two,
            layer_ffn_saved,
        )
        stream = result
        saved_state = layer_saved_state
        stashed.append(saved_state)
    layer_out = stream.astype(jnp.bfloat16)
    grad_stream = cotangent.astype(jnp.float32)
    totals = None
    shares = None
    for layer_index in reversed(range(LAYERS)):
        grad_stream, grad_terms = layer_backward(grad_stream, stashed[layer_index])
        totals = grad_terms if totals is None else jax.tree.map(jnp.add, totals, grad_terms)
    shares = (
        lax.psum_scatter(totals[0], "wide", scatter_dimension=1, tiled=True),
        lax.psum_scatter(totals[1], "wide", scatter_dimension=2, tiled=True),
        lax.psum_scatter(totals[2], "wide", scatter_dimension=0, tiled=True),
        lax.psum_scatter(totals[3], "wide", scatter_dimension=0, tiled=True),
        lax.psum_scatter(totals[4], "wide", scatter_dimension=1, tiled=True),
        lax.psum_scatter(totals[5], "wide", scatter_dimension=0, tiled=True),
        lax.psum_scatter(totals[6], "wide", scatter_dimension=0, tiled=True),
    )
    collected = (
        lax.all_gather(shares[0], "wide", axis=1, tiled=True),
        lax.all_gather(shares[1], "wide", axis=2, tiled=True),
        lax.all_gather(shares[2], "wide", axis=0, tiled=True),
        lax.all_gather(shares[3], "wide", axis=0, tiled=True),
        lax.all_gather(shares[4], "wide", axis=1, tiled=True),
        lax.all_gather(shares[5], "wide", axis=0, tiled=True),
        lax.all_gather(shares[6], "wide", axis=0, tiled=True),
    )
    return (
        layer_out,
        grad_stream.astype(jnp.bfloat16),
        collected[0],
        collected[1],
        collected[2],
        collected[3],
        collected[4],
        collected[5],
        collected[6],
    )


def solution(mesh):
    in_specs = (
        P("wide", None),
        P(),
        P(),
        P(None, "narrow"),
        P(None, "narrow"),
        P("narrow", None),
        P(),
        P(),
        P("wide", None),
        P("wide"),
        P("wide"),
        P("wide"),
        P(),
    )
    out_specs = (
        P("wide", None),
        P("wide", None),
        P("narrow", None, None),
        P("narrow", None, None),
        P(None, "narrow"),
        P(None, "narrow"),
        P("narrow", None),
        P(),
        P(),
    )
    return jax.shard_map(
        per_device, mesh=mesh, in_specs=in_specs, out_specs=out_specs, check_vma=False
    )
```

profile of v0, /device:TPU:0, one launch (start us, length us, event | category | flops | bytes accessed | tf_op | source)
XLA Modules:
  0.0 1168.8 jit_solution(11890386403265331140)
XLA Ops:
  12.4 2.5 convolution_bitcast_fusion.5
  21.8 2.3 gather_fusion.1
  26.3 52.0 %all-reduce.22.cloned.1.call-done = f32[512,960]{0,1:T(8,128)} async-done(((f32[512,960]{0,1:T(8,128)}), f32[512,960]{0,1:T(8,128)}) %all-reduce.22.cloned.1.call-update) | async-done | bytes 1966096 | tf_op jit(solution)/shard_map/psum | solution.py:285
  86.2 2.2 fusion.109
  89.0 49.0 %all-reduce.24.cloned.1.call-done = f32[512,960]{0,1:T(8,128)} async-done(((f32[512,960]{0,1:T(8,128)}), f32[512,960]{0,1:T(8,128)}) %all-reduce.24.cloned.1.call-update) | async-done | bytes 1966096 | tf_op jit(solution)/shard_map/psum | solution.py:291
  149.7 49.4 %all-reduce.26.cloned.1.call-done = f32[512,960]{0,1:T(8,128)} async-done(((f32[512,960]{0,1:T(8,128)}), f32[512,960]{0,1:T(8,128)}) %all-reduce.26.cloned.1.call-update) | async-done | bytes 1966096 | tf_op jit(solution)/shard_map/psum | solution.py:285
  199.1 2.7 multiply_reduce_fusion.6
  207.0 2.4 multiply_convert_fusion.5
  210.5 2.2 convolution_add_fusion.4
  213.5 48.7 %all-reduce.28.cloned.1.call-done = f32[512,960]{0,1:T(8,128)} async-done(((f32[512,960]{0,1:T(8,128)}), f32[512,960]{0,1:T(8,128)}) %all-reduce.28.cloned.1.call-update) | async-done | bytes 1966096 | tf_op jit(solution)/shard_map/psum | solution.py:192
  262.2 3.5 multiply_reduce_fusion.1
  265.7 2.8 convert_add_fusion.1
  269.2 5.7 fusion.3
  274.8 4.7 fusion.5
  284.4 2.3 convolution_bitcast_fusion.1
  286.8 49.4 %all-reduce.30.cloned.1.call-done = f32[512,960]{0,1:T(8,128)} async-done(((f32[512,960]{0,1:T(8,128)}), f32[512,960]{0,1:T(8,128)}) %all-reduce.30.cloned.1.call-update) | async-done | bytes 1966096 | tf_op jit(solution)/shard_map/psum | solution.py:221
  336.3 3.5 multiply_reduce_fusion.2
  339.8 2.2 multiply_add_fusion.1
  345.5 2.2 convolution_add_fusion.3
  349.1 3.4 fusion.61
  352.5 2.5 fusion.77
  355.0 42.2 %all-reduce.32.cloned.1.call-done = f32[512,960]{0,1:T(8,128)} async-done(((f32[512,960]{0,1:T(8,128)}), f32[512,960]{0,1:T(8,128)}) %all-reduce.32.cloned.1.call-update) | async-done | bytes 1966096 | tf_op jit(solution)/shard_map/psum | solution.py:192
  397.2 2.3 multiply_reduce_fusion
  399.6 2.7 multiply_add_fusion
  403.7 3.1 fusion
  416.4 2.5 add_bitcast_fusion
  419.0 2.5 fusion.117
  421.5 2.4 convolution_add_fusion
  427.5 2.4 convolution_add_fusion.1
  432.1 2.4 convolution_add_fusion.2
  434.6 3.8 fusion.112
  438.5 2.4 convolution_bitcast_fusion
  442.8 133.0 %all-reduce.34.cloned.1.call-done = (f32[2,960,320]{1,2,0:T(8,128)}, f32[2,192,960]{2,1,0:T(8,128)}) async-done(((f32[2,960,320]{1,2,0:T(8,128)}, f32[2,192,960]{2,1,0:T(8,128)}), (f32[2,960,320]{1,2,0:T(8,128)}, f32[2,192,960]{2,1,0:T(8,128)})) %all-reduce.34.cloned.1.call-update) | async-done | bytes 3932176
  577.8 70.9 %reduce-scatter.16.cloned.1.call-done = f32[640,120]{0,1:T(8,128)} async-done(((f32[640,960]{0,1:T(8,128)}), f32[640,120]{0,1:T(8,128)}) %reduce-scatter.16.cloned.1.call-update) | async-done | bytes 307216
  648.8 72.8 %reduce-scatter.14.cloned.1.call-done = f32[120,640]{1,0:T(8,128)} async-done(((f32[960,640]{1,0:T(8,128)}), f32[120,640]{1,0:T(8,128)}) %reduce-scatter.14.cloned.1.call-update) | async-done | bytes 307216
  721.7 72.9 %reduce-scatter.12.cloned.1.call-done = f32[120,640]{1,0:T(8,128)} async-done(((f32[960,640]{1,0:T(8,128)}), f32[120,640]{1,0:T(8,128)}) %reduce-scatter.12.cloned.1.call-update) | async-done | bytes 307216
  797.5 79.8 %all-reduce.36.cloned.1.call-done = (f32[512,960]{0,1:T(8,128)}, f32[512,960]{0,1:T(8,128)}) async-done(((f32[512,960]{0,1:T(8,128)}, f32[512,960]{0,1:T(8,128)}), (f32[512,960]{0,1:T(8,128)}, f32[512,960]{0,1:T(8,128)})) %all-reduce.36.cloned.1.call-update) | async-done | bytes 3932176 | tf_op jit(solution)/shard_map/psum | solution.py:291
  877.3 2.2 fusion.34
  879.5 21.8 %all-reduce.10 = (f32[960]{0:T(1024)S(1)}, f32[960]{0:T(1024)S(1)}) all-reduce(f32[960]{0:T(1024)S(1)} %add.261, f32[960]{0:T(1024)S(1)} %add.262), channel_id=7, replica_groups=mesh['wide'=8,'narrow'=4] {'wide'}, use_global_device_ids=true, to_apply=%region_32.33.clone | all-reduce | flops 1920 | bytes 15360
  901.6 18.4 %all-reduce.9 = (f32[960]{0:T(1024)}, f32[960]{0:T(1024)}) all-reduce(f32[960]{0:T(1024)S(1)} %dynamic-slice_dynamic-update-slice_fusion.1, f32[960]{0:T(1024)S(1)} %dynamic-slice_dynamic-update-slice_fusion), channel_id=1, replica_groups=mesh['wide'=8,'narrow'=4] {'wide'}, use_global_device_ids=true, to_apply=%add | all-reduce | flops 1920 | bytes 15360
  920.1 3.0 add_convert_fusion
  924.6 3.3 all-gather.8.cloned.1.call-done
  928.0 3.9 copy.53
  931.9 50.6 %all-gather.14.cloned.1.call-done = f32[640,960]{0,1:T(8,128)} async-done(((f32[640,120]{0,1:T(8,128)}), f32[640,960]{0,1:T(8,128)}) %all-gather.14.cloned.1.call-update) | async-done | bytes 2457616 | tf_op jit(solution)/shard_map/all_gather | solution.py:331
  982.5 53.7 %all-gather.12.cloned.1.call-done = f32[960,640]{1,0:T(8,128)} async-done(((f32[120,640]{1,0:T(8,128)}), f32[960,640]{1,0:T(8,128)}) %all-gather.12.cloned.1.call-update) | async-done | bytes 2457616 | tf_op jit(solution)/shard_map/all_gather | solution.py:330
  1036.3 53.7 %all-gather.10.cloned.1.call-done = f32[960,640]{1,0:T(8,128)} async-done(((f32[120,640]{1,0:T(8,128)}), f32[960,640]{1,0:T(8,128)}) %all-gather.10.cloned.1.call-update) | async-done | bytes 2457616 | tf_op jit(solution)/shard_map/all_gather | solution.py:329
  1090.0 59.6 %all-gather.6.cloned.1.call-done = f32[2,960,320]{2,0,1:T(2,128)} async-done(((f32[2,120,320]{2,0,1:T(2,128)}), f32[2,960,320]{2,0,1:T(2,128)}) %all-gather.6.cloned.1.call-update) | async-done | bytes 2457616 | tf_op jit(solution)/shard_map/all_gather | solution.py:327
  1149.6 5.6 copy.52
  (357 shorter events, 81.9 us)
Async XLA Ops:
  7.2 3.5 copy-start
  7.2 71.1 %all-reduce.22.cloned.1.call-start = ((), (), s32[]{:S(2)}) async-start(), calls=%async_computation.3 | async-start | bytes 3932160 | tf_op jit(solution)/shard_map/psum | solution.py:285
  9.1 14.9 %copy-start.92 = (pred[2]{0:T(512)(128)(4,1)}, pred[2]{0:T(512)(128)(4,1)S(1)}, u32[]{:S(2)}) copy-start(pred[2]{0:T(512)(128)(4,1)S(1)} %fusion.87) | copy-start | bytes 10
  10.7 4.2 copy-start.87
  15.0 3.6 copy-start.49
  19.8 4.3 copy-start.99
  21.8 4.4 copy-start.45
  24.1 54.2 %copy-start.9 = (bf16[512,960]{0,1:T(8,128)(2,1)S(1)}, bf16[512,960]{0,1:T(8,128)(2,1)}, u32[]{:S(2)}) copy-start(bf16[512,960]{0,1:T(8,128)(2,1)} %param.13) | copy-start | bytes 2949124
  26.2 54.1 %copy-start.72 = (f32[960]{0:T(1024)S(1)}, f32[960]{0:T(1024)}, u32[]{:S(2)}) copy-start(f32[960]{0:T(1024)} %param.20) | copy-start | bytes 11524
  26.2 111.7 %all-reduce.24.cloned.1.call-start = ((), (), s32[]{:S(2)}) async-start(), calls=%async_computation.4 | async-start | bytes 3932160 | tf_op jit(solution)/shard_map/psum | solution.py:291
  88.5 51.6 %copy-start.93 = (pred[2]{0:T(512)(128)(4,1)S(1)}, pred[2]{0:T(512)(128)(4,1)}, u32[]{:S(2)}) copy-start(pred[2]{0:T(512)(128)(4,1)} %copy-done.92) | copy-start | bytes 10
  88.5 110.6 %all-reduce.26.cloned.1.call-start = ((), (), s32[]{:S(2)}) async-start(), calls=%async_computation.5 | async-start | bytes 3932160 | tf_op jit(solution)/shard_map/psum | solution.py:285
  149.6 112.6 %all-reduce.28.cloned.1.call-start = ((), (), s32[]{:S(2)}) async-start(), calls=%async_computation.6 | async-start | bytes 3932160 | tf_op jit(solution)/shard_map/psum | solution.py:192
  212.7 123.5 %all-reduce.30.cloned.1.call-start = ((), (), s32[]{:S(2)}) async-start(), calls=%async_computation.7 | async-start | bytes 3932160 | tf_op jit(solution)/shard_map/psum | solution.py:221
  213.5 52.2 %copy-start.24 = (bf16[512,960]{0,1:T(8,128)(2,1)S(1)}, bf16[512,960]{0,1:T(8,128)(2,1)}, u32[]{:S(2)}) copy-start(bf16[512,960]{0,1:T(8,128)(2,1)} %param.21) | copy-start | bytes 2949124
  262.2 6.9 slice-start.2
  265.7 3.5 slice-start.3
  268.5 6.3 copy-start.18
  274.8 4.7 copy-start.69
  274.8 4.7 copy-start.71
  286.8 110.5 %all-reduce.32.cloned.1.call-start = ((), (), s32[]{:S(2)}) async-start(), calls=%async_computation.8 | async-start | bytes 3932160 | tf_op jit(solution)/shard_map/psum | solution.py:192
  336.2 3.5 copy-start.7
  336.2 3.5 copy-start.19
  347.8 228.1 %all-reduce.34.cloned.1.call-start = ((), (), s32[]{:S(2)}) async-start(), calls=%async_computation.17 | async-start | bytes 8388608
  349.1 3.5 copy-start.8
  349.1 3.5 copy-start.78
  397.2 6.5 slice-start
  399.6 4.2 slice-start.1
  418.9 229.8 %reduce-scatter.16.cloned.1.call-start = ((), (), s32[]{:S(2)}) async-start(), calls=%async_computation.16 | async-start | bytes 2764800
  423.9 3.6 copy-start.22
  423.9 297.7 %reduce-scatter.14.cloned.1.call-start = ((), (), s32[]{:S(2)}) async-start(), calls=%async_computation.15 | async-start | bytes 2764800
  429.9 364.6 %reduce-scatter.12.cloned.1.call-start = ((), (), s32[]{:S(2)}) async-start(), calls=%async_computation.14 | async-start | bytes 2764800
  434.5 3.9 copy-start.42
  434.5 3.9 copy-start.44
  434.5 3.9 copy-start.76
  434.5 3.9 copy-start.97
  434.5 3.9 copy-start.103
  434.6 442.7 %all-reduce.36.cloned.1.call-start = ((), (), s32[]{:S(2)}) async-start(), calls=%async_computation.18 | async-start | bytes 7864320 | tf_op jit(solution)/shard_map/psum | solution.py:291
  440.9 356.5 %copy-start.89 = (f32[960]{0:T(1024)S(1)}, f32[960]{0:T(1024)}, u32[]{:S(2)}) copy-start(f32[960]{0:T(1024)} %get-tuple-element.132) | copy-start | bytes 11524
  440.9 487.0 %all-gather.8.cloned.1.call-start = ((), (), s32[]{:S(2)}) async-start(), calls=%async_computation.10 | async-start | bytes 2211840 | tf_op jit(solution)/shard_map/all_gather | solution.py:328
  577.8 404.8 %all-gather.14.cloned.1.call-start = ((), (), s32[]{:S(2)}) async-start(), calls=%async_computation.13 | async-start | bytes 2764800 | tf_op jit(solution)/shard_map/all_gather | solution.py:331
  648.8 387.5 %all-gather.12.cloned.1.call-start = ((), (), s32[]{:S(2)}) async-start(), calls=%async_computation.12 | async-start | bytes 2764800 | tf_op jit(solution)/shard_map/all_gather | solution.py:330
  721.6 368.4 %all-gather.10.cloned.1.call-start = ((), (), s32[]{:S(2)}) async-start(), calls=%async_computation.11 | async-start | bytes 2764800 | tf_op jit(solution)/shard_map/all_gather | solution.py:329
  794.5 355.0 %all-gather.6.cloned.1.call-start = ((), (), s32[]{:S(2)}) async-start(), calls=%async_computation.9 | async-start | bytes 3317760 | tf_op jit(solution)/shard_map/all_gather | solution.py:327
  795.8 83.6 %copy-start.90 = (f32[960]{0:T(1024)S(1)}, f32[960]{0:T(1024)}, u32[]{:S(2)}) copy-start(f32[960]{0:T(1024)} %get-tuple-element.134) | copy-start | bytes 11524
  795.9 124.3 %copy-start.5 = (f32[512,960]{0,1:T(8,128)S(1)}, f32[512,960]{0,1:T(8,128)}, u32[]{:S(2)}) copy-start(f32[512,960]{0,1:T(8,128)} %copy-done.4) | copy-start | bytes 5898244
  1090.0 65.2 %copy-start.39 = (f32[960,640]{1,0:T(8,128)S(1)}, f32[960,640]{1,0:T(8,128)}, u32[]{:S(2)}) copy-start(f32[960,640]{1,0:T(8,128)} %all-gather.10.cloned.1.call-done) | copy-start | bytes 7372804
  1157.8 4.0 copy-start.1
  (88 other events, 164.6 us)
Sparse Core Ops, SparseCore 0:
  26.3 51.9 all-reduce.21
  88.6 49.3 all-reduce.23
  149.7 49.3 all-reduce.25
  212.9 49.2 all-reduce.27
  286.9 49.3 all-reduce.29
  347.9 49.3 all-reduce.31
  419.1 156.7 all-reduce.33
  580.0 68.7 reduce-scatter.15
  653.0 68.5 reduce-scatter.13
  725.6 68.8 reduce-scatter.11
  796.9 80.3 all-reduce.35
  879.9 48.0 all-gather.7
  930.1 52.3 all-gather.13
  984.5 51.6 all-gather.11
  1038.3 51.6 all-gather.9
  1092.6 56.9 all-gather.5
where the time goes:
time: 1180 us; the launch traced here: 1170 us
  waiting for transfers between devices  941 us (80%)
  matrix products  80.2 us (7%)
  other arithmetic  45.3 us (4%)
  local copies, waits for them, and re-layouts  42.6 us (4%)
  blocking collectives  40.3 us (3%)
  between operations  17.1 us (1%)
    unnamed x20, waiting for transfers between devices  350 us
    psum x2, waiting for transfers between devices, per_device(): result = hidden_stream + lax.psum(partial_ffn, 'narrow')  129 us
    psum x2, waiting for transfers between devices, per_device(): hidden_stream = stream + lax.psum(partial_attn, 'narrow')  101 us
    psum x2, waiting for transfers between devices, layer_backward(): grad_normed_two = lax.psum(grad_normed_two, 'narrow')  91 us
    all_gather x1, waiting for transfers between devices, per_device(): lax.all_gather(shares[0], 'wide', axis=1, tiled=True)  59.6 us
    all_gather x1, waiting for transfers between devices, per_device(): lax.all_gather(shares[3], 'wide', axis=0, tiled=True)  53.7 us
    all_gather x1, waiting for transfers between devices, per_device(): lax.all_gather(shares[2], 'wide', axis=0, tiled=True)  53.7 us
    all_gather x1, waiting for transfers between devices, per_device(): lax.all_gather(shares[4], 'wide', axis=1, tiled=True)  50.6 us
  transfers between devices with their start and end apart: 16, of which 16 were waited for; matrix products, arithmetic and copies ran while one was open for 4% of the time, Pallas kernels for 0%

commit v1 on v0

v1 whole, which is shorter than its diff:
```python
import functools
import math

import jax
import jax.numpy as jnp
from jax import lax
from jax.experimental import pallas as pl
from jax.experimental.pallas import tpu as pltpu
from jax.sharding import PartitionSpec as P

HEAD = 64
Q_PER = 3
SLOTS = 2
EPS = 1e-05
THETA = 10000.0
RB = 128
F32 = jnp.float32
BF16 = jnp.bfloat16
NEG = -1e30
VMEM_LIMIT = 56 * 1024 * 1024


def dot(a, b):
    return jnp.dot(a, b, preferred_element_type=F32)


def dot_nt(a, b):
    return lax.dot_general(a, b, (((1,), (1,)), ((), ())), preferred_element_type=F32)


def dot_tn(a, b):
    return lax.dot_general(a, b, (((0,), (0,)), ((), ())), preferred_element_type=F32)


def lane_iota(rows):
    return lax.broadcasted_iota(jnp.int32, (rows, 128), 1)


def low_half(rows):
    return lane_iota(rows) < HEAD


def rope128(v, cs, sn):
    lane = lane_iota(v.shape[0])
    partner = jnp.where((lane & 63) < 32, pltpu.roll(v, 96, 1), pltpu.roll(v, 32, 1))
    return v * cs + partner * sn


def allowed_bias(seqc_ref, seqr_ref, valr_ref, r0, nk):
    t = r0 + lax.broadcasted_iota(jnp.int32, (RB, nk), 0)
    u = lax.broadcasted_iota(jnp.int32, (RB, nk), 1)
    same = seqc_ref[r0 : r0 + RB, :] == seqr_ref[:, :nk]
    ok = (same & (u <= t) & (valr_ref[:, :nk] == 1)) | (u == t)
    return jnp.where(ok, 0.0, NEG).astype(F32)


def masked_heads(x, y):
    low = low_half(1).astype(F32)
    low_b, high_b = low.astype(BF16), (1.0 - low).astype(BF16)
    return jnp.concatenate([x * low_b, x * high_b, y * low_b], axis=0)


def fwd_kernel(
    second, t, groups, *refs
):
    it = iter(refs)
    x_ref = next(it)
    add_ref = next(it) if second else None
    win, wout, g1, g2, cs_ref, sn_ref, seqc, seqr, valr, wg, wu, wd = (next(it) for _ in range(12))
    cot = next(it) if second else None
    n1_ref, qk_ref, kt_ref, vt_ref, o_ref, lse_ref, h_ref, n2_ref = (next(it) for _ in range(8))
    if second:
        x_out, hid_ref, dgate_ref, dup_ref, part_ref, dn2_ref = (next(it) for _ in range(6))
    else:
        gate_ref, up_ref, hid_ref, part_ref = (next(it) for _ in range(4))
    acc = next(it)
    d = n1_ref.shape[1]

    if second:
        x = x_ref[...] + add_ref[...]
        x_out[...] = x
    else:
        x = x_ref[...].astype(F32)
    r1 = lax.rsqrt(jnp.mean(x * x, axis=1, keepdims=True) + EPS)
    n1_ref[...] = (x * r1 * g1[...]).astype(BF16)
    acc[...] = x
    lse_ref[...] = jnp.zeros_like(lse_ref)

    def group(g, carry):
        n1 = n1_ref[...]
        qk = dot(n1, win[g, :, :256])
        v = dot(n1, win[g, :, 256:320])
        cs, sn = cs_ref[...], sn_ref[...]
        xr = rope128(qk[:, :128], cs, sn)
        yr = rope128(qk[:, 128:], cs, sn)
        qk_ref[g, :, :128] = xr.astype(BF16)
        qk_ref[g, :, 128:] = yr.astype(BF16)
        kt_ref[g] = jnp.where(low_half(t), pltpu.roll(yr, 64, 1), yr).astype(BF16)
        vt_ref[g] = jnp.concatenate([v, v], axis=1).astype(BF16)
        for rb in range(t // RB):
            r0, nk = rb * RB, (rb + 1) * RB
            rows = slice(r0, r0 + RB)
            q = masked_heads(qk_ref[g, rows, :128], qk_ref[g, rows, 128:])
            s = dot_nt(q, kt_ref[g, :nk, :])
            bias = allowed_bias(seqc, seqr, valr, r0, nk)
            s = (s.reshape(3, RB, nk) * 0.125 + bias[None]).reshape(3 * RB, nk)
            m = jnp.max(s, axis=1, keepdims=True)
            e = jnp.exp(s - m)
            l = jnp.sum(e, axis=1, keepdims=True)
            o = dot(e.astype(BF16), vt_ref[g, :nk, :]) / l
            low = low_half(RB)
            o_ref[g, rows, :128] = jnp.where(low, o[:RB], o[RB : 2 * RB]).astype(BF16)
            o_ref[g, rows, 128:] = jnp.where(low, o[2 * RB :], 0.0).astype(BF16)
            ls = m + jnp.log(l)
            lane = lane_iota(RB)
            cur = lse_ref[rows, :]
            for j in range(3):
                cur = jnp.where(lane == g * 3 + j, ls[j * RB : (j + 1) * RB], cur)
            lse_ref[rows, :] = cur
        acc[...] += dot(o_ref[g, :, :192], wout[g])
        return carry

    lax.fori_loop(0, groups, group, 0)
    h = acc[...]
    h_ref[...] = h
    r2 = lax.rsqrt(jnp.mean(h * h, axis=1, keepdims=True) + EPS)
    n2_ref[...] = (h * r2 * g2[...]).astype(BF16)
    for rb in range(t // 256):
        rows = slice(rb * 256, rb * 256 + 256)
        n2 = n2_ref[rows, :]
        gate = dot(n2, wg[...])
        up = dot(n2, wu[...])
        sig = jax.nn.sigmoid(gate)
        act = gate * sig
        hid = (act * up).astype(BF16)
        hid_ref[rows, :] = hid
        part_ref[rows, :] = dot(hid, wd[...])
        if second:
            dhid = dot_nt(cot[rows, :], wd[...])
            dgate = (dhid * up * sig * (1.0 + gate * (1.0 - sig))).astype(BF16)
            dup = (dhid * act).astype(BF16)
            dgate_ref[rows, :] = dgate
            dup_ref[rows, :] = dup
            dn2_ref[rows, :] = dot_nt(dgate, wg[...]) + dot_nt(dup, wu[...])
        else:
            gate_ref[rows, :] = gate
            up_ref[rows, :] = up


def norm_back(dn, stream, gain):
    r = lax.rsqrt(jnp.mean(stream * stream, axis=1, keepdims=True) + EPS)
    m = stream * r
    dgain = jnp.sum(dn * m, axis=0, keepdims=True)
    dm = dn * gain
    return r * (dm - m * jnp.mean(dm * m, axis=1, keepdims=True)), dgain


def bwd_kernel(last, t, groups, *refs):
    it = iter(refs)
    (dz_ref, dn2_ref, h_ref, x_ref, qk_ref, kt_ref, vt_ref, o_ref, lse_ref,
     win, wout, g1, g2, cs_ref, sn_ref, seqc, seqr, valr) = (next(it) for _ in range(18))
    da_ref, dproj_ref, dx_ref, dg1_ref, dg2_ref = (next(it) for _ in range(5))
    acc, dkv = next(it), next(it)

    dh, dg2 = norm_back(dn2_ref[...], h_ref[...], g2[...])
    dh = dz_ref[...].astype(F32) + dh
    dg2_ref[...] = dg2
    da_ref[...] = dh.astype(BF16)
    acc[...] = jnp.zeros_like(acc)

    def group(g, carry):
        da = da_ref[...]
        cs, sn = cs_ref[...], -sn_ref[...]
        dkv[...] = jnp.zeros_like(dkv)
        low = low_half(RB)
        lane = lane_iota(RB)
        for rb in range(t // RB):
            r0, nk = rb * RB, (rb + 1) * RB
            rows = slice(r0, r0 + RB)
            do = dot_nt(da[rows], wout[g])
            dox = do[:, :128].astype(BF16)
            doy = jnp.concatenate([do[:, 128:192], jnp.zeros((RB, 64), F32)], axis=1).astype(BF16)
            px = dox.astype(F32) * o_ref[g, rows, :128].astype(F32)
            py = doy.astype(F32) * o_ref[g, rows, 128:].astype(F32)
            delta = jnp.concatenate(
                [
                    jnp.sum(jnp.where(low, px, 0.0), axis=1, keepdims=True),
                    jnp.sum(jnp.where(low, 0.0, px), axis=1, keepdims=True),
                    jnp.sum(py, axis=1, keepdims=True),
                ],
                axis=0,
            )
            ls = lse_ref[rows, :]
            lse = jnp.concatenate(
                [jnp.sum(jnp.where(lane == g * 3 + j, ls, 0.0), axis=1, keepdims=True) for j in range(3)],
                axis=0,
            )
            q = masked_heads(qk_ref[g, rows, :128], qk_ref[g, rows, 128:])
            dos = masked_heads(dox, doy)
            s = dot_nt(q, kt_ref[g, :nk, :])
            dp = dot_nt(dos, vt_ref[g, :nk, :])
            bias = allowed_bias(seqc, seqr, valr, r0, nk)
            s = (s.reshape(3, RB, nk) * 0.125 + bias[None]).reshape(3 * RB, nk)
            p = jnp.exp(s - lse)
            ds = (p * (dp - delta)).astype(BF16)
            dq = dot(ds, kt_ref[g, :nk, :])
            dkv[0, :nk, :] += dot_tn(ds, q)
            dkv[1, :nk, :] += dot_tn(p.astype(BF16), dos)
            dqx = jnp.where(low, dq[:RB], dq[RB : 2 * RB]) * 0.125
            dproj_ref[g, rows, :128] = rope128(dqx, cs[rows], sn[rows]).astype(BF16)
            dkv[2, rows, :] = dq[2 * RB :] * 0.125
        dk = dkv[0]
        dk = (dk + pltpu.roll(dk, 64, 1)) * 0.125
        dy = jnp.where(low_half(t), dkv[2], dk)
        dproj_ref[g, :, 128:256] = rope128(dy, cs, sn).astype(BF16)
        dv = dkv[1]
        dv = dv + pltpu.roll(dv, 64, 1)
        dproj_ref[g, :, 256:320] = dv[:, :64].astype(BF16)
        acc[...] += dot_nt(dproj_ref[g], win[g])
        return carry

    lax.fori_loop(0, groups, group, 0)
    dx, dg1 = norm_back(acc[...], x_ref[...].astype(F32), g1[...])
    dg1_ref[...] = dg1
    dx = dx + (dz_ref[...].astype(F32) + norm_back(dn2_ref[...], h_ref[...], g2[...])[0])
    dx_ref[...] = dx.astype(dx_ref.dtype)


def ffn_back_kernel(t, dz_ref, gate_ref, up_ref, wg, wu, wd, dgate_ref, dup_ref, dn2_ref, df_ref):
    for rb in range(t // 256):
        rows = slice(rb * 256, rb * 256 + 256)
        df = dz_ref[rows, :].astype(BF16)
        df_ref[rows, :] = df
        dhid = dot_nt(df, wd[...])
        gate, up = gate_ref[rows, :], up_ref[rows, :]
        sig = jax.nn.sigmoid(gate)
        dgate = (dhid * up * sig * (1.0 + gate * (1.0 - sig))).astype(BF16)
        dup = (dhid * gate * sig).astype(BF16)
        dgate_ref[rows, :] = dgate
        dup_ref[rows, :] = dup
        dn2_ref[rows, :] = dot_nt(dgate, wg[...]) + dot_nt(dup, wu[...])


def ffn_grad_kernel(add, *refs):
    n2, dgate, dup, hid, df = refs[:5]
    outs = refs[-3:]
    old = refs[5:8] if add else (None,) * 3
    for out, base, a, b in zip(outs, old, (n2, n2, hid), (dgate, dup, df)):
        rows = out.shape[0]
        for r in range(0, rows, 320):
            v = dot_tn(a[:, r : r + 320], b[...])
            out[r : r + 320, :] = v + base[r : r + 320, :] if add else v


def attn_grad_kernel(idx, n1a, n1b, dpa, dpb, oa, ob, daa, dab, gin, gout):
    for s in range(SLOTS):
        g = idx[s]
        live = idx[SLOTS + s].astype(F32)
        gin[s] = (dot_tn(n1a[...], dpa[g]) + dot_tn(n1b[...], dpb[g])) * live
        gout[s] = (dot_tn(oa[g, :, :192], daa[...]) + dot_tn(ob[g, :, :192], dab[...])) * live


def call(kernel, outs, ins, scratch=(), smem=0, flops=0):
    specs = [pl.BlockSpec(memory_space=pltpu.SMEM)] * smem
    specs += [pl.BlockSpec(memory_space=pltpu.VMEM)] * (len(ins) - smem)
    moved = sum(math.prod(a.shape) * a.dtype.itemsize for a in list(ins) + list(outs))
    return pl.pallas_call(
        kernel,
        out_shape=tuple(outs),
        in_specs=specs,
        out_specs=tuple(pl.BlockSpec(memory_space=pltpu.VMEM) for _ in outs),
        scratch_shapes=list(scratch),
        compiler_params=pltpu.CompilerParams(vmem_limit_bytes=VMEM_LIMIT),
        cost_estimate=pl.CostEstimate(flops=flops, bytes_accessed=moved, transcendentals=0),
    )(*ins)


def S(shape, dtype):
    return jax.ShapeDtypeStruct(shape, dtype)


class Links:
    def __init__(self, mesh):
        self.wide, self.narrow = mesh.shape["wide"], mesh.shape["narrow"]
        self.known = (self.wide, self.narrow) == (8, 4)

    def permute(self, v, step):
        pairs = []
        for w in range(self.wide):
            for n in range(self.narrow):
                to = step(w // 2, w % 2, n // 2, n % 2)
                if to is not None:
                    z, x, y, c = to
                    pairs.append((w * self.narrow + n, (z * 2 + x) * self.narrow + y * 2 + c))
        return lax.ppermute(v, ("wide", "narrow"), pairs)

    def core(self, v):
        return self.permute(v, lambda z, x, y, c: (z, x, y, 1 - c))

    def y(self, v):
        return self.permute(v, lambda z, x, y, c: (z, x, 1 - y, c))

    def x(self, v):
        return self.permute(v, lambda z, x, y, c: (z, 1 - x, y, c))

    def inward(self, v):
        return self.permute(v, lambda z, x, y, c: ({0: 1, 3: 2}[z], x, y, c) if z in (0, 3) else None)

    def outward(self, v):
        return self.permute(v, lambda z, x, y, c: ({1: 0, 2: 3}[z], x, y, c) if z in (1, 2) else None)

    def middle(self, v):
        return self.permute(v, lambda z, x, y, c: (3 - z, x, y, c) if z in (1, 2) else None)

    def sum_narrow(self, v):
        if not self.known:
            return lax.psum(v, "narrow")
        c = lax.axis_index("narrow") % 2
        h = v.shape[0] // 2
        keep = lax.dynamic_slice_in_dim(v, c * h, h, 0)
        send = lax.dynamic_slice_in_dim(v, (1 - c) * h, h, 0)
        r = keep + self.core(send)
        r = r + self.y(r)
        o = self.core(r)
        return jnp.where(c == 0, jnp.concatenate([r, o], 0), jnp.concatenate([o, r], 0))

    def sum_wide(self, v):
        if not self.known:
            return lax.psum(v, "wide")
        w = lax.axis_index("wide")
        x, z = w % 2, w // 2
        h = v.shape[0] // 2
        keep = lax.dynamic_slice_in_dim(v, x * h, h, 0)
        send = lax.dynamic_slice_in_dim(v, (1 - x) * h, h, 0)
        r = keep + self.x(send)
        r = r + self.inward(r)
        r = r + self.middle(r)
        r = jnp.where((z == 1) | (z == 2), r, self.outward(r))
        o = self.x(r)
        return jnp.where(x == 0, jnp.concatenate([r, o], 0), jnp.concatenate([o, r], 0))


def per_device(links, tokens, attn_in, attn_out, gate_weight, up_weight, down_weight, attn_gain, ffn_gain,
               cotangent, seq_ids, positions, valid_mask, group_owner):
    t, d = tokens.shape
    groups = attn_in.shape[0]
    f = gate_weight.shape[1]
    member = lax.axis_index("narrow")
    order = jnp.arange(groups, dtype=jnp.int32)
    sharing = (group_owner[:, None] == group_owner[None, :]) & (order[None, :] < order[:, None])
    rank = jnp.sum(sharing.astype(jnp.int32), axis=1)
    pick = (group_owner[None, :] == member) & (rank[None, :] == jnp.arange(SLOTS, dtype=jnp.int32)[:, None])
    live = jnp.any(pick, axis=1)
    chosen = jnp.sum(jnp.where(pick, order[None, :], 0), axis=1)
    idx = jnp.concatenate([chosen, live.astype(jnp.int32)]).astype(jnp.int32)

    lane = jnp.arange(128, dtype=jnp.int32)
    half = HEAD // 2
    freq = THETA ** (-(lane % half).astype(F32) / half)
    angles = positions.astype(F32)[:, None] * freq[None, :]
    cs = jnp.cos(angles)
    sn = jnp.sin(angles) * jnp.where(lane % HEAD < half, -1.0, 1.0).astype(F32)[None, :]
    seqc, seqr, valr = seq_ids.reshape(t, 1), seq_ids.reshape(1, t), valid_mask.reshape(1, t)
    g1, g2 = attn_gain.reshape(1, d), ffn_gain.reshape(1, d)

    saved = [S((t, d), BF16), S((groups, t, 256), BF16), S((groups, t, 128), BF16), S((groups, t, 128), BF16),
             S((groups, t, 256), BF16), S((t, 128), F32), S((t, d), F32), S((t, d), BF16)]
    scratch = [pltpu.VMEM((t, d), F32)]
    weights = [attn_in, attn_out, g1, g2, cs, sn, seqc, seqr, valr]
    ffn_w = [gate_weight, up_weight, down_weight]
    *kept1, gate1, up1, hid1, part1 = call(
        functools.partial(fwd_kernel, False, t, groups),
        saved + [S((t, f), F32), S((t, f), F32), S((t, f), BF16), S((t, d), F32)],
        [tokens] + weights + ffn_w, scratch, flops=6 * 10**9,
    )
    sum1 = links.sum_narrow(part1)
    *kept2, x1, hid2, dgate2, dup2, part2, dn2p2 = call(
        functools.partial(fwd_kernel, True, t, groups),
        saved + [S((t, d), F32), S((t, f), BF16), S((t, f), BF16), S((t, f), BF16), S((t, d), F32), S((t, d), F32)],
        [kept1[6], sum1] + weights + ffn_w + [cotangent], scratch, flops=8 * 10**9,
    )
    n1a, qk1, kt1, vt1, o1, lse1, h1, n2a = kept1
    n1b, qk2, kt2, vt2, o2, lse2, h2, n2b = kept2
    dn2_2 = links.sum_narrow(dn2p2)
    grads = call(
        functools.partial(ffn_grad_kernel, False),
        [S((d, f), F32), S((d, f), F32), S((f, d), F32)],
        [n2b, dgate2, dup2, hid2, cotangent], flops=2 * 10**9,
    )
    bscratch = [pltpu.VMEM((t, d), F32), pltpu.VMEM((3, t, 128), F32)]
    bouts = [S((t, d), BF16), S((groups, t, 320), BF16)]
    gains = [S((1, d), F32), S((1, d), F32)]
    da2, dproj2, dz1, dg1b, dg2b = call(
        functools.partial(bwd_kernel, False, t, groups), bouts + [S((t, d), F32)] + gains,
        [cotangent, dn2_2, h2, x1, qk2, kt2, vt2, o2, lse2] + weights, bscratch, flops=8 * 10**9,
    )
    dgate1, dup1, dn2p1, df1 = call(
        functools.partial(ffn_back_kernel, t), [S((t, f), BF16), S((t, f), BF16), S((t, d), F32), S((t, d), BF16)],
        [dz1, gate1, up1] + ffn_w, flops=2 * 10**9,
    )
    dn2_1 = links.sum_narrow(dn2p1)
    grads = call(
        functools.partial(ffn_grad_kernel, True),
        [S((d, f), F32), S((d, f), F32), S((f, d), F32)],
        [n2a, dgate1, dup1, hid1, df1, *grads], flops=2 * 10**9,
    )
    da1, dproj1, dx, dg1a, dg2a = call(
        functools.partial(bwd_kernel, True, t, groups), bouts + [S((t, d), BF16)] + gains,
        [dz1, dn2_1, h1, tokens, qk1, kt1, vt1, o1, lse1] + weights, bscratch, flops=8 * 10**9,
    )
    gin, gout = call(
        attn_grad_kernel, [S((SLOTS, d, 320), F32), S((SLOTS, 192, d), F32)],
        [idx, n1a, n1b, dproj1, dproj2, o1, o2, da1, da2], smem=1, flops=2 * 10**9,
    )
    small = jnp.concatenate([dg1a + dg1b, dg2a + dg2b], axis=0)
    small = lax.psum(small, "wide")
    ggate, gup, gdown = (links.sum_wide(v) for v in grads)
    gin = links.sum_wide(gin.reshape(SLOTS * d, 320)).reshape(SLOTS, d, 320)
    gout = links.sum_wide(gout.reshape(SLOTS * 192, d)).reshape(SLOTS, 192, d)
    layer_out = (h2 + lax.psum(part2, "narrow")).astype(BF16)
    return layer_out, dx, gin, gout, ggate, gup, gdown, small[0], small[1]


def solution(mesh):
    in_specs = (P("wide", None), P(), P(), P(None, "narrow"), P(None, "narrow"), P("narrow", None), P(), P(),
                P("wide", None), P("wide"), P("wide"), P("wide"), P())
    out_specs = (P("wide", None), P("wide", None), P("narrow", None, None), P("narrow", None, None),
                 P(None, "narrow"), P(None, "narrow"), P("narrow", None), P(), P())
    return jax.shard_map(functools.partial(per_device, Links(mesh)), mesh=mesh, in_specs=in_specs,
                         out_specs=out_specs, check_vma=False)
```

time: 1180 us -> 654 us (0.55)
  waiting for transfers between devices: 941 us -> 227 us
  Pallas kernels: 0 us -> 151 us
  matrix products: 80.2 us -> 0 us
  starting transfers between devices: 1.76 us -> 58.7 us
  other arithmetic: 45.3 us -> 79.3 us
  blocking collectives: 40.3 us -> 66.6 us
    psum x7 -> x1, waiting for transfers between devices: 371 us -> 19.4 us  [per_device(): layer_out = (h2 + lax.psum(part2, 'narrow')).astype(BF16)]
    unnamed x20 -> x1, waiting for transfers between devices: 350 us -> 0.02 us
    all_gather x5 -> x0, waiting for transfers between devices: 221 us -> none  [the longest x1 59.6 us: per_device(): lax.all_gather(shares[0], 'wide', axis=1, tiled=True)]
    ppermute x0 -> x34, waiting for transfers between devices: none -> 208 us  [permute(): return lax.ppermute(v, ('wide', 'narrow'), pairs)]
    pallas_call x0 -> x8, Pallas kernels: none -> 151 us  [call(): pl.pallas_call(kernel, out_shape=tuple(outs), in_specs=specs, out_specs=t...]
    dot_general x42 -> x0, matrix products: 80.2 us -> none  [the longest x2 8.75 us: one_block(): jnp.einsum('sqjh,skh->sjqk', grad_mixed, value_low, preferred_element_typ...]
    psum x0 -> x1, blocking collectives: none -> 66.6 us  [per_device(): small = lax.psum(small, 'wide')]
    ppermute x0 -> x34, starting transfers between devices: none -> 58.7 us  [permute(): return lax.ppermute(v, ('wide', 'narrow'), pairs)]
  transfers between devices with their start and end apart: 16 -> 35, of which waited for: 16 -> 17; matrix products, arithmetic and copies ran while one was open for 4% -> 13% of each run, Pallas kernels for 0% -> 8%
where the time goes in v1:
time: 654 us; the launch traced here: 646 us
  waiting for transfers between devices  227 us (35%)
  Pallas kernels  151 us (23%)
  other arithmetic  79.3 us (12%)
  blocking collectives  66.6 us (10%)
  starting transfers between devices  58.7 us (9%)
  local copies, waits for them, and re-layouts  47.7 us (7%)
  between operations  15.1 us (2%)
    ppermute x34, waiting for transfers between devices, permute(): return lax.ppermute(v, ('wide', 'narrow'), pairs)  208 us
    pallas_call x8, Pallas kernels, call(): pl.pallas_call(kernel, out_shape=tuple(outs), in_specs=specs, out_specs=t...  151 us
    psum x1, blocking collectives, per_device(): small = lax.psum(small, 'wide')  66.6 us
    ppermute x34, starting transfers between devices, permute(): return lax.ppermute(v, ('wide', 'narrow'), pairs)  58.7 us
    unnamed x42, local copies, waits for them, and re-layouts  23.3 us
    psum x1, waiting for transfers between devices, per_device(): layer_out = (h2 + lax.psum(part2, 'narrow')).astype(BF16)  19.4 us
    select_n x5, other arithmetic, sum_wide(): jnp.where(x == 0, jnp.concatenate([r, o], 0), jnp.concatenate([o, r], 0))  19.2 us
  transfers between devices with their start and end apart: 35, of which 17 were waited for; matrix products, arithmetic and copies ran while one was open for 13% of the time, Pallas kernels for 8%

profile of v1, /device:TPU:0, one launch (start us, length us, event | category | flops | bytes accessed | tf_op | source)
XLA Modules:
  0.0 645.7 jit_solution(11501016182821920903)
XLA Ops:
  9.5 5.9 copy.146.refs_1_.refs_2_.refs_9_
  19.9 23.2 %shard_map.196 = (bf16[512,960]{1,0:T(8,128)(2,1)}, bf16[5,512,256]{2,1,0:T(8,128)(2,1)}, bf16[5,512,128]{2,1,0:T(8,128)(2,1)}, bf16[5,512,128]{2,1,0:T(8,128)(2...) custom-call(bf16[512,960]{1,0:T(8,128)(2,1)} %copy.145.refs_0_.refs_, ...), custom_call_target="tpu_custom_call" | custom-call | flops 6000000000 | bytes 23492096 | tf_op jit(solution)/shard_map/pallas_call | solution.py:267
  49.6 2.9 collective-permute-start.1
  52.5 22.1 %collective-permute-done.1 = f32[256,960]{0,1:T(8,128)S(1)} collective-permute-done((f32[256,960]{0,1:T(8,128)S(1)}, f32[256,960]{0,1:T(8,128)S(1)}, u32[]{:S(2)}, u32[]{:S(2)}) %collective-permute-start.1) | collective-permute-done | bytes 983072 | tf_op jit(solution)/shard_map/ppermute | solution.py:295
  81.0 28.0 %shard_map.197 = (bf16[512,960]{1,0:T(8,128)(2,1)}, bf16[5,512,256]{2,1,0:T(8,128)(2,1)}, bf16[5,512,128]{2,1,0:T(8,128)(2,1)}, bf16[5,512,128]{2,1,0:T(8,128)(2...) custom-call(f32[512,960]{1,0:T(8,128)} %get-tuple-element.57.refs_0_, ...), custom_call_target="tpu_custom_call" | custom-call | flops 8000000000 | bytes 30045696 | tf_op jit(solution)/shard_map/pallas_call | solution.py:267
  110.8 2.4 collective-permute-done.3
  117.1 22.1 %collective-permute-done.4 = f32[256,960]{0,1:T(8,128)S(1)} collective-permute-done((f32[256,960]{0,1:T(8,128)S(1)}, f32[256,960]{0,1:T(8,128)S(1)}, u32[]{:S(2)}, u32[]{:S(2)}) %collective-permute-start.4) | collective-permute-done | bytes 983072 | tf_op jit(solution)/shard_map/ppermute | solution.py:295
  140.1 2.6 collective-permute-done.5
  144.5 38.5 %shard_map.198 = (bf16[512,960]{1,0:T(8,128)(2,1)}, bf16[5,512,320]{2,1,0:T(8,128)(2,1)}, f32[512,960]{1,0:T(8,128)}, f32[1,960]{1,0:T(1,128)}, f32[1,960]{1,0:T(1,128)}) custom-call(bf16[512,960]{1,0:T(8,128)(2,1)} %copy.159.refs_14_.refs_0_.refs_4_, f32[512,960]{1,0:T(8,128)} %maximum_select_fusion.5.refs_1_, f32[512,960]{1,0:T(8,128)} %get-tuple-element.59.refs_2_, ...), custom_call_target="tpu_custom_call" | custom-call | flops 8000000000 | bytes 21124096 | tf_op jit(solution)/shard_map/pallas_call | solution.py:267
  182.9 8.3 %shard_map.199 = (bf16[512,640]{1,0:T(8,128)(2,1)}, bf16[512,640]{1,0:T(8,128)(2,1)}, f32[512,960]{1,0:T(8,128)}, bf16[512,960]{1,0:T(8,128)(2,1)}) custom-call(f32[512,960]{1,0:T(8,128)} %get-tuple-element.68.dz_ref.refs_0_, f32[512,640]{1,0:T(8,128)} %get-tuple-element.69.gate_ref, f32[512,640]{1,0:T(8,128)} %get-tuple-element.70.up_ref, ...), custom_call_target="tpu_custom_call" | custom-call | flops 2000000000 | bytes 12533760 | tf_op jit(solution)/shard_map/pallas_call | solution.py:267
  193.0 2.4 collective-permute-done.6
  199.7 21.7 %collective-permute-done.7 = f32[256,960]{0,1:T(8,128)S(1)} collective-permute-done((f32[256,960]{0,1:T(8,128)S(1)}, f32[256,960]{0,1:T(8,128)S(1)}, u32[]{:S(2)}, u32[]{:S(2)}) %collective-permute-start.7) | collective-permute-done | bytes 983072 | tf_op jit(solution)/shard_map/ppermute | solution.py:295
  223.0 6.3 shard_map.202
  229.3 8.6 %shard_map.203 = (f32[960,640]{1,0:T(8,128)}, f32[960,640]{1,0:T(8,128)}, f32[640,960]{1,0:T(8,128)}) custom-call(bf16[512,960]{1,0:T(8,128)(2,1)} %get-tuple-element.86.refs_0_, bf16[512,640]{1,0:T(8,128)(2,1)} %get-tuple-element.87.refs_1_, bf16[512,640]{1,0:T(8,128)(2,1)} %get-tuple-element.88.refs_2_, bf16[512,640]{1,0:T(8,128)(2,1)} %get-tuple-element.89.refs_3_, ...), custom_call_target="tpu_custom_call" | custom-call | flops 2000000000 | bytes 18677760 | tf_op jit(solution)/shard_map/pallas_call | solution.py:267
  238.0 2.6 constant_dynamic-slice_fusion.2
  249.9 29.5 %shard_map.200 = (bf16[512,960]{1,0:T(8,128)(2,1)}, bf16[5,512,320]{2,1,0:T(8,128)(2,1)}, bf16[512,960]{1,0:T(8,128)(2,1)}, f32[1,960]{1,0:T(1,128)}, f32[1,960]{1,0:T(1,128)}) custom-call(f32[512,960]{1,0:T(8,128)} %get-tuple-element.68.dz_ref.refs_0_, f32[512,960]{1,0:T(8,128)} %maximum_select_fusion.6.refs_1_, ...), custom_call_target="tpu_custom_call" | custom-call | flops 8000000000 | bytes 20141056 | tf_op jit(solution)/shard_map/pallas_call | solution.py:267
  279.4 8.8 %shard_map.201 = (f32[2,960,320]{2,1,0:T(8,128)}, f32[2,192,960]{2,1,0:T(8,128)}) custom-call(s32[4]{0:T(128)} %pad_add_fusion.idx, bf16[512,960]{1,0:T(8,128)(2,1)} %get-tuple-element.78.n1a, bf16[512,960]{1,0:T(8,128)(2,1)} %get-tuple-element.79.n1b, bf16[5,512,320]{2,1,0:T(8,128)(2,1)} %get-tuple-element.80.dpa, ...), custom_call_target="tpu_custom_call" | custom-call | flops 2000000000 | bytes 13762576 | tf_op jit(solution)/shard_map/pallas_call | solution.py:267
  292.1 2.8 dynamic-slice_add_fusion.2
  294.9 4.8 collective-permute-start.20
  299.7 25.4 %collective-permute-done.29 = f32[320,960]{1,0:T(8,128)} collective-permute-done((f32[320,960]{1,0:T(8,128)}, f32[320,960]{1,0:T(8,128)}, u32[]{:S(2)}, u32[]{:S(2)}) %collective-permute-start.29) | collective-permute-done | bytes 1228832 | tf_op jit(solution)/shard_map/ppermute | solution.py:295
  327.0 4.8 collective-permute-start.30
  331.8 2.5 dynamic-slice_add_fusion.1
  338.1 14.7 %collective-permute-done.9 = f32[960,320]{0,1:T(8,128)} collective-permute-done((f32[960,320]{0,1:T(8,128)}, f32[960,320]{0,1:T(8,128)}, u32[]{:S(2)}, u32[]{:S(2)}) %collective-permute-start.9) | collective-permute-done | bytes 1228832 | tf_op jit(solution)/shard_map/ppermute | solution.py:295
  352.8 3.0 add.159
  355.8 4.8 collective-permute-start.10
  360.6 2.8 add.170
  370.4 15.9 %collective-permute-done.25 = f32[480,640]{1,0:T(8,128)} collective-permute-done((f32[480,640]{1,0:T(8,128)}, f32[480,640]{1,0:T(8,128)}, u32[]{:S(2)}, u32[]{:S(2)}) %collective-permute-start.25) | collective-permute-done | bytes 1228832 | tf_op jit(solution)/shard_map/ppermute | solution.py:295
  386.4 2.8 add.173
  390.9 21.9 %collective-permute-done.10 = f32[960,320]{0,1:T(8,128)} collective-permute-done((f32[960,320]{0,1:T(8,128)}, f32[960,320]{0,1:T(8,128)}, u32[]{:S(2)}, u32[]{:S(2)}) %collective-permute-start.10) | collective-permute-done | bytes 1228832 | tf_op jit(solution)/shard_map/ppermute | solution.py:295
  416.5 2.9 add.171
  422.1 8.2 %collective-permute-start.15 = (f32[192,960]{1,0:T(8,128)S(1)}, f32[192,960]{1,0:T(8,128)}, u32[]{:S(2)}, u32[]{:S(2)}) collective-permute-start(f32[192,960]{1,0:T(8,128)S(1)} %dynamic-slice_add_fusion.6), channel_id=1, source_target_pairs={{0,8},{1,9},{2,10},{3,11},{4,12},{5,13},{6,14},{7,15},{24,16},{25,... | collective-permute-start | bytes 2211848 | tf_op jit(solution)/shard_map/ppermute | solution.py:295
  433.2 2.8 add.174
  437.3 7.1 %collective-permute-done.15 = f32[192,960]{1,0:T(8,128)} collective-permute-done((f32[192,960]{1,0:T(8,128)S(1)}, f32[192,960]{1,0:T(8,128)}, u32[]{:S(2)}, u32[]{:S(2)}) %collective-permute-start.15) | collective-permute-done | bytes 737312 | tf_op jit(solution)/shard_map/ppermute | solution.py:295
  450.4 19.4 %all-reduce.2.cloned.1.call-done = f32[512,960]{1,0:T(8,128)} async-done(((f32[512,960]{1,0:T(8,128)}), f32[512,960]{1,0:T(8,128)}) %all-reduce.2.cloned.1.call-update) | async-done | bytes 1966096 | tf_op jit(solution)/shard_map/psum | solution.py:420
  469.9 3.5 add_convert_fusion
  475.7 2.5 broadcast_select_fusion.3
  481.4 2.6 broadcast_select_fusion
  488.0 19.7 %collective-permute-done.27 = f32[480,640]{1,0:T(8,128)} collective-permute-done((f32[480,640]{1,0:T(8,128)}, f32[480,640]{1,0:T(8,128)}, u32[]{:S(2)}, u32[]{:S(2)}) %collective-permute-start.27) | collective-permute-done | bytes 1228832 | tf_op jit(solution)/shard_map/ppermute | solution.py:295
  507.7 2.4 broadcast_select_fusion.2
  511.7 24.1 %collective-permute-done.12 = f32[960,320]{0,1:T(8,128)} collective-permute-done((f32[960,320]{0,1:T(8,128)S(1)}, f32[960,320]{0,1:T(8,128)}, u32[]{:S(2)}, u32[]{:S(2)}) %collective-permute-start.12) | collective-permute-done | bytes 1228832 | tf_op jit(solution)/shard_map/ppermute | solution.py:295
  535.8 2.6 broadcast_select_fusion.1
  542.2 66.6 %psum.15 = f32[2,960]{1,0:T(2,128)S(1)} all-reduce(f32[2,960]{1,0:T(2,128)S(1)} %pad_maximum_fusion), channel_id=1, replica_groups=mesh['wide'=8,'narrow'=4] {'wide'}, use_global_device_ids=true, to_apply=%region_4.5 | all-reduce | flops 1920 | bytes 15360 | tf_op jit(solution)/shard_map/psum | solution.py:416
  610.7 3.1 maximum_select_fusion
  615.8 4.2 maximum_select_fusion.2
  620.0 4.3 maximum_select_fusion.3
  624.3 2.8 maximum_select_fusion.7
  627.1 4.8 maximum_select_fusion.1
  631.9 4.1 select_n.212
  (150 shorter events, 100.6 us)
Async XLA Ops:
  7.2 462.7 %all-reduce.2.cloned.1.call-start = ((), (), s32[]{:S(2)}) async-start(), calls=%async_computation | async-start | bytes 4194304 | tf_op jit(solution)/shard_map/psum | solution.py:420
  9.5 5.9 copy-start.14
  9.5 5.9 copy-start.13
  9.5 6.8 %copy-start.7 = (bf16[640,960]{0,1:T(8,128)(2,1)S(1)}, bf16[640,960]{0,1:T(8,128)(2,1)}, u32[]{:S(2)}) copy-start(bf16[640,960]{0,1:T(8,128)(2,1)} %param.18) | copy-start | bytes 3686404
  44.8 2.7 collective-permute-start
  49.6 25.0 %collective-permute-start.1 = (f32[256,960]{0,1:T(8,128)S(1)}, f32[256,960]{0,1:T(8,128)S(1)}, u32[]{:S(2)}, u32[]{:S(2)}) collective-permute-start(f32[256,960]{0,1:T(8,128)S(1)} %copy.151), channel_id=1, source_target_pairs={{0,2},{1,3},{2,0},{3,1},{4,6},{5,7},{6,4},{7,5},{8,10},{9,11},{10,... | collective-permute-start | bytes 2949128 | tf_op jit(solution)/shard_map/ppermute | solution.py:295
  76.4 2.8 collective-permute-start.2
  110.6 2.6 collective-permute-start.3
  115.3 23.9 %collective-permute-start.4 = (f32[256,960]{0,1:T(8,128)S(1)}, f32[256,960]{0,1:T(8,128)S(1)}, u32[]{:S(2)}, u32[]{:S(2)}) collective-permute-start(f32[256,960]{0,1:T(8,128)S(1)} %copy.162), channel_id=1, source_target_pairs={{0,2},{1,3},{2,0},{3,1},{4,6},{5,7},{6,4},{7,5},{8,10},{9,11},{10,... | collective-permute-start | bytes 2949128 | tf_op jit(solution)/shard_map/ppermute | solution.py:295
  140.0 2.6 collective-permute-start.5
  192.8 2.6 collective-permute-start.6
  197.5 23.9 %collective-permute-start.7 = (f32[256,960]{0,1:T(8,128)S(1)}, f32[256,960]{0,1:T(8,128)S(1)}, u32[]{:S(2)}, u32[]{:S(2)}) collective-permute-start(f32[256,960]{0,1:T(8,128)S(1)} %copy.173), channel_id=1, source_target_pairs={{0,2},{1,3},{2,0},{3,1},{4,6},{5,7},{6,4},{7,5},{8,10},{9,11},{10,... | collective-permute-start | bytes 2949128 | tf_op jit(solution)/shard_map/ppermute | solution.py:295
  222.2 25.9 %collective-permute-start.8 = (f32[256,960]{0,1:T(8,128)S(1)}, f32[256,960]{0,1:T(8,128)S(1)}, u32[]{:S(2)}, u32[]{:S(2)}) collective-permute-start(f32[256,960]{0,1:T(8,128)S(1)} %copy.175), channel_id=1, source_target_pairs={{0,1},{1,0},{2,3},{3,2},{4,5},{5,4},{6,7},{7,6},{8,9},{9,8},{10,11... | collective-permute-start | bytes 2949128 | tf_op jit(solution)/shard_map/ppermute | solution.py:295
  238.0 7.0 %copy-start.3 = (f32[640,960]{1,0:T(8,128)S(1)}, f32[640,960]{1,0:T(8,128)}, u32[]{:S(2)}) copy-start(f32[640,960]{1,0:T(8,128)} %get-tuple-element.100) | copy-start | bytes 7372804
  240.6 51.5 %collective-permute-start.19 = (f32[480,640]{1,0:T(8,128)}, f32[480,640]{1,0:T(8,128)}, u32[]{:S(2)}, u32[]{:S(2)}) collective-permute-start(f32[480,640]{1,0:T(8,128)} %constant_dynamic-slice_fusion.2), channel_id=1, source_target_pairs={{0,4},{1,5},{2,6},{3,7},{4,0},{5,1},{6,2},{7,3},{8,12},{9,13},{10,... | collective-permute-start | bytes 3686408 | tf_op jit(solution)/shard_map/ppermute | solution.py:295
  244.7 87.1 %collective-permute-start.24 = (f32[480,640]{1,0:T(8,128)}, f32[480,640]{1,0:T(8,128)}, u32[]{:S(2)}, u32[]{:S(2)}) collective-permute-start(f32[480,640]{1,0:T(8,128)} %constant_dynamic-slice_fusion.1), channel_id=1, source_target_pairs={{0,4},{1,5},{2,6},{3,7},{4,0},{5,1},{6,2},{7,3},{8,12},{9,13},{10,... | collective-permute-start | bytes 3686408 | tf_op jit(solution)/shard_map/ppermute | solution.py:295
  246.1 79.0 %collective-permute-start.29 = (f32[320,960]{1,0:T(8,128)}, f32[320,960]{1,0:T(8,128)}, u32[]{:S(2)}, u32[]{:S(2)}) collective-permute-start(f32[320,960]{1,0:T(8,128)} %constant_dynamic-slice_fusion), channel_id=1, source_target_pairs={{0,4},{1,5},{2,6},{3,7},{4,0},{5,1},{6,2},{7,3},{8,12},{9,13},{10,... | collective-permute-start | bytes 3686408 | tf_op jit(solution)/shard_map/ppermute | solution.py:295
  291.8 61.0 %collective-permute-start.9 = (f32[960,320]{0,1:T(8,128)}, f32[960,320]{0,1:T(8,128)}, u32[]{:S(2)}, u32[]{:S(2)}) collective-permute-start(f32[960,320]{0,1:T(8,128)} %copy.189), channel_id=1, source_target_pairs={{0,4},{1,5},{2,6},{3,7},{4,0},{5,1},{6,2},{7,3},{8,12},{9,13},{10,... | collective-permute-start | bytes 3686408 | tf_op jit(solution)/shard_map/ppermute | solution.py:295
  294.9 65.7 %collective-permute-start.20 = (f32[480,640]{1,0:T(8,128)}, f32[480,640]{1,0:T(8,128)}, u32[]{:S(2)}, u32[]{:S(2)}) collective-permute-start(f32[480,640]{1,0:T(8,128)} %dynamic-slice_add_fusion.2), channel_id=1, source_target_pairs={{0,8},{1,9},{2,10},{3,11},{4,12},{5,13},{6,14},{7,15},{24,16},{25,... | collective-permute-start | bytes 3686408 | tf_op jit(solution)/shard_map/ppermute | solution.py:295
  299.7 32.1 %copy-start.4 = (f32[960,640]{1,0:T(8,128)S(1)}, f32[960,640]{1,0:T(8,128)}, u32[]{:S(2)}) copy-start(f32[960,640]{1,0:T(8,128)} %get-tuple-element.99) | copy-start | bytes 7372804
  327.0 38.2 %collective-permute-start.30 = (f32[320,960]{1,0:T(8,128)S(1)}, f32[320,960]{1,0:T(8,128)}, u32[]{:S(2)}, u32[]{:S(2)}) collective-permute-start(f32[320,960]{1,0:T(8,128)S(1)} %dynamic-slice_add_fusion), channel_id=1, source_target_pairs={{0,8},{1,9},{2,10},{3,11},{4,12},{5,13},{6,14},{7,15},{24,16},{25,... | collective-permute-start | bytes 3686408 | tf_op jit(solution)/shard_map/ppermute | solution.py:295
  334.3 52.1 %collective-permute-start.25 = (f32[480,640]{1,0:T(8,128)}, f32[480,640]{1,0:T(8,128)}, u32[]{:S(2)}, u32[]{:S(2)}) collective-permute-start(f32[480,640]{1,0:T(8,128)} %dynamic-slice_add_fusion.1), channel_id=1, source_target_pairs={{0,8},{1,9},{2,10},{3,11},{4,12},{5,13},{6,14},{7,15},{24,16},{25,... | collective-permute-start | bytes 3686408 | tf_op jit(solution)/shard_map/ppermute | solution.py:295
  355.8 56.9 %collective-permute-start.10 = (f32[960,320]{0,1:T(8,128)}, f32[960,320]{0,1:T(8,128)}, u32[]{:S(2)}, u32[]{:S(2)}) collective-permute-start(f32[960,320]{0,1:T(8,128)} %add.159), channel_id=1, source_target_pairs={{0,8},{1,9},{2,10},{3,11},{4,12},{5,13},{6,14},{7,15},{24,16},{25,... | collective-permute-start | bytes 3686408 | tf_op jit(solution)/shard_map/ppermute | solution.py:295
  363.4 53.0 %collective-permute-start.21 = (f32[480,640]{1,0:T(8,128)}, f32[480,640]{1,0:T(8,128)}, u32[]{:S(2)}, u32[]{:S(2)}) collective-permute-start(f32[480,640]{1,0:T(8,128)} %add.170), channel_id=1, source_target_pairs={{8,16},{9,17},{10,18},{11,19},{12,20},{13,21},{14,22},{15,23},{16,... | collective-permute-start | bytes 3686408 | tf_op jit(solution)/shard_map/ppermute | solution.py:295
  365.2 3.6 copy-start.5
  366.8 22.4 %copy-start.1 = (f32[320,960]{1,0:T(8,128)}, f32[320,960]{1,0:T(8,128)S(1)}, u32[]{:S(2)}) copy-start(f32[320,960]{1,0:T(8,128)S(1)} %add.178) | copy-start | bytes 3686404
  366.8 63.5 %collective-permute-start.31 = (f32[320,960]{1,0:T(8,128)S(1)}, f32[320,960]{1,0:T(8,128)}, u32[]{:S(2)}, u32[]{:S(2)}) collective-permute-start(f32[320,960]{1,0:T(8,128)S(1)} %add.178), channel_id=1, source_target_pairs={{8,16},{9,17},{10,18},{11,19},{12,20},{13,21},{14,22},{15,23},{16,... | collective-permute-start | bytes 3686408 | tf_op jit(solution)/shard_map/ppermute | solution.py:295
  368.9 52.0 %collective-permute-start.14 = (f32[192,960]{1,0:T(8,128)S(1)}, f32[192,960]{1,0:T(8,128)}, u32[]{:S(2)}, u32[]{:S(2)}) collective-permute-start(f32[192,960]{1,0:T(8,128)S(1)} %constant_dynamic-slice_fusion.3), channel_id=1, source_target_pairs={{0,4},{1,5},{2,6},{3,7},{4,0},{5,1},{6,2},{7,3},{8,12},{9,13},{10,... | collective-permute-start | bytes 2211848 | tf_op jit(solution)/shard_map/ppermute | solution.py:295
  389.2 44.0 %collective-permute-start.26 = (f32[480,640]{1,0:T(8,128)}, f32[480,640]{1,0:T(8,128)}, u32[]{:S(2)}, u32[]{:S(2)}) collective-permute-start(f32[480,640]{1,0:T(8,128)} %add.173), channel_id=1, source_target_pairs={{8,16},{9,17},{10,18},{11,19},{12,20},{13,21},{14,22},{15,23},{16,... | collective-permute-start | bytes 3686408 | tf_op jit(solution)/shard_map/ppermute | solution.py:295
  414.7 4.7 copy-start
  414.7 32.5 %collective-permute-start.11 = (f32[960,320]{0,1:T(8,128)S(1)}, f32[960,320]{0,1:T(8,128)}, u32[]{:S(2)}, u32[]{:S(2)}) collective-permute-start(f32[960,320]{0,1:T(8,128)S(1)} %add.160), channel_id=1, source_target_pairs={{8,16},{9,17},{10,18},{11,19},{12,20},{13,21},{14,22},{15,23},{16,... | collective-permute-start | bytes 3686408 | tf_op jit(solution)/shard_map/ppermute | solution.py:295
  416.4 4.4 copy-start.6
  419.4 10.9 %copy-start.2 = (f32[320,960]{1,0:T(8,128)S(1)}, f32[320,960]{1,0:T(8,128)}, u32[]{:S(2)}) copy-start(f32[320,960]{1,0:T(8,128)} %copy-done.1) | copy-start | bytes 3686404
  419.4 56.3 %collective-permute-start.22 = (f32[480,640]{1,0:T(8,128)}, f32[480,640]{1,0:T(8,128)}, u32[]{:S(2)}, u32[]{:S(2)}) collective-permute-start(f32[480,640]{1,0:T(8,128)} %add.171), channel_id=1, source_target_pairs={{8,0},{9,1},{10,2},{11,3},{12,4},{13,5},{14,6},{15,7},{16,24},{17,... | collective-permute-start | bytes 3686408 | tf_op jit(solution)/shard_map/ppermute | solution.py:295
  422.1 22.3 %collective-permute-start.15 = (f32[192,960]{1,0:T(8,128)S(1)}, f32[192,960]{1,0:T(8,128)}, u32[]{:S(2)}, u32[]{:S(2)}) collective-permute-start(f32[192,960]{1,0:T(8,128)S(1)} %dynamic-slice_add_fusion.6), channel_id=1, source_target_pairs={{0,8},{1,9},{2,10},{3,11},{4,12},{5,13},{6,14},{7,15},{24,16},{25,... | collective-permute-start | bytes 2211848 | tf_op jit(solution)/shard_map/ppermute | solution.py:295
  431.9 49.5 %collective-permute-start.32 = (f32[320,960]{1,0:T(8,128)S(1)}, f32[320,960]{1,0:T(8,128)}, u32[]{:S(2)}, u32[]{:S(2)}) collective-permute-start(f32[320,960]{1,0:T(8,128)S(1)} %add.179), channel_id=1, source_target_pairs={{8,0},{9,1},{10,2},{11,3},{12,4},{13,5},{14,6},{15,7},{16,24},{17,... | collective-permute-start | bytes 3686408 | tf_op jit(solution)/shard_map/ppermute | solution.py:295
  436.0 71.7 %collective-permute-start.27 = (f32[480,640]{1,0:T(8,128)}, f32[480,640]{1,0:T(8,128)}, u32[]{:S(2)}, u32[]{:S(2)}) collective-permute-start(f32[480,640]{1,0:T(8,128)} %add.174), channel_id=1, source_target_pairs={{8,0},{9,1},{10,2},{11,3},{12,4},{13,5},{14,6},{15,7},{16,24},{17,... | collective-permute-start | bytes 3686408 | tf_op jit(solution)/shard_map/ppermute | solution.py:295
  446.5 38.9 %collective-permute-start.16 = (f32[192,960]{1,0:T(8,128)}, f32[192,960]{1,0:T(8,128)S(1)}, u32[]{:S(2)}, u32[]{:S(2)}) collective-permute-start(f32[192,960]{1,0:T(8,128)} %add.165), channel_id=1, source_target_pairs={{8,16},{9,17},{10,18},{11,19},{12,20},{13,21},{14,22},{15,23},{16,... | collective-permute-start | bytes 2211848 | tf_op jit(solution)/shard_map/ppermute | solution.py:295
  449.1 86.7 %collective-permute-start.12 = (f32[960,320]{0,1:T(8,128)S(1)}, f32[960,320]{0,1:T(8,128)}, u32[]{:S(2)}, u32[]{:S(2)}) collective-permute-start(f32[960,320]{0,1:T(8,128)S(1)} %add.161), channel_id=1, source_target_pairs={{8,0},{9,1},{10,2},{11,3},{12,4},{13,5},{14,6},{15,7},{16,24},{17,... | collective-permute-start | bytes 3686408 | tf_op jit(solution)/shard_map/ppermute | solution.py:295
  473.4 2.3 copy-start.12
  473.4 2.3 copy-start.9
  473.4 2.3 copy-start.11
  478.2 137.7 %collective-permute-start.23 = (f32[480,640]{1,0:T(8,128)}, f32[480,640]{1,0:T(8,128)}, u32[]{:S(2)}, u32[]{:S(2)}) collective-permute-start(f32[480,640]{1,0:T(8,128)} %broadcast_select_fusion.3), channel_id=1, source_target_pairs={{0,4},{1,5},{2,6},{3,7},{4,0},{5,1},{6,2},{7,3},{8,12},{9,13},{10,... | collective-permute-start | bytes 3686408 | tf_op jit(solution)/shard_map/ppermute | solution.py:295
  483.9 126.8 %collective-permute-start.33 = (f32[320,960]{1,0:T(8,128)}, f32[320,960]{1,0:T(8,128)}, u32[]{:S(2)}, u32[]{:S(2)}) collective-permute-start(f32[320,960]{1,0:T(8,128)} %broadcast_select_fusion), channel_id=1, source_target_pairs={{0,4},{1,5},{2,6},{3,7},{4,0},{5,1},{6,2},{7,3},{8,12},{9,13},{10,... | collective-permute-start | bytes 3686408 | tf_op jit(solution)/shard_map/ppermute | solution.py:295
  486.7 122.1 %collective-permute-start.17 = (f32[192,960]{1,0:T(8,128)S(1)}, f32[192,960]{1,0:T(8,128)}, u32[]{:S(2)}, u32[]{:S(2)}) collective-permute-start(f32[192,960]{1,0:T(8,128)S(1)} %add.166), channel_id=1, source_target_pairs={{8,0},{9,1},{10,2},{11,3},{12,4},{13,5},{14,6},{15,7},{16,24},{17,... | collective-permute-start | bytes 2211848 | tf_op jit(solution)/shard_map/ppermute | solution.py:295
  510.2 109.9 %collective-permute-start.28 = (f32[480,640]{1,0:T(8,128)}, f32[480,640]{1,0:T(8,128)}, u32[]{:S(2)}, u32[]{:S(2)}) collective-permute-start(f32[480,640]{1,0:T(8,128)} %broadcast_select_fusion.2), channel_id=1, source_target_pairs={{0,4},{1,5},{2,6},{3,7},{4,0},{5,1},{6,2},{7,3},{8,12},{9,13},{10,... | collective-permute-start | bytes 3686408 | tf_op jit(solution)/shard_map/ppermute | solution.py:295
  538.4 88.7 %collective-permute-start.13 = (f32[960,320]{0,1:T(8,128)}, f32[960,320]{0,1:T(8,128)}, u32[]{:S(2)}, u32[]{:S(2)}) collective-permute-start(f32[960,320]{0,1:T(8,128)} %broadcast_select_fusion.1), channel_id=1, source_target_pairs={{0,4},{1,5},{2,6},{3,7},{4,0},{5,1},{6,2},{7,3},{8,12},{9,13},{10,... | collective-permute-start | bytes 3686408 | tf_op jit(solution)/shard_map/ppermute | solution.py:295
  610.0 14.3 %collective-permute-start.18 = (f32[192,960]{1,0:T(8,128)S(1)}, f32[192,960]{1,0:T(8,128)}, u32[]{:S(2)}, u32[]{:S(2)}) collective-permute-start(f32[192,960]{1,0:T(8,128)S(1)} %broadcast_select_fusion.4), channel_id=1, source_target_pairs={{0,4},{1,5},{2,6},{3,7},{4,0},{5,1},{6,2},{7,3},{8,12},{9,13},{10,... | collective-permute-start | bytes 2211848 | tf_op jit(solution)/shard_map/ppermute | solution.py:295
  (3 other events, 5.7 us)
Sparse Core Ops, SparseCore 0:
  416.6 53.2 all-reduce.1

commit v2 on v1

v2 whole, which is shorter than its diff:
```python
import functools
import math

import jax
import jax.numpy as jnp
from jax import lax
from jax.experimental import pallas as pl
from jax.experimental.pallas import tpu as pltpu
from jax.sharding import PartitionSpec as P

HEAD = 64
Q_PER = 3
SLOTS = 2
EPS = 1e-05
THETA = 10000.0
RB = 128
VMEM = 56
F32 = jnp.float32
BF16 = jnp.bfloat16
NEG = -1e30


def dot(a, b):
    return jnp.dot(a, b, preferred_element_type=F32)


def dot_nt(a, b):
    return lax.dot_general(a, b, (((1,), (1,)), ((), ())), preferred_element_type=F32)


def dot_tn(a, b):
    return lax.dot_general(a, b, (((0,), (0,)), ((), ())), preferred_element_type=F32)


def lane_iota(rows):
    return lax.broadcasted_iota(jnp.int32, (rows, 128), 1)


def low_half(rows):
    return lane_iota(rows) < HEAD


def rope128(v, cs, sn):
    lane = lane_iota(v.shape[0])
    partner = jnp.where((lane & 63) < 32, pltpu.roll(v, 96, 1), pltpu.roll(v, 32, 1))
    return v * cs + partner * sn


def allowed_bias(seqr_ref, valr_ref, r0, nk):
    t = r0 + lax.broadcasted_iota(jnp.int32, (RB, nk), 0)
    u = lax.broadcasted_iota(jnp.int32, (RB, nk), 1)
    mine = jnp.broadcast_to(seqr_ref[:, r0 : r0 + RB].astype(F32), (128, RB)).T[:, :1]
    same = mine == seqr_ref[:, :nk].astype(F32)
    ok = (same & (u <= t) & (valr_ref[:, :nk] == 1)) | (u == t)
    return jnp.where(ok, 0.0, NEG).astype(F32)


def masked_heads(x, y):
    low = low_half(1).astype(F32)
    low_b, high_b = low.astype(BF16), (1.0 - low).astype(BF16)
    return jnp.concatenate([x * low_b, x * high_b, y * low_b], axis=0)


def pack_half(xi, a, b):
    low = low_half(a.shape[0])
    at, bt = a[:, 512:], b[:, 512:]
    if xi == 0:
        return a[:, :256], b[:, :256], jnp.where(low, at, pltpu.roll(bt, 64, 1))
    return a[:, 256:512], b[:, 256:512], jnp.where(low, pltpu.roll(at, 64, 1), bt)


def store_pair(idx, ref, rows, a, b):
    for xi in range(2):
        @pl.when(idx[0] == xi)
        def _():
            p, q, r = pack_half(xi, a, b)
            ref[rows, :256] = p.astype(ref.dtype)
            ref[rows, 256:512] = q.astype(ref.dtype)
            ref[rows, 512:] = r.astype(ref.dtype)


def store_one(idx, ref, rows, a):
    low = low_half(a.shape[0])
    at = a[:, 512:]
    for xi in range(2):
        @pl.when(idx[0] == xi)
        def _():
            ref[rows, :256] = a[:, xi * 256 : xi * 256 + 256].astype(ref.dtype)
            ref[rows, 256:] = jnp.where(low, at if xi == 0 else pltpu.roll(at, 64, 1), 0.0).astype(ref.dtype)


def ffn_back(dhid, gate, up, sig):
    return dhid * up * sig * (1.0 + gate * (1.0 - sig)), dhid * (gate * sig)


def put_wide(ref, v):
    d = v.shape[1]
    ref[:, :d] = v
    if ref.shape[1] > d:
        ref[:, d:] = jnp.zeros((ref.shape[0], ref.shape[1] - d), ref.dtype)


def half_rows(ref, which, n):
    return ref[pl.ds(pl.multiple_of(which * n, 8), n), :]


def split_send(idx, whole, keep, send):
    n = keep.shape[0]
    put_wide(keep, half_rows(whole, idx[1], n))
    put_wide(send, half_rows(whole, 1 - idx[1], n))


def take_sum(idx, pieces, out):
    d = out.shape[1]
    if len(pieces) == 1:
        out[...] = pieces[0][:, :d]
        return
    n = pieces[0].shape[0]
    out[pl.ds(pl.multiple_of(idx[1] * n, n), n), :] = pieces[0][:, :d]
    out[pl.ds(pl.multiple_of((1 - idx[1]) * n, n), n), :] = pieces[1][:, :d]


class Late:
    def __init__(self, source, buffer, sems, at, grouped):
        self.source, self.buffer, self.sems, self.at, self.grouped = source, buffer, sems, at, grouped
        self.waited = False

    def copy(self, g=None):
        if g is None:
            return pltpu.make_async_copy(self.source, self.buffer, self.sems.at[self.at])
        return pltpu.make_async_copy(self.source.at[g], self.buffer.at[g], self.sems.at[self.at + g])

    def start(self):
        if self.grouped:
            for g in range(self.buffer.shape[0]):
                self.copy(g).start()
        else:
            self.copy().start()

    def wait(self):
        if not self.waited:
            self.copy().wait()
            self.waited = True
        return self.buffer


def ready(*refs):
    got = [r.wait() if isinstance(r, Late) else r for r in refs]
    return got if len(got) > 1 else got[0]


def ready_group(g, *refs):
    for r in refs:
        r.copy(g).wait()


def buffers(*refs):
    return [r.buffer for r in refs]


def fwd_kernel(second, split, part, groups, *refs):
    it = iter(refs)
    idx = next(it)
    x_ref = next(it)
    add_refs = [next(it) for _ in range(2 if split else 1)] if second else None
    win, wout, g1, g2, cs_ref, sn_ref, seqr, valr, wg, wu, wdt = (next(it) for _ in range(11))
    kt_old, vt_old, n2_old = (next(it) for _ in range(3)) if part else (None, None, None)
    cot = next(it) if second else None
    n1_ref, qk_ref, kt_ref, vt_ref, o_ref, lse_ref, h_ref, n2_ref, hidh_ref = (next(it) for _ in range(9))
    n2s_ref = next(it) if part else None
    x_out = next(it)
    if second:
        duh_ref, part_ref = next(it), next(it)
    else:
        gate_ref, up_ref = next(it), next(it)
    outs = [next(it) for _ in range(2 if split else 1)]
    acc, whole, ktf, vtf = (next(it) for _ in range(4))
    t = n1_ref.shape[0]
    base = part * t

    if second:
        take_sum(idx, add_refs, acc)
        x = x_ref[...] + acc[...]
        x_out[...] = x
    else:
        x = x_ref[:, base : base + t].astype(F32).T
        x_out[...] = x.astype(BF16)
    r1 = lax.rsqrt(jnp.mean(x * x, axis=1, keepdims=True) + EPS)
    n1_ref[...] = (x * r1 * g1[...]).astype(BF16)
    acc[...] = x
    flush(n1_ref)
    flush(x_out)
    lse_ref[...] = jnp.zeros_like(lse_ref)
    cs_ref, sn_ref = ready(cs_ref, sn_ref)
    win_l, wout_l = win, wout
    win, wout = buffers(win, wout)

    def group(g, carry):
        ready_group(g, win_l, wout_l)
        n1 = n1_ref[...]
        qk = dot_nt(n1, win[g, :256, :])
        v = dot_nt(n1, win[g, 256:320, :])
        cs, sn = cs_ref[base : base + t, :], sn_ref[base : base + t, :]
        xr = rope128(qk[:, :128], cs, sn)
        yr = rope128(qk[:, 128:], cs, sn)
        qk_ref[g, :, :128] = xr.astype(BF16)
        qk_ref[g, :, 128:] = yr.astype(BF16)
        kt = jnp.where(low_half(t), pltpu.roll(yr, 64, 1), yr).astype(BF16)
        vt = jnp.concatenate([v, v], axis=1).astype(BF16)
        kt_ref[g] = kt
        vt_ref[g] = vt
        if part:
            ktf[:base, :] = kt_old[g]
            vtf[:base, :] = vt_old[g]
        ktf[base : base + t, :] = kt
        vtf[base : base + t, :] = vt
        for rb in range(t // RB):
            r0 = rb * RB
            nk = base + r0 + RB
            rows = slice(r0, r0 + RB)
            q = masked_heads(qk_ref[g, rows, :128], qk_ref[g, rows, 128:])
            s = dot_nt(q, ktf[:nk, :])
            bias = allowed_bias(seqr, valr, base + r0, nk)
            s = (s.reshape(3, RB, nk) * 0.125 + bias[None]).reshape(3 * RB, nk)
            m = jnp.max(s, axis=1, keepdims=True)
            e = jnp.exp(s - m)
            l = jnp.sum(e, axis=1, keepdims=True)
            o = dot(e.astype(BF16), vtf[:nk, :]) / l
            low = low_half(RB)
            o_ref[g, rows, :128] = jnp.where(low, o[:RB], o[RB : 2 * RB]).astype(BF16)
            o_ref[g, rows, 128:] = jnp.where(low, o[2 * RB :], 0.0).astype(BF16)
            ls = m + jnp.log(l)
            lane = lane_iota(RB)
            cur = lse_ref[rows, :]
            for j in range(3):
                cur = jnp.where(lane == g * 3 + j, ls[j * RB : (j + 1) * RB], cur)
            lse_ref[rows, :] = cur
        acc[...] += dot(o_ref[g, :, :192], wout[g])
        return carry

    lax.fori_loop(0, groups, group, 0)
    for ref in (qk_ref, kt_ref, vt_ref, o_ref, lse_ref):
        flush(ref)
    h = acc[...]
    h_ref[...] = h
    flush(h_ref)
    r2 = lax.rsqrt(jnp.mean(h * h, axis=1, keepdims=True) + EPS)
    n2 = (h * r2 * g2[...]).astype(BF16)
    n2_ref[...] = n2
    flush(n2_ref)
    if part:
        n2_old = ready(n2_old)
        if split:
            for c in range(2):
                @pl.when(idx[1] == c)
                def _():
                    put_wide(n2s_ref, (n2_old if c == 0 else n2_ref)[...].astype(F32))
        else:
            put_wide(n2s_ref.at[:t, :], n2_old[...].astype(F32))
            put_wide(n2s_ref.at[t:, :], n2_ref[...].astype(F32))
    if part:
        flush(n2s_ref)
    wg, wu, wdt = ready(wg, wu, wdt)
    every = slice(0, t)
    gate = dot(n2, wg[...])
    up = dot(n2, wu[...])
    sig = jax.nn.sigmoid(gate)
    hid = gate * sig * up
    store_one(idx, hidh_ref, every, hid)
    flush(hidh_ref)
    if second:
        cot = ready(cot)
        part_ref[...] = dot_nt(hid.astype(BF16), wdt[...])
        flush(part_ref)
        dgate, dup = ffn_back(dot(cot[base : base + t, :], wdt[...]), gate, up, sig)
        store_pair(idx, duh_ref, every, dgate, dup)
        flush(duh_ref)
        whole[...] = dot_nt(dgate.astype(BF16), wg[...]) + dot_nt(dup.astype(BF16), wu[...])
    else:
        gate_ref[...] = gate
        up_ref[...] = up
        flush(gate_ref)
        flush(up_ref)
        whole[...] = dot_nt(hid.astype(BF16), wdt[...])
    if split:
        split_send(idx, whole, *outs)
    else:
        put_wide(outs[0], whole[...])


def norm_back(dn, stream, gain):
    r = lax.rsqrt(jnp.mean(stream * stream, axis=1, keepdims=True) + EPS)
    m = stream * r
    dgain = jnp.sum(dn * m, axis=0, keepdims=True)
    dm = dn * gain
    return r * (dm - m * jnp.mean(dm * m, axis=1, keepdims=True)), dgain


def bwd_enter(idx, dn2_refs, dz_ref, h_ref, g2, dh_ref, da_ref, dg2_ref):
    take_sum(idx, dn2_refs, dh_ref)
    dh, dg2 = norm_back(dh_ref[...], h_ref[...], g2[...])
    dh = dz_ref[...].astype(F32) + dh
    dh_ref[...] = dh
    da_ref[...] = dh.astype(BF16)
    dg2_ref[...] = dg2


def bwd_block(g, r0, base, da, qk_ref, o_ref, lse_ref, ktf, vtf, wout, seqr, valr, dkv):
    low, lane = low_half(RB), lane_iota(RB)
    nk = base + r0 + RB
    rows = slice(r0, r0 + RB)
    do = dot_nt(da[rows], wout[g])
    dox = do[:, :128].astype(BF16)
    doy = jnp.concatenate([do[:, 128:192], jnp.zeros((RB, 64), F32)], axis=1).astype(BF16)
    px = dox.astype(F32) * o_ref[g, rows, :128].astype(F32)
    py = doy.astype(F32) * o_ref[g, rows, 128:].astype(F32)
    delta = jnp.concatenate(
        [
            jnp.sum(jnp.where(low, px, 0.0), axis=1, keepdims=True),
            jnp.sum(jnp.where(low, 0.0, px), axis=1, keepdims=True),
            jnp.sum(py, axis=1, keepdims=True),
        ],
        axis=0,
    )
    ls = lse_ref[rows, :]
    lse = jnp.concatenate(
        [jnp.sum(jnp.where(lane == g * 3 + j, ls, 0.0), axis=1, keepdims=True) for j in range(3)], axis=0
    )
    q = masked_heads(qk_ref[g, rows, :128], qk_ref[g, rows, 128:])
    dos = masked_heads(dox, doy)
    kt = ktf(nk)
    s = dot_nt(q, kt)
    dp = dot_nt(dos, vtf(nk))
    bias = allowed_bias(seqr, valr, base + r0, nk)
    s = (s.reshape(3, RB, nk) * 0.125 + bias[None]).reshape(3 * RB, nk)
    p = jnp.exp(s - lse)
    ds = (p * (dp - delta)).astype(BF16)
    dq = dot(ds, kt) * 0.125
    dkv[0, :nk, :] += dot_tn(ds, q)
    dkv[1, :nk, :] += dot_tn(p.astype(BF16), dos)
    return jnp.where(low, dq[:RB], dq[RB : 2 * RB]), dq[2 * RB :]


def bwd_a_kernel(split, groups, *refs):
    it = iter(refs)
    idx = next(it)
    dn2_refs = [next(it) for _ in range(2 if split else 1)]
    dz_ref, h_ref, qk_ref, kt_ref, vt_ref, o_ref, lse_ref, wout, g2, cs_ref, sn_ref, seqr, valr = (
        next(it) for _ in range(13))
    dh_ref, da_ref, dqx_ref, dqy_ref, dkv_ref, dg2_ref = (next(it) for _ in range(6))
    t = dh_ref.shape[0]
    bwd_enter(idx, dn2_refs, dz_ref, h_ref, g2, dh_ref, da_ref, dg2_ref)
    flush(dh_ref)
    flush(da_ref)
    dkv_ref[...] = jnp.zeros_like(dkv_ref)
    lse_ref, cs_ref, sn_ref = ready(lse_ref, cs_ref, sn_ref)
    waits = (qk_ref, kt_ref, vt_ref, o_ref, wout)
    qk_ref, kt_ref, vt_ref, o_ref, wout = buffers(*waits)

    def group(g, carry):
        ready_group(g, *waits)
        da = da_ref[...]
        for r0 in range(0, t, RB):
            rows = slice(r0, r0 + RB)
            dqx, dqy = bwd_block(g, r0, 0, da, qk_ref, o_ref, lse_ref, lambda n: kt_ref[g, :n, :],
                                 lambda n: vt_ref[g, :n, :], wout, seqr, valr, dkv_ref.at[g])
            dqx_ref[g, rows, :] = rope128(dqx, cs_ref[rows, :], -sn_ref[rows, :]).astype(BF16)
            dqy_ref[g, rows, :] = dqy
        return carry

    lax.fori_loop(0, groups, group, 0)


def bwd_b_kernel(last, split, groups, *refs):
    it = iter(refs)
    idx = next(it)
    dn2_refs = [next(it) for _ in range(2 if split else 1)]
    (dz_ref, h_ref, qk_ref, kt_ref, vt_ref, o_ref, lse_ref, xa_ref, xb_ref, kt_old, vt_old, dha_ref, dqxa_ref, dqya_ref,
     dkva_ref, win, wout, g1, g2, cs_ref, sn_ref, seqr, valr) = (next(it) for _ in range(23))
    da_ref, dpa_ref, dpb_ref, dxa_ref, dxb_ref, dg1_ref, dg2_ref = (next(it) for _ in range(7))
    dfs_ref = None if last else next(it)
    dh_ref, acca, accb, dkv, ktf, vtf, dqy_ref = (next(it) for _ in range(7))
    t = dh_ref.shape[0]
    bwd_enter(idx, dn2_refs, dz_ref, h_ref, g2, dh_ref, da_ref, dg2_ref)
    acca[...] = jnp.zeros_like(acca)
    flush(da_ref)
    accb[...] = jnp.zeros_like(accb)
    lse_ref, cs_ref, sn_ref = ready(lse_ref, cs_ref, sn_ref)
    waits = (qk_ref, kt_ref, vt_ref, o_ref, kt_old, vt_old, dqxa_ref, dqya_ref, dkva_ref, win, wout)
    qk_ref, kt_ref, vt_ref, o_ref, kt_old, vt_old, dqxa_ref, dqya_ref, dkva_ref, win, wout = buffers(*waits)

    def group(g, carry):
        ready_group(g, *waits)
        da = da_ref[...]
        ktf[:t, :] = kt_old[g]
        ktf[t:, :] = kt_ref[g]
        vtf[:t, :] = vt_old[g]
        vtf[t:, :] = vt_ref[g]
        dkv[:, :t, :] = dkva_ref[g]
        dkv[:, t:, :] = jnp.zeros((2, t, 128), F32)
        for r0 in range(0, t, RB):
            rows = slice(r0, r0 + RB)
            dqx, dqy = bwd_block(g, r0, t, da, qk_ref, o_ref, lse_ref, lambda n: ktf[:n, :], lambda n: vtf[:n, :],
                                 wout, seqr, valr, dkv)
            full = slice(t + r0, t + r0 + RB)
            dpb_ref[g, rows, :128] = rope128(dqx, cs_ref[full, :], -sn_ref[full, :]).astype(BF16)
            dqy_ref[rows, :] = dqy
        dpa_ref[g, :, :128] = dqxa_ref[g]
        low = low_half(t)
        for k, (ref, dqy) in enumerate(((dpa_ref, dqya_ref[g]), (dpb_ref, dqy_ref[...]))):
            rows = slice(k * t, k * t + t)
            dk, dv = dkv[0, rows, :], dkv[1, rows, :]
            dk = (dk + pltpu.roll(dk, 64, 1)) * 0.125
            dv = dv + pltpu.roll(dv, 64, 1)
            dy = jnp.where(low, dqy, dk)
            ref[g, :, 128:256] = rope128(dy, cs_ref[rows, :], -sn_ref[rows, :]).astype(BF16)
            ref[g, :, 256:320] = dv[:, :64].astype(BF16)
        acca[...] += dot(dpa_ref[g], win[g])
        accb[...] += dot(dpb_ref[g], win[g])
        return carry

    lax.fori_loop(0, groups, group, 0)
    flush(dpa_ref)
    flush(dpb_ref)
    xa_ref, xb_ref, dha_ref = ready(xa_ref, xb_ref, dha_ref)
    dxa, dg1a = norm_back(acca[...], xa_ref[...].astype(F32), g1[...])
    dxb, dg1b = norm_back(accb[...], xb_ref[...].astype(F32), g1[...])
    dg1_ref[...] = dg1a + dg1b
    dxa_ref[...] = (dxa + dha_ref[...]).astype(dxa_ref.dtype)
    dxb_ref[...] = (dxb + dh_ref[...]).astype(dxb_ref.dtype)
    flush(dxa_ref)
    flush(dxb_ref)
    if not last:
        if split:
            for c in range(2):
                @pl.when(idx[1] == c)
                def _():
                    put_wide(dfs_ref, (dxa_ref if c == 0 else dxb_ref)[...].astype(BF16).astype(F32))
        else:
            put_wide(dfs_ref.at[:t, :], dxa_ref[...].astype(BF16).astype(F32))
            put_wide(dfs_ref.at[t:, :], dxb_ref[...].astype(BF16).astype(F32))


def ffn_back_kernel(split, *refs):
    idx, dza, dzb, gatea, gateb, upa, upb, wg, wu, wdt, duha, duhb, dfa, dfb, *rest = refs
    outs, whole = rest[:-1], rest[-1]
    per = len(outs) // 2
    for k, (dz_ref, gate_ref, up_ref, duh_ref, df_ref) in enumerate(
            ((dza, gatea, upa, duha, dfa), (dzb, gateb, upb, duhb, dfb))):
        df = ready(dz_ref)[...].astype(BF16)
        df_ref[...] = df
        flush(df_ref)
        wdt, gate_ref, up_ref = ready(wdt, gate_ref, up_ref)
        gate, up = gate_ref[...], up_ref[...]
        dgate, dup = ffn_back(dot(df, wdt[...]), gate, up, jax.nn.sigmoid(gate))
        store_pair(idx, duh_ref, slice(0, df.shape[0]), dgate, dup)
        flush(duh_ref)
        wg, wu = ready(wg, wu)
        whole[...] = dot_nt(dgate.astype(BF16), wg[...]) + dot_nt(dup.astype(BF16), wu[...])
        if split:
            split_send(idx, whole, *outs[per * k : per * k + per])
        else:
            put_wide(outs[k], whole[...])
        for ref in outs[per * k : per * k + per]:
            flush(ref)


def own_grads(n2, duh, hidh, df, base, put):
    for r in range(0, n2[0].shape[1], 320):
        put(0, r, sum((dot_tn(a[:, r : r + 320], b[...]) for a, b in zip(n2, duh)), base(0, r)))
        put(1, r, sum((dot_tn(a[:, r : r + 320], b[...]) for a, b in zip(df, hidh)), base(1, r)))


def peer_acts(n2, df, wgu, wdh, du, hd, rows):
    gu = dot(n2, wgu[...])
    dh = dot(df, wdh[...])
    ga, ua, tile = gu[:, :256], gu[:, 256:512], gu[:, 512:]
    turned = pltpu.roll(tile, 64, 1)
    sa, sb = jax.nn.sigmoid(ga), jax.nn.sigmoid(tile)
    low = low_half(n2.shape[0])
    hd[rows, :256] = (ga * sa * ua).astype(BF16)
    hd[rows, 256:] = jnp.where(low, tile * sb * turned, 0.0).astype(BF16)
    dga, dua = ffn_back(dh[:, :256], ga, ua, sa)
    dgb, dub = ffn_back(dh[:, 256:], tile, turned, sb)
    du[rows, :256] = dga.astype(BF16)
    du[rows, 256:512] = dua.astype(BF16)
    du[rows, 512:] = jnp.where(low, dgb, pltpu.roll(dub, 64, 1)).astype(BF16)


def peer_grads(n2p, dfp, wgu, wdh, scratch, base, put):
    n2, df, du, hd = scratch
    d = n2.shape[1]
    n = n2p[0].shape[0]
    for i in range(len(n2p)):
        rows = slice(i * n, i * n + n)
        n2[rows, :] = n2p[i][:, :d].astype(BF16)
        df[rows, :] = dfp[i][:, :d].astype(BF16)
        for r in range(i * n, i * n + n, 256):
            part = slice(r, r + 256)
            peer_acts(n2[part, :], df[part, :], wgu, wdh, du, hd, part)
    own_grads([n2], [du], [hd], [df], base, put)


def own_grads_kernel(*refs):
    n2, duh, hidh, cot, outs = refs[:2], refs[2:4], refs[4:6], refs[6], refs[7:]
    t = n2[0].shape[0]

    def put(k, r, v):
        outs[k][r : r + 320, :] = v
        flush(outs[k], slice(r, r + 320))

    own_grads(n2, duh, hidh, [cot.at[:t, :], cot.at[t:, :]], lambda k, r: 0.0, put)


def both_grads_kernel(count, *refs):
    n2p, dfp = refs[:count], refs[count : 2 * count]
    wgu, wdh, *rest = refs[2 * count :]
    n2, duh, hidh, df = (rest[2 * k : 2 * k + 2] for k in range(4))
    old, outs, scratch = rest[8:10], rest[10:12], rest[12:]

    def put(k, r, v):
        outs[k][r : r + 320, :] = v

    def put_last(k, r, v):
        outs[k][r : r + 320, :] = v
        flush(outs[k], slice(r, r + 320))

    old = ready(*old)
    own_grads(n2, duh, hidh, df, lambda k, r: old[k][r : r + 320, :], put)
    n2p, dfp = [ready(r) for r in n2p], [ready(r) for r in dfp]
    wgu, wdh = ready(wgu, wdh)
    peer_grads(n2p, dfp, wgu, wdh, scratch, lambda k, r: outs[k][r : r + 320, :], put_last)


def last_grads_kernel(count, n_chunks, *refs):
    n2p, dfp = refs[:count], refs[count : 2 * count]
    wgu, wdh, *rest = refs[2 * count :]
    old, chunks, scratch = rest[:2], rest[2 : 2 + n_chunks], rest[2 + n_chunks : 6 + n_chunks]
    gu, dn = rest[6 + n_chunks :]

    def put(k, r, v):
        (gu, dn)[k][r : r + 320, :] = v

    peer_grads(n2p, dfp, wgu, wdh, scratch, lambda k, r: ready(old[k])[r : r + 320, :], put)
    at = 0
    half = dn.shape[0] // 2
    for out in chunks:
        n = out.shape[0]
        if at < gu.shape[0]:
            out[...] = gu[at : at + n, :]
        else:
            r = at - gu.shape[0]
            a, b = dn[r : r + n, :], dn[half + r : half + r + n, :]
            out[:, :256] = a[:, :256]
            out[:, 256:512] = b[:, :256]
            out[:, 512:] = jnp.where(low_half(n), a[:, 256:], pltpu.roll(b[:, 256:], 64, 1))
        flush(out)
        at += n


def unpack_kernel(count, stacked, *refs):
    idx = refs[0]
    own, other, outs = refs[1 : 1 + count], refs[1 + count : 1 + 2 * count], refs[1 + 2 * count :]
    at = 0
    for o, p in zip(own, other):
        o, p = ready(o, p)
        n = o.shape[0]
        for xi in range(2):
            @pl.when(idx[0] == xi)
            def _():
                a, b = (o, p) if xi == 0 else (p, o)
                low = low_half(n)
                at4, bt4 = a[:, 512:], b[:, 512:]
                firsts = jnp.where(low, at4, pltpu.roll(bt4, 64, 1))
                seconds = jnp.where(low, pltpu.roll(at4, 64, 1), bt4)
                for k, tile in ((0, firsts), (1, seconds)):
                    ref = outs[0] if stacked else outs[k]
                    r = at + (k * (ref.shape[0] // 2) if stacked else 0)
                    ref[r : r + n, :256] = a[:, 256 * k : 256 * k + 256]
                    ref[r : r + n, 256:512] = b[:, 256 * k : 256 * k + 256]
                    ref[r : r + n, 512:] = tile
        for k in range(2):
            ref = outs[0] if stacked else outs[k]
            r = at + (k * (ref.shape[0] // 2) if stacked else 0)
            flush(ref, slice(r, r + n))
        at += n


def attn_grad_kernel(idx, *refs):
    n1, dp, o, da = (refs[4 * k : 4 * k + 4] for k in range(4))
    gains, keep2, keep0, keep1, send, whole, extra = refs[16:]

    def grads(g, out, at):
        out[at : at + 320, :] = sum(dot_tn(p[g], n[...]) for p, n in zip(dp, n1))
        out[at + 320 : at + 512, :] = sum(dot_tn(v[g, :, :192], a[...]) for v, a in zip(o, da))

    grads(idx[2], whole, 0)
    half = whole.shape[0] // 2
    lead = send.shape[0] - half
    for k, ref in enumerate((keep0, keep1)):
        put_wide(ref, whole[pl.ds(pl.multiple_of(idx[0] * half + k * (half // 2), 8), half // 2), :])
    put_wide(send.at[lead:, :], half_rows(whole, 1 - idx[0], half))
    grads(idx[3], whole, 0)
    rows_in, rows_out = 320 // idx_parts(extra), 192 // idx_parts(extra)
    extra[:rows_in, :] = whole[pl.ds(pl.multiple_of(idx[4] * rows_in, 8), rows_in), :]
    extra[rows_in : rows_in + rows_out, :] = whole[pl.ds(pl.multiple_of(320 + idx[4] * rows_out, 8), rows_out), :]
    n = rows_in + rows_out
    extra[n:, :] = jnp.zeros((extra.shape[0] - n, extra.shape[1]), F32)
    extra[n : n + 2, :] = gains[...]
    half = extra.shape[0] // 2
    put_wide(keep2, half_rows(extra, idx[0], half))
    put_wide(send.at[:lead, :], half_rows(extra, 1 - idx[0], half))


def attn_finish_kernel(parts, idx, a0, a1, b0, b1, slot1, gin, gout):
    d = gin.shape[2]
    for xi in range(2):
        @pl.when(idx[0] == xi)
        def _():
            p0, p1, q0, q1 = (a0, a1, b0, b1) if xi == 0 else (b0, b1, a0, a1)
            gin[0, :128, :] = p0[:, :d]
            gin[0, 128:256, :] = p1[:, :d]
            gin[0, 256:, :] = q0[:64, :d]
            gout[0, :64, :] = q0[64:, :d]
            gout[0, 64:, :] = q1[:, :d]
    mine = idx[5].astype(F32)
    rows_in, rows_out = 320 // parts, 192 // parts
    for k in range(parts):
        r = k * (rows_in + rows_out)
        gin[1, k * rows_in : (k + 1) * rows_in, :] = slot1[r : r + rows_in, :d] * mine
        gout[1, k * rows_out : (k + 1) * rows_out, :] = slot1[r + rows_in : r + rows_in + rows_out, :d] * mine


def idx_parts(extra):
    return 512 // (extra.shape[0] - 16)


BIG = 32 * 1024
OUT = {}


def flush(ref, rows=None):
    out, sem, whole = OUT[id(ref)]
    part = ref if rows is None else ref.at[rows, :]
    to = out if rows is None else out.at[rows, :]
    pltpu.make_async_copy(part, to, sem).start()
    OUT[id(ref)] = (out, sem, True)


def size(a):
    return math.prod(a.shape) * jnp.dtype(a.dtype).itemsize


def call(kernel, outs, ins, scratch=(), smem=0, flops=0, late=(), grouped=()):
    n_in, n_out = len(ins), len(outs)
    big_in = [i for i in range(smem, n_in) if size(ins[i]) >= BIG]
    big_out = [i for i in range(n_out) if size(outs[i]) >= BIG]
    in_specs = [
        pl.BlockSpec(memory_space=pltpu.SMEM if i < smem else pl.ANY if i in big_in else pltpu.VMEM) for i in range(n_in)
    ]
    out_specs = [pl.BlockSpec(memory_space=pl.ANY if i in big_out else pltpu.VMEM) for i in range(n_out)]
    buffers = [pltpu.VMEM(ins[i].shape, ins[i].dtype) for i in big_in]
    buffers += [pltpu.VMEM(outs[i].shape, outs[i].dtype) for i in big_out]
    at, n_sems = {}, 0
    for i in big_in:
        at[i] = n_sems
        n_sems += ins[i].shape[0] if i in grouped else 1
    out_at = n_sems
    sems = pltpu.SemaphoreType.DMA((n_sems + len(big_out),))

    def body(*refs):
        ins_, outs_, rest = list(refs[:n_in]), list(refs[n_in : n_in + n_out]), list(refs[n_in + n_out :])
        own, (bufs, sem) = rest[: len(scratch)], (rest[len(scratch) : -1], rest[-1])
        kept = []
        order = [i for i in big_in if i not in late and i not in grouped]
        order += [i for i in big_in if i in grouped] + [i for i in late if i in big_in]
        for i in order:
            k = big_in.index(i)
            item = Late(ins_[i], bufs[k], sem, at[i], i in grouped)
            item.start()
            kept.append((i, item))
        for i, item in kept:
            early = i not in late and i not in grouped
            ins_[i] = item.wait() if early else item
        OUT.clear()
        for k, i in enumerate(big_out):
            buf = bufs[len(big_in) + k]
            OUT[id(buf)] = (outs_[i], sem.at[out_at + k], False)
            outs_[i] = buf
        kernel(*ins_, *outs_, *own)
        for i in big_out:
            if not OUT[id(outs_[i])][2]:
                flush(outs_[i])
        for i, item in kept:
            assert item.grouped or item.waited
        for i in big_out:
            out, s, _ = OUT[id(outs_[i])]
            pltpu.make_async_copy(outs_[i], out, s).wait()
        OUT.clear()

    moved = sum(size(a) for a in list(ins) + list(outs))
    return pl.pallas_call(
        body,
        out_shape=tuple(outs),
        in_specs=in_specs,
        out_specs=tuple(out_specs),
        scratch_shapes=list(scratch) + buffers + [sems],
        compiler_params=pltpu.CompilerParams(vmem_limit_bytes=VMEM * 1024 * 1024),
        cost_estimate=pl.CostEstimate(flops=flops, bytes_accessed=moved, transcendentals=0),
    )(*ins)


def S(shape, dtype):
    return jax.ShapeDtypeStruct(shape, dtype)


class Links:
    def __init__(self, mesh):
        self.wide, self.narrow = mesh.shape["wide"], mesh.shape["narrow"]
        self.known = (self.wide, self.narrow) == (8, 4)

    def permute(self, v, step):
        pairs = []
        for w in range(self.wide):
            for n in range(self.narrow):
                to = step(w // 2, w % 2, n // 2, n % 2)
                if to is not None:
                    z, x, y, c = to
                    pairs.append((w * self.narrow + n, (z * 2 + x) * self.narrow + y * 2 + c))
        return lax.ppermute(v, ("wide", "narrow"), pairs)

    def core(self, v):
        return self.permute(v, lambda z, x, y, c: (z, x, y, 1 - c))

    def y(self, v):
        return self.permute(v, lambda z, x, y, c: (z, x, 1 - y, c))

    def x(self, v):
        return self.permute(v, lambda z, x, y, c: (z, 1 - x, y, c))

    def inward(self, v):
        return self.permute(v, lambda z, x, y, c: ({0: 1, 3: 2}[z], x, y, c) if z in (0, 3) else None)

    def outward(self, v):
        return self.permute(v, lambda z, x, y, c: ({1: 0, 2: 3}[z], x, y, c) if z in (1, 2) else None)

    def middle(self, v):
        return self.permute(v, lambda z, x, y, c: (3 - z, x, y, c) if z in (1, 2) else None)

    def sum_cores(self, pieces):
        return pieces[0] + self.core(pieces[1]) if self.known else pieces[0]

    def y_start(self, r):
        return self.y(r) if self.known else r

    def sum_chips(self, r, got):
        if not self.known:
            return [lax.psum(r, "narrow")]
        r = r + got
        return [r, self.core(r)]

    def both_cores(self, got):
        return [got, self.core(got)] if self.known else [got]

    def sum_lines(self, chunks, jobs, hooks):
        last = chunks[0]
        if not self.known:
            for job in jobs:
                last = job(last)
            *keeps, send = last
            n = len(chunks) + len(keeps)
            got = self.x(send)
            pairs, at = [], 0
            for keep in keeps:
                pairs.append((keep, at))
                at += keep.shape[0]
            vals, theirs, results = list(chunks) + [None] * len(pairs), [None] * n, {}
            groups = [list(range(k, self.wide, 2)) for k in range(2)]
            for i, (keep, at) in enumerate(pairs):
                vals[len(chunks) + i] = keep + got[at : at + keep.shape[0]]
            vals = [lax.psum(r, "wide", axis_index_groups=groups) for r in vals]
            theirs = [self.x(r) for r in vals]
            for c, hook in hooks.items():
                results[c] = hook(vals, theirs)
            return vals, theirs, results
        z = lax.axis_index("wide") // 2
        inner = (z == 1) | (z == 2)
        n_keep = 3
        n = len(chunks) + n_keep
        order = [*range(4), len(chunks), *range(4, len(chunks)), *range(len(chunks) + 1, n)]
        moved = [self.inward(r) for r in chunks] + [None] * n_keep
        vals, theirs, results = list(chunks) + [None] * n_keep, [None] * n, {}
        last = jobs[0](last)[0]
        for s in range(n + 3):
            for stage in range(4):
                c = s - stage
                if not 0 <= c < n:
                    continue
                c = order[c]
                if stage == 3:
                    theirs[c] = last = after(theirs[c], last)
                    if c in hooks:
                        results[c] = hooks[c](vals, theirs)
                        last = results[c][0]
                    continue
                new = after(moved[c], last)
                vals[c] = jnp.where(inner, vals[c], new) if stage == 2 else vals[c] + new
                last = vals[c]
                if stage == 0:
                    moved[c] = self.middle(vals[c])
                elif stage == 1:
                    moved[c] = self.outward(vals[c])
                else:
                    theirs[c] = self.x(vals[c])
            if s == 0:
                last = jobs[1](last)[0]
            if s == 1:
                *keeps, send = jobs[2](last)
                last = keeps[0]
                got = self.x(send)
            if s == 3:
                got = after(got, last)
                at = 0
                for i, keep in enumerate(keeps):
                    c = len(chunks) + i
                    vals[c] = last = keep + got[at : at + keep.shape[0]]
                    at += keep.shape[0]
                    moved[c] = self.inward(last)
        return vals, theirs, results

    def gather_narrow(self, v):
        if not self.known:
            return lax.all_gather(v, "narrow", axis=0, tiled=True)
        n = lax.axis_index("narrow")
        o = self.core(v)
        two = jnp.where(n % 2 == 0, jnp.concatenate([v, o], 0), jnp.concatenate([o, v], 0))
        o = self.y(two)
        return jnp.where(n // 2 == 0, jnp.concatenate([two, o], 0), jnp.concatenate([o, two], 0))


def tie(*groups):
    return lax.optimization_barrier(groups)


def after(v, *deps):
    return lax.optimization_barrier((v, *deps))[0]


CHUNKS = (240, 240, 240, 240, 240, 240)


def per_device(links, tokens, attn_in, attn_out, gate_weight, up_weight, down_weight, attn_gain, ffn_gain,
               cotangent, seq_ids, positions, valid_mask, group_owner):
    t, d = tokens.shape
    groups = attn_in.shape[0]
    f = gate_weight.shape[1]
    split = links.known
    member = lax.axis_index("narrow")
    xi = lax.axis_index("wide") % 2
    core = member % 2
    idx = jnp.stack([xi, core]).astype(jnp.int32)
    lane = jnp.arange(128, dtype=jnp.int32)
    half = HEAD // 2
    freq = THETA ** (-(lane % half).astype(F32) / half)
    angles = positions.astype(F32)[:, None] * freq[None, :]
    cs = jnp.cos(angles)
    sn = jnp.sin(angles) * jnp.where(lane % HEAD < half, -1.0, 1.0).astype(F32)[None, :]
    seqr, valr = seq_ids.reshape(1, t), valid_mask.reshape(1, t)
    g1, g2 = attn_gain.reshape(1, d), ffn_gain.reshape(1, d)
    win_t = jnp.swapaxes(attn_in, 1, 2)
    wd_t = down_weight.T

    def x_half(w):
        return lax.dynamic_slice_in_dim(w, xi * 256, 256, 1), lax.dynamic_slice_in_dim(w, 512 + xi * 64, 64, 1)

    (ga, gb), (ua, ub), (wa, wb) = x_half(gate_weight), x_half(up_weight), x_half(wd_t)
    wgu = jnp.concatenate([ga, ua, gb, ub], axis=1)
    wdh = jnp.concatenate([wa, wb, jnp.zeros((d, 64), BF16)], axis=1)

    th = t // 2
    sent = th if split else t
    wd = -(-d // 128) * 128
    piece = S((sent, wd), F32)
    sums = [S((th // 2, wd), F32)] * 2 if split else [S((th, wd), F32)]
    n_sums = len(sums)
    saved = [S((th, d), BF16), S((groups, th, 256), BF16), S((groups, th, 128), BF16), S((groups, th, 128), BF16),
             S((groups, th, 256), BF16), S((th, 128), F32), S((th, d), F32), S((th, d), BF16), S((th, 384), BF16)]
    scratch = [pltpu.VMEM((th, d), F32)] * 2 + [pltpu.VMEM((t, 128), BF16)] * 2
    weights = [win_t, attn_out, g1, g2, cs, sn, seqr, valr]
    ffn_w = [gate_weight, up_weight, wd_t]

    def forward(second, x, adds, old):
        part = old is not None
        outs = list(saved) + ([piece] if part else [])
        outs += [S((th, d), F32), S((th, f), BF16), S((th, d), F32)] if second else [S((th, d), BF16)] + [S((th, f), F32)] * 2
        ins = [idx, x, *adds] + weights + ffn_w
        at = 2 + len(adds)
        ins += [old[2], old[3], old[7]] if part else []
        ins += [cotangent] if second else []
        res = call(functools.partial(fwd_kernel, second, split, int(part), groups), outs + sums, ins, scratch, smem=1,
                   flops=4 * 10**9, grouped=[at, at + 1],
                   late=[at + 4, at + 5, at + 8, at + 9, at + 10] + ([at + 13] if part else [])
                   + ([len(ins) - 1] if second else []))
        return list(res[:-n_sums]), list(res[-n_sums:])

    cot_rows = lax.dynamic_slice_in_dim(cotangent, core * sent, sent, 0) if split else cotangent
    cot_s = jnp.pad(cot_rows.astype(F32), ((0, 0), (0, wd - d)))

    tokens_t = tokens.T
    cot_x = links.x(cot_s)
    a1, s1a = forward(False, tokens_t, [], None)
    *a1, tok_a, gate1a, up1a = a1
    r1a = links.sum_cores(s1a)
    y1a = links.y_start(r1a)
    b1, s1b = forward(False, after(tokens_t, r1a), [], a1)
    *b1, n2as, tok_b, gate1b, up1b = b1
    s1b, n2as, y1a, cot_x = tie(s1b, n2as, y1a, cot_x)
    sum1a = links.sum_chips(r1a, y1a)
    r1b = links.sum_cores(s1b)
    y1b = links.y_start(r1b)
    n2a_x = links.x(n2as)
    cot_p = links.both_cores(cot_x)
    a2, s2a = forward(True, after(a1[6], r1b), sum1a, None)
    *a2, x1a, duh2a, part2a = a2
    s2a, y1b, n2a_x = tie(s2a, y1b, n2a_x)
    sum1b = links.sum_chips(r1b, y1b)
    n2a_p = links.both_cores(n2a_x)
    r2a = links.sum_cores(s2a)
    y2a = links.y_start(r2a)
    b2, s2b = forward(True, after(b1[6], r2a, n2a_p, cot_p), sum1b, a2)
    *b2, n2bs, x1b, duh2b, part2b = b2
    h2a, h2b = a2[6], b2[6]
    s2b, n2bs, y2a = tie(s2b, n2bs, y2a)
    sum2a = links.sum_chips(r2a, y2a)
    r2b = links.sum_cores(s2b)
    y2b = links.y_start(r2b)
    n2b_x = links.x(n2bs)
    grad_outs = [S((d, f), F32), S((d, 384), F32)]
    gscratch = [pltpu.VMEM((t, d), BF16), pltpu.VMEM((t, d), BF16), pltpu.VMEM((t, f), BF16), pltpu.VMEM((t, 384), BF16)]

    tail = [cs, sn, seqr, valr]

    def backward_a(sums, dz, r):
        outs = [S((th, d), F32), S((th, d), BF16), S((groups, th, 128), BF16), S((groups, th, 128), F32),
                S((groups, 2, th, 128), F32), S((1, d), F32)]
        return call(
            functools.partial(bwd_a_kernel, split, groups), outs,
            [idx, *sums, dz, r[6], *r[1:6], attn_out, g2] + tail, smem=1, flops=4 * 10**9,
            grouped=[n_sums + 3, n_sums + 4, n_sums + 5, n_sums + 6, n_sums + 8], late=[n_sums + 7, n_sums + 10, n_sums + 11],
        )

    def backward_b(last, sums, dz, first, ra, rb, xa, xb):
        xt = BF16 if last else F32
        outs = [S((th, d), BF16), S((groups, th, 320), BF16), S((groups, th, 320), BF16), S((th, d), xt), S((th, d), xt),
                S((1, d), F32), S((1, d), F32)] + ([] if last else [piece])
        dha, _, dqxa, dqya, dkva, _ = first
        return call(
            functools.partial(bwd_b_kernel, last, split, groups), outs,
            [idx, *sums, dz, rb[6], *rb[1:6], xa, xb, ra[2], ra[3], dha, dqxa, dqya, dkva, win_t, attn_out, g1, g2] + tail,
            [pltpu.VMEM((th, d), F32)] * 3 + [pltpu.VMEM((2, t, 128), F32), pltpu.VMEM((t, 128), BF16),
             pltpu.VMEM((t, 128), BF16), pltpu.VMEM((th, 128), F32)],
            smem=1, flops=6 * 10**9,
            grouped=[n_sums + k for k in (3, 4, 5, 6, 10, 11, 13, 14, 15, 16, 17)],
            late=[n_sums + k for k in (7, 20, 21, 8, 9, 12)],
        )

    acc = call(own_grads_kernel, grad_outs, [after(a2[7], r2b, sum2a), b2[7], duh2a, duh2b, a2[8], b2[8], cotangent],
               flops=2 * 10**9)
    first2 = backward_a(after(sum2a, acc), cotangent[:th], a2)
    first2, y2b = tie(first2, y2b)
    sum2b = links.sum_chips(r2b, y2b)
    da2b, dp2a, dp2b, dz1a, dz1b, dg1b, dg2b1, dfs = backward_b(
        False, sum2b, cotangent[th:], first2, a2, b2, x1a, x1b)
    dfs, dz1a, dz1b, n2b_x = tie(dfs, dz1a, dz1b, n2b_x)
    df_x = links.x(dfs)
    n2b_p = links.both_cores(n2b_x)
    da2a, dg2b0 = first2[1], first2[5]
    res = call(
        functools.partial(ffn_back_kernel, split), [S((th, f), BF16)] * 2 + [S((th, d), BF16)] * 2 + sums * 2,
        [idx, dz1a, dz1b, gate1a, gate1b, up1a, up1b] + ffn_w, [pltpu.VMEM((th, d), F32)], smem=1, flops=2 * 10**9,
        late=[1, 9, 3, 5, 7, 8, 2, 4, 6],
    )
    duh1, df1, s3 = res[:2], res[2:4], res[4:]
    r3a, r3b = links.sum_cores(s3[:n_sums]), links.sum_cores(s3[n_sums:])
    y3a, y3b = links.y_start(r3a), links.y_start(r3b)
    acc = call(
        functools.partial(both_grads_kernel, len(n2b_p)), grad_outs,
        [*n2b_p, *cot_p, wgu, wdh, after(a1[7], r3a, r3b), b1[7], *duh1, a1[8], b1[8], *df1, *acc], gscratch,
        flops=6 * 10**9, late=[12 + 2 * len(n2b_p) - 2 + 0, 12 + 2 * len(n2b_p) - 1, *range(2 * len(n2b_p) + 2)],
    )
    acc, df_x = tie(acc, df_x)
    df_p = links.both_cores(df_x)
    count = len(df_p)
    chunks = call(
        functools.partial(last_grads_kernel, count, len(CHUNKS)), [S((n, f), F32) for n in CHUNKS],
        [*n2a_p, *df_p, wgu, wdh, *acc], gscratch + [pltpu.VMEM((d, f), F32), pltpu.VMEM((d, 384), F32)],
        flops=4 * 10**9, late=[2 * count + 2, 2 * count + 3],
    )
    quarter = 512 // links.narrow
    group_owner = after(group_owner, acc)
    order = jnp.arange(groups, dtype=jnp.int32)
    sharing = (group_owner[:, None] == group_owner[None, :]) & (order[None, :] < order[:, None])
    rank = jnp.sum(sharing.astype(jnp.int32), axis=1)
    first = jnp.sum(jnp.where((group_owner == member) & (rank == 0), order, 0))
    extra = jnp.sum(jnp.where(rank == 1, order, 0))
    extra_owner = jnp.sum(jnp.where(rank == 1, group_owner, 0))
    idx = jnp.stack([xi, core, first, extra, member, (extra_owner == member).astype(jnp.int32)]).astype(jnp.int32)
    chunks, y3a = tie(chunks, y3a)
    sum3a = links.sum_chips(r3a, y3a)
    lead = quarter // 2 + 8
    made = {}

    def job_a(dep):
        made["a"] = backward_a(after(sum3a, dep), dz1a, a1)
        return made["a"]

    def job_b(dep):
        first, got = tie(made["a"], y3b)
        sums = links.sum_chips(r3b, got)
        made["b"] = backward_b(True, after(sums, dep), dz1b, first, a1, b1, tok_a, tok_b)
        return made["b"]

    def job_grads(dep):
        first, (da1b, dp1a, dp1b, _, _, dg1a, dg2a1) = made["a"], made["b"]
        gains = jnp.concatenate([dg1a + dg1b, first[5] + dg2a1 + dg2b0 + dg2b1], axis=0)
        return call(
            attn_grad_kernel, [S((n, wd), F32) for n in (lead, 128, 128, lead + 256)],
            [idx, after(a1[0], dep), b1[0], a2[0], b2[0], dp1a, dp1b, dp2a, dp2b, a1[4], b1[4], a2[4], b2[4], first[1],
             da1b, da2a, da2b, gains],
            [pltpu.VMEM((512, d), F32), pltpu.VMEM((quarter + 16, d), F32)], smem=1, flops=2 * 10**9,
        )

    part2 = lax.psum(after((part2a, part2b), y3b), "narrow")

    def finish_out(vals, theirs):
        total = after(part2, vals[4])
        return [jnp.concatenate([h + p for h, p in zip((h2a, h2b), total)], axis=0).astype(BF16)]

    def unpack(vals, theirs):
        return call(functools.partial(unpack_kernel, 4, False), [S((d, f), F32)] * 2,
                    [idx, *vals[:4], *theirs[:4]], smem=1, late=[1, 5, 2, 6, 3, 7, 4, 8])

    def unpack_down(vals, theirs):
        return call(functools.partial(unpack_kernel, 2, True), [S((d, f), F32)],
                    [idx, *vals[4:6], *theirs[4:6]], smem=1, late=[1, 3, 2, 4])

    def collect(vals, theirs):
        r, o = vals[6], theirs[6]
        second = jnp.where(xi == 0, jnp.concatenate([r, o], 0), jnp.concatenate([o, r], 0))
        return second, links.gather_narrow(second[:quarter])

    done, theirs, results = links.sum_lines(
        chunks, [job_a, job_b, job_grads], {4: finish_out, 3: unpack, 5: unpack_down, 6: collect})
    layer_out = results[4][0]
    dx = jnp.concatenate(made["b"][3:5], axis=0)
    ggate, gup = results[3]
    gdown, = results[5]
    second, slot1 = results[6]
    small = second[quarter : quarter + 2, :d]
    gin, gout = call(
        functools.partial(attn_finish_kernel, links.narrow), [S((SLOTS, 320, d), F32), S((SLOTS, 192, d), F32)],
        [idx, *done[7:], *theirs[7:], slot1], smem=1,
    )
    gin = jnp.swapaxes(gin, 1, 2)
    return layer_out, dx, gin, gout, ggate, gup, gdown.T, small[0], small[1]


def _pad(outs, split):
    return list(outs) if split else list(outs) + [None]


def solution(mesh):
    in_specs = (P("wide", None), P(), P(), P(None, "narrow"), P(None, "narrow"), P("narrow", None), P(), P(),
                P("wide", None), P("wide"), P("wide"), P("wide"), P())
    out_specs = (P("wide", None), P("wide", None), P("narrow", None, None), P("narrow", None, None),
                 P(None, "narrow"), P(None, "narrow"), P("narrow", None), P(), P())
    return jax.shard_map(functools.partial(per_device, Links(mesh)), mesh=mesh, in_specs=in_specs,
                         out_specs=out_specs, check_vma=False)
```

time: 654 us -> 479 us (0.73)
  waiting for transfers between devices: 227 us -> 106 us
  blocking collectives: 66.6 us -> 0 us
  Pallas kernels: 151 us -> 194 us
  other arithmetic: 79.3 us -> 41.1 us
  starting transfers between devices: 58.7 us -> 94.2 us
  local copies, waits for them, and re-layouts: 47.7 us -> 19.9 us
    ppermute x34 -> x65, waiting for transfers between devices: 208 us -> 94.2 us  [permute(): return lax.ppermute(v, ('wide', 'narrow'), pairs)]
    psum x1 -> x0, blocking collectives: 66.6 us -> none  [per_device(): small = lax.psum(small, 'wide')]
    pallas_call x8 -> x16, Pallas kernels: 151 us -> 194 us  [call(): pl.pallas_call(body, out_shape=tuple(outs), in_specs=in_specs, out_specs=...]
    ppermute x34 -> x65, starting transfers between devices: 58.7 us -> 94.2 us  [permute(): return lax.ppermute(v, ('wide', 'narrow'), pairs)]
    select_n x13 -> x12, other arithmetic: 35 us -> 14.1 us  [the longest x9 8.32 us: sum_lines(): vals[c] = jnp.where(inner, vals[c], new) if stage == 2 else vals[c] + new]
    add x23 -> x34, other arithmetic: 37.9 us -> 17.8 us  [the longest x18 9.37 us: sum_lines(): vals[c] = jnp.where(inner, vals[c], new) if stage == 2 else vals[c] + new]
    unnamed x42 -> x121, local copies, waits for them, and re-layouts: 23.3 us -> 10.4 us
    dynamic_slice x11 -> x4, local copies, waits for them, and re-layouts: 13 us -> 4.83 us  [the longest x2 2.5 us: x_half(): lax.dynamic_slice_in_dim(w, xi * 256, 256, 1)]
  transfers between devices with their start and end apart: 35 -> 66, of which waited for: 17 -> 18; matrix products, arithmetic and copies ran while one was open for 13% -> 11% of each run, Pallas kernels for 8% -> 37%
where the time goes in v2:
time: 479 us; the launch traced here: 471 us
  Pallas kernels  194 us (41%)
  waiting for transfers between devices  106 us (22%)
  starting transfers between devices  94.2 us (20%)
  other arithmetic  41.1 us (9%)
  local copies, waits for them, and re-layouts  19.9 us (4%)
  between operations  16.6 us (3%)
    pallas_call x16, Pallas kernels, call(): pl.pallas_call(body, out_shape=tuple(outs), in_specs=in_specs, out_specs=...  194 us
    ppermute x65, waiting for transfers between devices, permute(): return lax.ppermute(v, ('wide', 'narrow'), pairs)  94.2 us
    ppermute x65, starting transfers between devices, permute(): return lax.ppermute(v, ('wide', 'narrow'), pairs)  94.2 us
    psum x1, waiting for transfers between devices, per_device(): part2 = lax.psum(after((part2a, part2b), y3b), 'narrow')  11.4 us
    unnamed x121, local copies, waits for them, and re-layouts  10.4 us
  transfers between devices with their start and end apart: 66, of which 18 were waited for; matrix products, arithmetic and copies ran while one was open for 11% of the time, Pallas kernels for 37%

profile of v2, /device:TPU:0, one launch (start us, length us, event | category | flops | bytes accessed | tf_op | source)
XLA Modules:
  0.0 471.1 jit_solution(13350112831157496086)
XLA Ops:
  10.4 14.8 %shard_map.196 = (bf16[256,960]{1,0:T(8,128)(2,1)}, bf16[5,256,256]{2,1,0:T(8,128)(2,1)}, bf16[5,256,128]{2,1,0:T(8,128)(2,1)}, bf16[5,256,128]{2,1,0:T(8,128)(2...) custom-call(s32[2]{0:T(128)} %pad_add_fusion.refs_0_, ...), custom_call_target="tpu_custom_call" | custom-call | flops 4000000000 | bytes 17231368 | tf_op jit(solution)/shard_map/pallas_call | solution.py:702
  27.5 2.6 collective-permute-start.2
  31.8 17.9 %shard_map.197 = (bf16[256,960]{1,0:T(8,128)(2,1)}, bf16[5,256,256]{2,1,0:T(8,128)(2,1)}, bf16[5,256,128]{2,1,0:T(8,128)(2,1)}, bf16[5,256,128]{2,1,0:T(8,128)(2...) custom-call(s32[2]{0:T(128)} %pad_add_fusion.refs_0_, ...), custom_call_target="tpu_custom_call" | custom-call | flops 4000000000 | bytes 19426824 | tf_op jit(solution)/shard_map/pallas_call | solution.py:702
  49.7 4.2 collective-permute-done.2.refs_2_
  59.8 16.8 %shard_map.198 = (bf16[256,960]{1,0:T(8,128)(2,1)}, bf16[5,256,256]{2,1,0:T(8,128)(2,1)}, bf16[5,256,128]{2,1,0:T(8,128)(2,1)}, bf16[5,256,128]{2,1,0:T(8,128)(2...) custom-call(s32[2]{0:T(128)} %pad_add_fusion.refs_0_, ...), custom_call_target="tpu_custom_call" | custom-call | flops 4000000000 | bytes 19754504 | tf_op jit(solution)/shard_map/pallas_call | solution.py:702
  76.6 3.1 collective-permute-done.6.refs_0_
  80.4 3.3 collective-permute-done.7
  87.5 20.2 %shard_map.199 = (bf16[256,960]{1,0:T(8,128)(2,1)}, bf16[5,256,256]{2,1,0:T(8,128)(2,1)}, bf16[5,256,128]{2,1,0:T(8,128)(2,1)}, bf16[5,256,128]{2,1,0:T(8,128)(2...) custom-call(s32[2]{0:T(128)} %pad_add_fusion.refs_0_, ...), custom_call_target="tpu_custom_call" | custom-call | flops 4000000000 | bytes 21949960 | tf_op jit(solution)/shard_map/pallas_call | solution.py:702
  111.5 4.7 %shard_map.200 = (f32[960,640]{1,0:T(8,128)}, f32[960,384]{1,0:T(8,128)}) custom-call(bf16[256,960]{1,0:T(8,128)(2,1)} %get-tuple-element.249.refs_17_.refs_0_, bf16[256,960]{1,0:T(8,128)(2,1)} %get-tuple-element.250.refs_1_, bf16[256,640]{1,0:T(8,128)(2,1)} %get-tuple-element.251.refs_2_, bf16[256,640]{1,0:T(8,128)(2,1)} %get-tuple-element.252.refs_3_, ...), custom_call_target="tpu_custom_call" | custom-call | flops 2000000000 | bytes 6946816 | tf_op jit(solution)/shard_map/pallas_call | solution.py:702
  116.2 13.1 %shard_map.201 = (f32[256,960]{1,0:T(8,128)}, bf16[256,960]{1,0:T(8,128)(2,1)}, bf16[5,256,128]{2,1,0:T(8,128)(2,1)}, f32[5,256,128]{2,1,0:T(8,128)}, f32[5,2,256,128]{3,2,1,0:T(8,128)}, /*index=5*/f32[1,960]{1,0:T(1,128)}) custom-call(s32[2]{0:T(128)} %pad_add_fusion.refs_0_, f32[128,1024]{1,0:T(8,128)} %copy-done.31, f32[128,1024]{1,0:T(8,128)} %copy-done.57, ...), custom_call_target="tpu_custom_call" | custom-call | flops 4000000000 | bytes 10767880 | tf_op jit(solution)/shard_map/pallas_call | solution.py:702
  129.6 1.9 collective-permute-start.16
  132.2 23.1 %shard_map.202 = (bf16[256,960]{1,0:T(8,128)(2,1)}, bf16[5,256,320]{2,1,0:T(8,128)(2,1)}, bf16[5,256,320]{2,1,0:T(8,128)(2,1)}, f32[256,960]{1,0:T(8,128)}, f32[...) custom-call(s32[2]{0:T(128)} %pad_add_fusion.refs_0_, f32[128,1024]{1,0:T(8,128)} %copy-done.24, ...), custom_call_target="tpu_custom_call" | custom-call | flops 6000000000 | bytes 21122056 | tf_op jit(solution)/shard_map/pallas_call | solution.py:702
  158.0 7.8 %shard_map.203 = (bf16[256,640]{1,0:T(8,128)(2,1)}, bf16[256,640]{1,0:T(8,128)(2,1)}, bf16[256,960]{1,0:T(8,128)(2,1)}, bf16[256,960]{1,0:T(8,128)(2,1)}, f32[12...) custom-call(s32[2]{0:T(128)} %pad_add_fusion.refs_0_, ...), custom_call_target="tpu_custom_call" | custom-call | flops 2000000000 | bytes 12009480 | tf_op jit(solution)/shard_map/pallas_call | solution.py:702
  174.1 9.0 %shard_map.204 = (f32[960,640]{1,0:T(8,128)}, f32[960,384]{1,0:T(8,128)}) custom-call(f32[256,1024]{1,0:T(8,128)} %copy-done.47, f32[256,1024]{1,0:T(8,128)} %copy-done.50, f32[256,1024]{1,0:T(8,128)} %copy-done.43, f32[256,1024]{1,0:T(8,128)} %copy-done.46, bf16[960,640]{1,0:T(8,128)(2,1)} %pad_maximum_fusion.refs_4_, ...), custom_call_target="tpu_custom_call" | custom-call | flops 6000000000 | bytes 17039360 | tf_op jit(solution)/shard_map/pallas_call | solution.py:702
  183.1 10.0 %collective-permute-done.21.refs_2_ = f32[256,1024]{1,0:T(8,128)S(1)} collective-permute-done((f32[256,1024]{1,0:T(8,128)S(1)}, f32[256,1024]{1,0:T(8,128)S(1)}, u32[]{:S(2)}, u32[]{:S(2)}) %collective-permute-start.21) | collective-permute-done | bytes 1048608 | tf_op jit(solution)/shard_map/ppermute | solution.py:730
  196.8 7.9 %shard_map.205 = (f32[240,640]{1,0:T(8,128)}, f32[240,640]{1,0:T(8,128)}, f32[240,640]{1,0:T(8,128)}, f32[240,640]{1,0:T(8,128)}, f32[240,640]{1,0:T(8,128)}, /*index=5*/f32[240,640]{1,0:T(8,128)}) custom-call(f32[256,1024]{1,0:T(8,128)} %copy-done.44, f32[256,1024]{1,0:T(8,128)} %copy-done.45, f32[256,1024]{1,0:T(8,128)} %copy-done.51, ...), custom_call_target="tpu_custom_call" | custom-call | flops 4000000000 | bytes 13778944 | tf_op jit(solution)/shard_map/pallas_call | solution.py:702
  204.6 2.8 collective-permute-done.23
  210.9 2.0 stack.37.refs_0_
  212.8 3.7 collective-permute-start.28
  217.4 13.3 %shard_map.206 = (f32[256,960]{1,0:T(8,128)}, bf16[256,960]{1,0:T(8,128)(2,1)}, bf16[5,256,128]{2,1,0:T(8,128)(2,1)}, f32[5,256,128]{2,1,0:T(8,128)}, f32[5,2,256,128]{3,2,1,0:T(8,128)}, /*index=5*/f32[1,960]{1,0:T(1,128)}) custom-call(s32[6]{0:T(128)} %stack.37.refs_0_, f32[128,1024]{1,0:T(8,128)} %copy-done.28, f32[128,1024]{1,0:T(8,128)} %copy-done.55, ...), custom_call_target="tpu_custom_call" | custom-call | flops 4000000000 | bytes 11259416 | tf_op jit(solution)/shard_map/pallas_call | solution.py:702
  235.5 22.6 %shard_map.207 = (bf16[256,960]{1,0:T(8,128)(2,1)}, bf16[5,256,320]{2,1,0:T(8,128)(2,1)}, bf16[5,256,320]{2,1,0:T(8,128)(2,1)}, bf16[256,960]{1,0:T(8,128)(2,1)}...) custom-call(s32[6]{0:T(128)} %stack.37.refs_0_, f32[128,1024]{1,0:T(8,128)} %copy-done.26, ...), custom_call_target="tpu_custom_call" | custom-call | flops 6000000000 | bytes 18598936 | tf_op jit(solution)/shard_map/pallas_call | solution.py:702
  263.0 9.0 %shard_map.208 = (f32[72,1024]{1,0:T(8,128)}, f32[128,1024]{1,0:T(8,128)}, f32[128,1024]{1,0:T(8,128)}, f32[328,1024]{1,0:T(8,128)}) custom-call(s32[6]{0:T(128)} %stack.37.refs_0_, bf16[256,960]{1,0:T(8,128)(2,1)} %get-tuple-element.354.refs_1_, bf16[256,960]{1,0:T(8,128)(2,1)} %get-tuple-element.355.refs_2_, bf16[256,960]{1,0:T(8,128)(2,1)} %get-tuple-element.356.refs_3_, ...), custom_call_target="tpu_custom_call" | custom-call | flops 2000000000 | bytes 12525080 | tf_op jit(solution)/shard_map/pallas_call | solution.py:702
  273.6 5.7 %collective-permute-start.34 = (f32[240,640]{1,0:T(8,128)S(1)}, f32[240,640]{1,0:T(8,128)S(1)}, u32[]{:S(2)}, u32[]{:S(2)}) collective-permute-start(f32[240,640]{1,0:T(8,128)S(1)} %copy-done.17), channel_id=1, source_target_pairs={{0,8},{1,9},{2,10},{3,11},{4,12},{5,13},{6,14},{7,15},{24,16},{25,... | collective-permute-start | bytes 1843208 | tf_op jit(solution)/shard_map/ppermute | solution.py:730
  284.5 7.5 %collective-permute-done.34 = f32[240,640]{1,0:T(8,128)S(1)} collective-permute-done((f32[240,640]{1,0:T(8,128)S(1)}, f32[240,640]{1,0:T(8,128)S(1)}, u32[]{:S(2)}, u32[]{:S(2)}) %collective-permute-start.34) | collective-permute-done | bytes 614432 | tf_op jit(solution)/shard_map/ppermute | solution.py:730
  292.0 4.4 collective-permute-start.24
  299.6 17.5 %collective-permute-done.40.refs_5_ = f32[240,640]{1,0:T(8,128)S(1)} collective-permute-done((f32[240,640]{1,0:T(8,128)S(1)}, f32[240,640]{1,0:T(8,128)S(1)}, u32[]{:S(2)}, u32[]{:S(2)}) %collective-permute-start.40) | collective-permute-done | bytes 614432 | tf_op jit(solution)/shard_map/ppermute | solution.py:730
  319.7 5.1 %collective-permute-start.41 = (f32[72,1024]{1,0:T(8,128)S(1)}, f32[72,1024]{1,0:T(8,128)S(1)}, u32[]{:S(2)}, u32[]{:S(2)}) collective-permute-start(f32[72,1024]{1,0:T(8,128)S(1)} %slice_add_fusion.2), channel_id=1, source_target_pairs={{0,8},{1,9},{2,10},{3,11},{4,12},{5,13},{6,14},{7,15},{24,16},{25,... | collective-permute-start | bytes 884744 | tf_op jit(solution)/shard_map/ppermute | solution.py:730
  324.8 2.2 slice_add_fusion
  327.0 2.7 collective-permute-done.41
  331.1 4.9 %collective-permute-start.43 = (f32[240,640]{1,0:T(8,128)S(1)}, f32[240,640]{1,0:T(8,128)S(1)}, u32[]{:S(2)}, u32[]{:S(2)}) collective-permute-start(f32[240,640]{1,0:T(8,128)S(1)} %copy-done.15), channel_id=1, source_target_pairs={{0,8},{1,9},{2,10},{3,11},{4,12},{5,13},{6,14},{7,15},{24,16},{25,... | collective-permute-start | bytes 1843208 | tf_op jit(solution)/shard_map/ppermute | solution.py:730
  338.2 6.9 %collective-permute-done.45 = f32[240,640]{1,0:T(8,128)S(1)} collective-permute-done((f32[240,640]{1,0:T(8,128)S(1)}, f32[240,640]{1,0:T(8,128)S(1)}, u32[]{:S(2)}, u32[]{:S(2)}) %collective-permute-start.45) | collective-permute-done | bytes 614432 | tf_op jit(solution)/shard_map/ppermute | solution.py:730
  345.8 7.1 %collective-permute-done.44.refs_7_ = f32[240,640]{1,0:T(8,128)S(1)} collective-permute-done((f32[240,640]{1,0:T(8,128)S(1)}, f32[240,640]{1,0:T(8,128)S(1)}, u32[]{:S(2)}, u32[]{:S(2)}) %collective-permute-start.44) | collective-permute-done | bytes 614432 | tf_op jit(solution)/shard_map/ppermute | solution.py:730
  357.2 11.7 %collective-permute-start.49 = (f32[128,1024]{1,0:T(8,128)S(1)}, f32[128,1024]{1,0:T(8,128)}, u32[]{:S(2)}, u32[]{:S(2)}) collective-permute-start(f32[128,1024]{1,0:T(8,128)S(1)} %get-tuple-element.440), channel_id=1, source_target_pairs={{0,8},{1,9},{2,10},{3,11},{4,12},{5,13},{6,14},{7,15},{24,16},{25,... | collective-permute-start | bytes 1572872 | tf_op jit(solution)/shard_map/ppermute | solution.py:730
  368.9 10.9 %collective-permute-done.51 = f32[72,1024]{1,0:T(8,128)S(1)} collective-permute-done((f32[72,1024]{1,0:T(8,128)S(1)}, f32[72,1024]{1,0:T(8,128)S(1)}, u32[]{:S(2)}, u32[]{:S(2)}) %collective-permute-start.51) | collective-permute-done | bytes 294944 | tf_op jit(solution)/shard_map/ppermute | solution.py:730
  379.8 2.2 collective-permute-start.53
  383.5 4.8 %shard_map.209 = (f32[960,640]{1,0:T(8,128)}, f32[960,640]{1,0:T(8,128)}) custom-call(s32[6]{0:T(128)} %stack.37.refs_0_, f32[240,640]{1,0:T(8,128)} %copy-done.1, f32[240,640]{1,0:T(8,128)} %copy-done.2, f32[240,640]{1,0:T(8,128)} %copy-done.4, f32[240,640]{1,0:T(8,128)} %copy-done.5, f32[240,640]{1,0:T(8,128)} %copy-done.21, f32[240,640]{1,0:T(8,128)} %copy-done.22, ...), custom_call_target="tpu_custom_call" | custom-call | bytes 9830424 | tf_op jit(solution)/shard_map/pallas_call | solution.py:702
  400.9 11.4 %all-reduce.4.cloned.1.call-done = (f32[256,960]{1,0:T(8,128)}, f32[256,960]{1,0:T(8,128)}) async-done(((f32[256,960]{1,0:T(8,128)}, f32[256,960]{1,0:T(8,128)}), (f32[256,960]{1,0:T(8,128)}, f32[256,960]{1,0:T(8,128)})) %all-reduce.4.cloned.1.call-update) | async-done | bytes 1966096 | tf_op jit(solution)/shard_map/psum | solution.py:1033
  412.3 1.8 add_convert_fusion.1
  414.7 1.9 add.216
  420.7 1.9 add.217
  426.0 7.6 %collective-permute-done.55 = f32[128,1024]{1,0:T(8,128)} collective-permute-done((f32[128,1024]{1,0:T(8,128)}, f32[128,1024]{1,0:T(8,128)}, u32[]{:S(2)}, u32[]{:S(2)}) %collective-permute-start.55) | collective-permute-done | bytes 524320 | tf_op jit(solution)/shard_map/ppermute | solution.py:730
  433.6 1.9 broadcast_select_fusion.7.refs_1_
  437.0 3.5 shard_map.210
  440.6 3.1 collective-permute-done.57
  443.6 1.9 broadcast_select_fusion.6.refs_2_
  451.1 3.3 maximum_select_fusion.refs_5_
  454.4 4.1 collective-permute-done.62.refs_4_
  458.6 5.2 %shard_map.211 = (f32[2,320,960]{2,1,0:T(8,128)}, f32[2,192,960]{2,1,0:T(8,128)}) custom-call(s32[6]{0:T(128)} %stack.37.refs_0_, f32[128,1024]{1,0:T(8,128)} %broadcast_select_fusion.7.refs_1_, f32[128,1024]{1,0:T(8,128)} %broadcast_select_fusion.6.refs_2_, f32[128,1024]{1,0:T(8,128)} %collective-permute-done.61.refs_3_, ...), custom_call_target="tpu_custom_call" | custom-call | bytes 8126488 | tf_op jit(solution)/shard_map/pallas_call | solution.py:702
  (292 shorter events, 99.5 us)
Async XLA Ops:
  7.2 405.1 %all-reduce.4.cloned.1.call-start = ((), (), s32[]{:S(2)}) async-start(), calls=%async_computation | async-start | bytes 4194304 | tf_op jit(solution)/shard_map/psum | solution.py:1033
  27.5 26.4 %collective-permute-start.2 = (f32[256,1024]{1,0:T(8,128)S(1)}, f32[256,1024]{1,0:T(8,128)S(1)}, u32[]{:S(2)}, u32[]{:S(2)}) collective-permute-start(f32[256,1024]{1,0:T(8,128)S(1)} %pad_convert_fusion), channel_id=1, source_target_pairs={{0,4},{1,5},{2,6},{3,7},{4,0},{5,1},{6,2},{7,3},{8,12},{9,13},{10,... | collective-permute-start | bytes 3145736 | tf_op jit(solution)/shard_map/ppermute | solution.py:730
  30.2 19.5 %collective-permute-start.1 = (f32[128,1024]{1,0:T(8,128)S(1)}, f32[128,1024]{1,0:T(8,128)S(1)}, u32[]{:S(2)}, u32[]{:S(2)}) collective-permute-start(f32[128,1024]{1,0:T(8,128)S(1)} %add.175), channel_id=1, source_target_pairs={{0,2},{1,3},{2,0},{3,1},{4,6},{5,7},{6,4},{7,5},{8,10},{9,11},{10,... | collective-permute-start | bytes 1572872 | tf_op jit(solution)/shard_map/ppermute | solution.py:730
  53.9 25.8 %collective-permute-start.6 = (f32[256,1024]{1,0:T(8,128)}, f32[256,1024]{1,0:T(8,128)S(1)}, u32[]{:S(2)}, u32[]{:S(2)}) collective-permute-start(f32[256,1024]{1,0:T(8,128)} %get-tuple-element.232), channel_id=1, source_target_pairs={{0,4},{1,5},{2,6},{3,7},{4,0},{5,1},{6,2},{7,3},{8,12},{9,13},{10,... | collective-permute-start | bytes 3145736 | tf_op jit(solution)/shard_map/ppermute | solution.py:730
  57.2 19.4 %collective-permute-start.5 = (f32[128,1024]{1,0:T(8,128)S(1)}, f32[128,1024]{1,0:T(8,128)S(1)}, u32[]{:S(2)}, u32[]{:S(2)}) collective-permute-start(f32[128,1024]{1,0:T(8,128)S(1)} %add.177), channel_id=1, source_target_pairs={{0,2},{1,3},{2,0},{3,1},{4,6},{5,7},{6,4},{7,5},{8,10},{9,11},{10,... | collective-permute-start | bytes 1572872 | tf_op jit(solution)/shard_map/ppermute | solution.py:730
  58.9 27.7 %collective-permute-start.9 = (f32[256,1024]{1,0:T(8,128)S(1)}, f32[256,1024]{1,0:T(8,128)S(1)}, u32[]{:S(2)}, u32[]{:S(2)}) collective-permute-start(f32[256,1024]{1,0:T(8,128)S(1)} %collective-permute-done.2.refs_2_), channel_id=1, source_target_pairs={{0,1},{1,0},{2,3},{3,2},{4,5},{5,4},{6,7},{7,6},{8,9},{9,8},{10,11... | collective-permute-start | bytes 3145736 | tf_op jit(solution)/shard_map/ppermute | solution.py:730
  84.9 22.9 %collective-permute-start.11 = (f32[128,1024]{1,0:T(8,128)S(1)}, f32[128,1024]{1,0:T(8,128)S(1)}, u32[]{:S(2)}, u32[]{:S(2)}) collective-permute-start(f32[128,1024]{1,0:T(8,128)S(1)} %add.179), channel_id=1, source_target_pairs={{0,2},{1,3},{2,0},{3,1},{4,6},{5,7},{6,4},{7,5},{8,10},{9,11},{10,... | collective-permute-start | bytes 1572872 | tf_op jit(solution)/shard_map/ppermute | solution.py:730
  111.1 18.3 %collective-permute-start.14 = (f32[128,1024]{1,0:T(8,128)S(1)}, f32[128,1024]{1,0:T(8,128)S(1)}, u32[]{:S(2)}, u32[]{:S(2)}) collective-permute-start(f32[128,1024]{1,0:T(8,128)S(1)} %add.181), channel_id=1, source_target_pairs={{0,2},{1,3},{2,0},{3,1},{4,6},{5,7},{6,4},{7,5},{8,10},{9,11},{10,... | collective-permute-start | bytes 1572872 | tf_op jit(solution)/shard_map/ppermute | solution.py:730
  129.6 25.7 %collective-permute-start.16 = (f32[256,1024]{1,0:T(8,128)S(1)}, f32[256,1024]{1,0:T(8,128)S(1)}, u32[]{:S(2)}, u32[]{:S(2)}) collective-permute-start(f32[256,1024]{1,0:T(8,128)S(1)} %copy-done.48), channel_id=1, source_target_pairs={{0,4},{1,5},{2,6},{3,7},{4,0},{5,1},{6,2},{7,3},{8,12},{9,13},{10,... | collective-permute-start | bytes 3145736 | tf_op jit(solution)/shard_map/ppermute | solution.py:730
  155.3 17.8 %collective-permute-start.19 = (f32[256,1024]{1,0:T(8,128)S(1)}, f32[256,1024]{1,0:T(8,128)S(1)}, u32[]{:S(2)}, u32[]{:S(2)}) collective-permute-start(f32[256,1024]{1,0:T(8,128)S(1)} %collective-permute-done.16.refs_0_), channel_id=1, source_target_pairs={{0,1},{1,0},{2,3},{3,2},{4,5},{5,4},{6,7},{7,6},{8,9},{9,8},{10,11... | collective-permute-start | bytes 3145736 | tf_op jit(solution)/shard_map/ppermute | solution.py:730
  167.8 25.3 %collective-permute-start.21 = (f32[256,1024]{1,0:T(8,128)S(1)}, f32[256,1024]{1,0:T(8,128)S(1)}, u32[]{:S(2)}, u32[]{:S(2)}) collective-permute-start(f32[256,1024]{1,0:T(8,128)S(1)} %copy-done.49), channel_id=1, source_target_pairs={{0,4},{1,5},{2,6},{3,7},{4,0},{5,1},{6,2},{7,3},{8,12},{9,13},{10,... | collective-permute-start | bytes 3145736 | tf_op jit(solution)/shard_map/ppermute | solution.py:730
  193.1 14.3 %collective-permute-start.23 = (f32[128,1024]{1,0:T(8,128)S(1)}, f32[128,1024]{1,0:T(8,128)S(1)}, u32[]{:S(2)}, u32[]{:S(2)}) collective-permute-start(f32[128,1024]{1,0:T(8,128)S(1)} %add.188), channel_id=1, source_target_pairs={{0,2},{1,3},{2,0},{3,1},{4,6},{5,7},{6,4},{7,5},{8,10},{9,11},{10,... | collective-permute-start | bytes 1572872 | tf_op jit(solution)/shard_map/ppermute | solution.py:730
  207.6 23.1 %collective-permute-start.18 = (f32[128,1024]{1,0:T(8,128)S(1)}, f32[128,1024]{1,0:T(8,128)S(1)}, u32[]{:S(2)}, u32[]{:S(2)}) collective-permute-start(f32[128,1024]{1,0:T(8,128)S(1)} %add.184), channel_id=1, source_target_pairs={{0,2},{1,3},{2,0},{3,1},{4,6},{5,7},{6,4},{7,5},{8,10},{9,11},{10,... | collective-permute-start | bytes 1572872 | tf_op jit(solution)/shard_map/ppermute | solution.py:730
  212.8 21.0 %collective-permute-start.28 = (f32[240,640]{1,0:T(8,128)}, f32[240,640]{1,0:T(8,128)S(1)}, u32[]{:S(2)}, u32[]{:S(2)}) collective-permute-start(f32[240,640]{1,0:T(8,128)} %get-tuple-element.322), channel_id=1, source_target_pairs={{0,8},{1,9},{2,10},{3,11},{4,12},{5,13},{6,14},{7,15},{24,16},{25,... | collective-permute-start | bytes 1843208 | tf_op jit(solution)/shard_map/ppermute | solution.py:730
  230.9 27.1 %collective-permute-start.25 = (f32[240,640]{1,0:T(8,128)S(1)}, f32[240,640]{1,0:T(8,128)S(1)}, u32[]{:S(2)}, u32[]{:S(2)}) collective-permute-start(f32[240,640]{1,0:T(8,128)S(1)} %copy-done.19), channel_id=1, source_target_pairs={{0,8},{1,9},{2,10},{3,11},{4,12},{5,13},{6,14},{7,15},{24,16},{25,... | collective-permute-start | bytes 1843208 | tf_op jit(solution)/shard_map/ppermute | solution.py:730
  232.5 46.9 %collective-permute-start.30 = (f32[240,640]{1,0:T(8,128)S(1)}, f32[240,640]{1,0:T(8,128)S(1)}, u32[]{:S(2)}, u32[]{:S(2)}) collective-permute-start(f32[240,640]{1,0:T(8,128)S(1)} %copy-done.18), channel_id=1, source_target_pairs={{0,8},{1,9},{2,10},{3,11},{4,12},{5,13},{6,14},{7,15},{24,16},{25,... | collective-permute-start | bytes 1843208 | tf_op jit(solution)/shard_map/ppermute | solution.py:730
  233.9 27.7 %collective-permute-start.31 = (f32[240,640]{1,0:T(8,128)S(1)}, f32[240,640]{1,0:T(8,128)S(1)}, u32[]{:S(2)}, u32[]{:S(2)}) collective-permute-start(f32[240,640]{1,0:T(8,128)S(1)} %add.191), channel_id=1, source_target_pairs={{8,16},{9,17},{10,18},{11,19},{12,20},{13,21},{14,22},{15,23},{16,... | collective-permute-start | bytes 1843208 | tf_op jit(solution)/shard_map/ppermute | solution.py:730
  258.1 22.2 %collective-permute-start.29 = (f32[240,640]{1,0:T(8,128)S(1)}, f32[240,640]{1,0:T(8,128)}, u32[]{:S(2)}, u32[]{:S(2)}) collective-permute-start(f32[240,640]{1,0:T(8,128)S(1)} %add.192), channel_id=1, source_target_pairs={{8,16},{9,17},{10,18},{11,19},{12,20},{13,21},{14,22},{15,23},{16,... | collective-permute-start | bytes 1843208 | tf_op jit(solution)/shard_map/ppermute | solution.py:730
  261.7 21.1 %collective-permute-start.35 = (f32[240,640]{1,0:T(8,128)S(1)}, f32[240,640]{1,0:T(8,128)}, u32[]{:S(2)}, u32[]{:S(2)}) collective-permute-start(f32[240,640]{1,0:T(8,128)S(1)} %add.193), channel_id=1, source_target_pairs={{8,0},{9,1},{10,2},{11,3},{12,4},{13,5},{14,6},{15,7},{16,24},{17,... | collective-permute-start | bytes 1843208 | tf_op jit(solution)/shard_map/ppermute | solution.py:730
  272.0 46.7 %collective-permute-start.39 = (f32[328,1024]{1,0:T(8,128)}, f32[328,1024]{1,0:T(8,128)}, u32[]{:S(2)}, u32[]{:S(2)}) collective-permute-start(f32[328,1024]{1,0:T(8,128)} %get-tuple-element.377), channel_id=1, source_target_pairs={{0,4},{1,5},{2,6},{3,7},{4,0},{5,1},{6,2},{7,3},{8,12},{9,13},{10,... | collective-permute-start | bytes 4030472 | tf_op jit(solution)/shard_map/ppermute | solution.py:730
  273.6 18.3 %collective-permute-start.34 = (f32[240,640]{1,0:T(8,128)S(1)}, f32[240,640]{1,0:T(8,128)S(1)}, u32[]{:S(2)}, u32[]{:S(2)}) collective-permute-start(f32[240,640]{1,0:T(8,128)S(1)} %copy-done.17), channel_id=1, source_target_pairs={{0,8},{1,9},{2,10},{3,11},{4,12},{5,13},{6,14},{7,15},{24,16},{25,... | collective-permute-start | bytes 1843208 | tf_op jit(solution)/shard_map/ppermute | solution.py:730
  279.5 17.0 %collective-permute-start.33 = (f32[240,640]{1,0:T(8,128)S(1)}, f32[240,640]{1,0:T(8,128)S(1)}, u32[]{:S(2)}, u32[]{:S(2)}) collective-permute-start(f32[240,640]{1,0:T(8,128)S(1)} %add.198), channel_id=1, source_target_pairs={{8,16},{9,17},{10,18},{11,19},{12,20},{13,21},{14,22},{15,23},{16,... | collective-permute-start | bytes 1843208 | tf_op jit(solution)/shard_map/ppermute | solution.py:730
  281.5 16.7 %collective-permute-start.32 = (f32[240,640]{1,0:T(8,128)S(1)}, f32[240,640]{1,0:T(8,128)S(1)}, u32[]{:S(2)}, u32[]{:S(2)}) collective-permute-start(f32[240,640]{1,0:T(8,128)S(1)} %add.199), channel_id=1, source_target_pairs={{8,0},{9,1},{10,2},{11,3},{12,4},{13,5},{14,6},{15,7},{16,24},{17,... | collective-permute-start | bytes 1843208 | tf_op jit(solution)/shard_map/ppermute | solution.py:730
  283.9 33.1 %collective-permute-start.40 = (f32[240,640]{1,0:T(8,128)S(1)}, f32[240,640]{1,0:T(8,128)S(1)}, u32[]{:S(2)}, u32[]{:S(2)}) collective-permute-start(f32[240,640]{1,0:T(8,128)S(1)} %broadcast_select_fusion.5.refs_1_), channel_id=1, source_target_pairs={{0,4},{1,5},{2,6},{3,7},{4,0},{5,1},{6,2},{7,3},{8,12},{9,13},{10,... | collective-permute-start | bytes 1843208 | tf_op jit(solution)/shard_map/ppermute | solution.py:730
  292.0 44.7 %collective-permute-start.24 = (f32[240,640]{1,0:T(8,128)S(1)}, f32[240,640]{1,0:T(8,128)S(1)}, u32[]{:S(2)}, u32[]{:S(2)}) collective-permute-start(f32[240,640]{1,0:T(8,128)S(1)} %copy-done.16), channel_id=1, source_target_pairs={{0,8},{1,9},{2,10},{3,11},{4,12},{5,13},{6,14},{7,15},{24,16},{25,... | collective-permute-start | bytes 1843208 | tf_op jit(solution)/shard_map/ppermute | solution.py:730
  296.5 33.2 %collective-permute-start.38 = (f32[240,640]{1,0:T(8,128)S(1)}, f32[240,640]{1,0:T(8,128)S(1)}, u32[]{:S(2)}, u32[]{:S(2)}) collective-permute-start(f32[240,640]{1,0:T(8,128)S(1)} %add.200), channel_id=1, source_target_pairs={{8,16},{9,17},{10,18},{11,19},{12,20},{13,21},{14,22},{15,23},{16,... | collective-permute-start | bytes 1843208 | tf_op jit(solution)/shard_map/ppermute | solution.py:730
  298.2 37.8 %collective-permute-start.37 = (f32[240,640]{1,0:T(8,128)S(1)}, f32[240,640]{1,0:T(8,128)S(1)}, u32[]{:S(2)}, u32[]{:S(2)}) collective-permute-start(f32[240,640]{1,0:T(8,128)S(1)} %add.201), channel_id=1, source_target_pairs={{8,0},{9,1},{10,2},{11,3},{12,4},{13,5},{14,6},{15,7},{16,24},{17,... | collective-permute-start | bytes 1843208 | tf_op jit(solution)/shard_map/ppermute | solution.py:730
  317.1 19.6 %collective-permute-start.36 = (f32[240,640]{1,0:T(8,128)S(1)}, f32[240,640]{1,0:T(8,128)S(1)}, u32[]{:S(2)}, u32[]{:S(2)}) collective-permute-start(f32[240,640]{1,0:T(8,128)S(1)} %broadcast_select_fusion.4.refs_2_), channel_id=1, source_target_pairs={{0,4},{1,5},{2,6},{3,7},{4,0},{5,1},{6,2},{7,3},{8,12},{9,13},{10,... | collective-permute-start | bytes 1843208 | tf_op jit(solution)/shard_map/ppermute | solution.py:730
  329.8 15.3 %collective-permute-start.45 = (f32[240,640]{1,0:T(8,128)S(1)}, f32[240,640]{1,0:T(8,128)S(1)}, u32[]{:S(2)}, u32[]{:S(2)}) collective-permute-start(f32[240,640]{1,0:T(8,128)S(1)} %add.205), channel_id=1, source_target_pairs={{8,0},{9,1},{10,2},{11,3},{12,4},{13,5},{14,6},{15,7},{16,24},{17,... | collective-permute-start | bytes 1843208 | tf_op jit(solution)/shard_map/ppermute | solution.py:730
  331.1 21.8 %collective-permute-start.43 = (f32[240,640]{1,0:T(8,128)S(1)}, f32[240,640]{1,0:T(8,128)S(1)}, u32[]{:S(2)}, u32[]{:S(2)}) collective-permute-start(f32[240,640]{1,0:T(8,128)S(1)} %copy-done.15), channel_id=1, source_target_pairs={{0,8},{1,9},{2,10},{3,11},{4,12},{5,13},{6,14},{7,15},{24,16},{25,... | collective-permute-start | bytes 1843208 | tf_op jit(solution)/shard_map/ppermute | solution.py:730
  336.0 16.9 %collective-permute-start.44 = (f32[240,640]{1,0:T(8,128)S(1)}, f32[240,640]{1,0:T(8,128)S(1)}, u32[]{:S(2)}, u32[]{:S(2)}) collective-permute-start(f32[240,640]{1,0:T(8,128)S(1)} %broadcast_select_fusion.3.refs_3_), channel_id=1, source_target_pairs={{0,4},{1,5},{2,6},{3,7},{4,0},{5,1},{6,2},{7,3},{8,12},{9,13},{10,... | collective-permute-start | bytes 1843208 | tf_op jit(solution)/shard_map/ppermute | solution.py:730
  336.7 17.8 %collective-permute-start.42 = (f32[240,640]{1,0:T(8,128)S(1)}, f32[240,640]{1,0:T(8,128)S(1)}, u32[]{:S(2)}, u32[]{:S(2)}) collective-permute-start(f32[240,640]{1,0:T(8,128)S(1)} %add.206), channel_id=1, source_target_pairs={{8,16},{9,17},{10,18},{11,19},{12,20},{13,21},{14,22},{15,23},{16,... | collective-permute-start | bytes 1843208 | tf_op jit(solution)/shard_map/ppermute | solution.py:730
  345.2 37.6 %collective-permute-start.50 = (f32[240,640]{1,0:T(8,128)S(1)}, f32[240,640]{1,0:T(8,128)}, u32[]{:S(2)}, u32[]{:S(2)}) collective-permute-start(f32[240,640]{1,0:T(8,128)S(1)} %broadcast_select_fusion.2.refs_4_), channel_id=1, source_target_pairs={{0,4},{1,5},{2,6},{3,7},{4,0},{5,1},{6,2},{7,3},{8,12},{9,13},{10,... | collective-permute-start | bytes 1843208 | tf_op jit(solution)/shard_map/ppermute | solution.py:730
  353.0 37.9 %collective-permute-start.48 = (f32[240,640]{1,0:T(8,128)S(1)}, f32[240,640]{1,0:T(8,128)}, u32[]{:S(2)}, u32[]{:S(2)}) collective-permute-start(f32[240,640]{1,0:T(8,128)S(1)} %add.208), channel_id=1, source_target_pairs={{8,16},{9,17},{10,18},{11,19},{12,20},{13,21},{14,22},{15,23},{16,... | collective-permute-start | bytes 1843208 | tf_op jit(solution)/shard_map/ppermute | solution.py:730
  354.6 38.7 %collective-permute-start.47 = (f32[240,640]{1,0:T(8,128)S(1)}, f32[240,640]{1,0:T(8,128)}, u32[]{:S(2)}, u32[]{:S(2)}) collective-permute-start(f32[240,640]{1,0:T(8,128)S(1)} %add.209), channel_id=1, source_target_pairs={{8,0},{9,1},{10,2},{11,3},{12,4},{13,5},{14,6},{15,7},{16,24},{17,... | collective-permute-start | bytes 1843208 | tf_op jit(solution)/shard_map/ppermute | solution.py:730
  355.9 23.9 %collective-permute-start.51 = (f32[72,1024]{1,0:T(8,128)S(1)}, f32[72,1024]{1,0:T(8,128)S(1)}, u32[]{:S(2)}, u32[]{:S(2)}) collective-permute-start(f32[72,1024]{1,0:T(8,128)S(1)} %add.207), channel_id=1, source_target_pairs={{8,0},{9,1},{10,2},{11,3},{12,4},{13,5},{14,6},{15,7},{16,24},{17,... | collective-permute-start | bytes 884744 | tf_op jit(solution)/shard_map/ppermute | solution.py:730
  357.2 31.0 %collective-permute-start.49 = (f32[128,1024]{1,0:T(8,128)S(1)}, f32[128,1024]{1,0:T(8,128)}, u32[]{:S(2)}, u32[]{:S(2)}) collective-permute-start(f32[128,1024]{1,0:T(8,128)S(1)} %get-tuple-element.440), channel_id=1, source_target_pairs={{0,8},{1,9},{2,10},{3,11},{4,12},{5,13},{6,14},{7,15},{24,16},{25,... | collective-permute-start | bytes 1572872 | tf_op jit(solution)/shard_map/ppermute | solution.py:730
  379.8 18.2 %collective-permute-start.53 = (f32[128,1024]{1,0:T(8,128)}, f32[128,1024]{1,0:T(8,128)}, u32[]{:S(2)}, u32[]{:S(2)}) collective-permute-start(f32[128,1024]{1,0:T(8,128)} %get-tuple-element.441), channel_id=1, source_target_pairs={{0,8},{1,9},{2,10},{3,11},{4,12},{5,13},{6,14},{7,15},{24,16},{25,... | collective-permute-start | bytes 1572872 | tf_op jit(solution)/shard_map/ppermute | solution.py:730
  389.4 25.3 %collective-permute-start.52 = (f32[128,1024]{1,0:T(8,128)S(1)}, f32[128,1024]{1,0:T(8,128)}, u32[]{:S(2)}, u32[]{:S(2)}) collective-permute-start(f32[128,1024]{1,0:T(8,128)S(1)} %add.211), channel_id=1, source_target_pairs={{8,16},{9,17},{10,18},{11,19},{12,20},{13,21},{14,22},{15,23},{16,... | collective-permute-start | bytes 1572872 | tf_op jit(solution)/shard_map/ppermute | solution.py:730
  392.0 25.9 %collective-permute-start.58 = (f32[240,640]{1,0:T(8,128)S(1)}, f32[240,640]{1,0:T(8,128)}, u32[]{:S(2)}, u32[]{:S(2)}) collective-permute-start(f32[240,640]{1,0:T(8,128)S(1)} %add.212), channel_id=1, source_target_pairs={{8,0},{9,1},{10,2},{11,3},{12,4},{13,5},{14,6},{15,7},{16,24},{17,... | collective-permute-start | bytes 1843208 | tf_op jit(solution)/shard_map/ppermute | solution.py:730
  394.6 31.5 %collective-permute-start.59 = (f32[240,640]{1,0:T(8,128)S(1)}, f32[240,640]{1,0:T(8,128)}, u32[]{:S(2)}, u32[]{:S(2)}) collective-permute-start(f32[240,640]{1,0:T(8,128)S(1)} %broadcast_select_fusion.1.refs_1_), channel_id=1, source_target_pairs={{0,4},{1,5},{2,6},{3,7},{4,0},{5,1},{6,2},{7,3},{8,12},{9,13},{10,... | collective-permute-start | bytes 1843208 | tf_op jit(solution)/shard_map/ppermute | solution.py:730
  398.0 25.9 %collective-permute-start.63 = (f32[128,1024]{1,0:T(8,128)S(1)}, f32[128,1024]{1,0:T(8,128)}, u32[]{:S(2)}, u32[]{:S(2)}) collective-permute-start(f32[128,1024]{1,0:T(8,128)S(1)} %slice.37), channel_id=1, source_target_pairs={{0,1},{1,0},{2,3},{3,2},{4,5},{5,4},{6,7},{7,6},{8,9},{9,8},{10,11... | collective-permute-start | bytes 1572872 | tf_op jit(solution)/shard_map/ppermute | solution.py:730
  399.4 21.3 %collective-permute-start.56 = (f32[128,1024]{1,0:T(8,128)S(1)}, f32[128,1024]{1,0:T(8,128)}, u32[]{:S(2)}, u32[]{:S(2)}) collective-permute-start(f32[128,1024]{1,0:T(8,128)S(1)} %add.215), channel_id=1, source_target_pairs={{8,16},{9,17},{10,18},{11,19},{12,20},{13,21},{14,22},{15,23},{16,... | collective-permute-start | bytes 1572872 | tf_op jit(solution)/shard_map/ppermute | solution.py:730
  416.6 17.0 %collective-permute-start.55 = (f32[128,1024]{1,0:T(8,128)}, f32[128,1024]{1,0:T(8,128)}, u32[]{:S(2)}, u32[]{:S(2)}) collective-permute-start(f32[128,1024]{1,0:T(8,128)} %add.216), channel_id=1, source_target_pairs={{8,0},{9,1},{10,2},{11,3},{12,4},{13,5},{14,6},{15,7},{16,24},{17,... | collective-permute-start | bytes 1572872 | tf_op jit(solution)/shard_map/ppermute | solution.py:730
  419.1 18.0 %collective-permute-start.60 = (f32[240,640]{1,0:T(8,128)S(1)}, f32[240,640]{1,0:T(8,128)}, u32[]{:S(2)}, u32[]{:S(2)}) collective-permute-start(f32[240,640]{1,0:T(8,128)S(1)} %broadcast_select_fusion.refs_2_), channel_id=1, source_target_pairs={{0,4},{1,5},{2,6},{3,7},{4,0},{5,1},{6,2},{7,3},{8,12},{9,13},{10,... | collective-permute-start | bytes 1843208 | tf_op jit(solution)/shard_map/ppermute | solution.py:730
  422.6 21.0 %collective-permute-start.57 = (f32[128,1024]{1,0:T(8,128)}, f32[128,1024]{1,0:T(8,128)}, u32[]{:S(2)}, u32[]{:S(2)}) collective-permute-start(f32[128,1024]{1,0:T(8,128)} %add.217), channel_id=1, source_target_pairs={{8,0},{9,1},{10,2},{11,3},{12,4},{13,5},{14,6},{15,7},{16,24},{17,... | collective-permute-start | bytes 1572872 | tf_op jit(solution)/shard_map/ppermute | solution.py:730
  425.3 25.8 %collective-permute-start.64 = (f32[256,1024]{1,0:T(8,128)S(1)}, f32[256,1024]{1,0:T(8,128)}, u32[]{:S(2)}, u32[]{:S(2)}) collective-permute-start(f32[256,1024]{1,0:T(8,128)S(1)} %maximum_select_fusion.1), channel_id=1, source_target_pairs={{0,2},{1,3},{2,0},{3,1},{4,6},{5,7},{6,4},{7,5},{8,10},{9,11},{10,... | collective-permute-start | bytes 3145736 | tf_op jit(solution)/shard_map/ppermute | solution.py:730
  435.6 15.6 %collective-permute-start.61 = (f32[128,1024]{1,0:T(8,128)}, f32[128,1024]{1,0:T(8,128)}, u32[]{:S(2)}, u32[]{:S(2)}) collective-permute-start(f32[128,1024]{1,0:T(8,128)} %broadcast_select_fusion.7.refs_1_), channel_id=1, source_target_pairs={{0,4},{1,5},{2,6},{3,7},{4,0},{5,1},{6,2},{7,3},{8,12},{9,13},{10,... | collective-permute-start | bytes 1572872 | tf_op jit(solution)/shard_map/ppermute | solution.py:730
  (77 other events, 743.6 us)
Sparse Core Ops, SparseCore 0:
  356.0 56.2 all-reduce.3

commit v3 on v2

--- a/solution.py
+++ b/solution.py
@@ -14,6 +14,7 @@
 EPS = 1e-05
 THETA = 10000.0
 RB = 128
+TR = 32
 VMEM = 56
 F32 = jnp.float32
 BF16 = jnp.bfloat16
@@ -131,11 +132,7 @@
         return pltpu.make_async_copy(self.source.at[g], self.buffer.at[g], self.sems.at[self.at + g])
 
     def start(self):
-        if self.grouped:
-            for g in range(self.buffer.shape[0]):
-                self.copy(g).start()
-        else:
-            self.copy().start()
+        self.copy().start()
 
     def wait(self):
         if not self.waited:
@@ -165,12 +162,13 @@
     add_refs = [next(it) for _ in range(2 if split else 1)] if second else None
     win, wout, g1, g2, cs_ref, sn_ref, seqr, valr, wg, wu, wdt = (next(it) for _ in range(11))
     kt_old, vt_old, n2_old = (next(it) for _ in range(3)) if part else (None, None, None)
+    part_old = next(it) if part and second else None
     cot = next(it) if second else None
     n1_ref, qk_ref, kt_ref, vt_ref, o_ref, lse_ref, h_ref, n2_ref, hidh_ref = (next(it) for _ in range(9))
     n2s_ref = next(it) if part else None
     x_out = next(it)
     if second:
-        duh_ref, part_ref = next(it), next(it)
+        duh_ref, part_refs = next(it), [next(it) for _ in range(2 if part and split else 1)]
     else:
         gate_ref, up_ref = next(it), next(it)
     outs = [next(it) for _ in range(2 if split else 1)]
@@ -221,11 +219,16 @@
             q = masked_heads(qk_ref[g, rows, :128], qk_ref[g, rows, 128:])
             s = dot_nt(q, ktf[:nk, :])
             bias = allowed_bias(seqr, valr, base + r0, nk)
-            s = (s.reshape(3, RB, nk) * 0.125 + bias[None]).reshape(3 * RB, nk)
-            m = jnp.max(s, axis=1, keepdims=True)
-            e = jnp.exp(s - m)
-            l = jnp.sum(e, axis=1, keepdims=True)
-            o = dot(e.astype(BF16), vtf[:nk, :]) / l
+            es, ms, lls = [], [], []
+            for r in range(0, 3 * RB, TR):
+                st = s[r : r + TR] * 0.125 + bias[r % RB : r % RB + TR]
+                mt = jnp.max(st, axis=1, keepdims=True)
+                et = jnp.exp(st - mt)
+                ms.append(mt)
+                lls.append(jnp.sum(et, axis=1, keepdims=True))
+                es.append(et.astype(BF16))
+            m, l = jnp.concatenate(ms, axis=0), jnp.concatenate(lls, axis=0)
+            o = dot(jnp.concatenate(es, axis=0), vtf[:nk, :]) / l
             low = low_half(RB)
             o_ref[g, rows, :128] = jnp.where(low, o[:RB], o[RB : 2 * RB]).astype(BF16)
             o_ref[g, rows, 128:] = jnp.where(low, o[2 * RB :], 0.0).astype(BF16)
@@ -270,8 +273,21 @@
     flush(hidh_ref)
     if second:
         cot = ready(cot)
-        part_ref[...] = dot_nt(hid.astype(BF16), wdt[...])
-        flush(part_ref)
+        if part and split:
+            part_old = ready(part_old)
+            half = t // 2
+            whole[...] = dot_nt(hid.astype(BF16), wdt[...])
+            for ref, which in zip(part_refs, (idx[1], 1 - idx[1])):
+                put_wide(ref.at[:half, :], half_rows(part_old, which, half))
+                put_wide(ref.at[half:, :], half_rows(whole, which, half))
+                flush(ref)
+        elif part:
+            part_old = ready(part_old)
+            put_wide(part_refs[0].at[:t, :], part_old[...])
+            put_wide(part_refs[0].at[t:, :], dot_nt(hid.astype(BF16), wdt[...]))
+        else:
+            part_refs[0][...] = dot_nt(hid.astype(BF16), wdt[...])
+            flush(part_refs[0])
         dgate, dup = ffn_back(dot(cot[base : base + t, :], wdt[...]), gate, up, sig)
         store_pair(idx, duh_ref, every, dgate, dup)
         flush(duh_ref)
@@ -332,12 +348,16 @@
     s = dot_nt(q, kt)
     dp = dot_nt(dos, vtf(nk))
     bias = allowed_bias(seqr, valr, base + r0, nk)
-    s = (s.reshape(3, RB, nk) * 0.125 + bias[None]).reshape(3 * RB, nk)
-    p = jnp.exp(s - lse)
-    ds = (p * (dp - delta)).astype(BF16)
+    ps, dss = [], []
+    for r in range(0, 3 * RB, TR):
+        part = slice(r, r + TR)
+        pt = jnp.exp(s[part] * 0.125 + bias[r % RB : r % RB + TR] - lse[part])
+        ps.append(pt.astype(BF16))
+        dss.append((pt * (dp[part] - delta[part])).astype(BF16))
+    p, ds = jnp.concatenate(ps, axis=0), jnp.concatenate(dss, axis=0)
     dq = dot(ds, kt) * 0.125
     dkv[0, :nk, :] += dot_tn(ds, q)
-    dkv[1, :nk, :] += dot_tn(p.astype(BF16), dos)
+    dkv[1, :nk, :] += dot_tn(p, dos)
     return jnp.where(low, dq[:RB], dq[RB : 2 * RB]), dq[2 * RB :]
 
 
@@ -377,7 +397,8 @@
     dn2_refs = [next(it) for _ in range(2 if split else 1)]
     (dz_ref, h_ref, qk_ref, kt_ref, vt_ref, o_ref, lse_ref, xa_ref, xb_ref, kt_old, vt_old, dha_ref, dqxa_ref, dqya_ref,
      dkva_ref, win, wout, g1, g2, cs_ref, sn_ref, seqr, valr) = (next(it) for _ in range(23))
-    da_ref, dpa_ref, dpb_ref, dxa_ref, dxb_ref, dg1_ref, dg2_ref = (next(it) for _ in range(7))
+    da_ref, dpa_ref, dpb_ref, dg1_ref, dg2_ref, dxa_ref = (next(it) for _ in range(6))
+    dxb_ref = None if last else next(it)
     dfs_ref = None if last else next(it)
     dh_ref, acca, accb, dkv, ktf, vtf, dqy_ref = (next(it) for _ in range(7))
     t = dh_ref.shape[0]
@@ -426,10 +447,14 @@
     dxa, dg1a = norm_back(acca[...], xa_ref[...].astype(F32), g1[...])
     dxb, dg1b = norm_back(accb[...], xb_ref[...].astype(F32), g1[...])
     dg1_ref[...] = dg1a + dg1b
-    dxa_ref[...] = (dxa + dha_ref[...]).astype(dxa_ref.dtype)
-    dxb_ref[...] = (dxb + dh_ref[...]).astype(dxb_ref.dtype)
-    flush(dxa_ref)
-    flush(dxb_ref)
+    if last:
+        dxa_ref[:, :t] = (dxa + dha_ref[...]).T.astype(BF16)
+        dxa_ref[:, t:] = (dxb + dh_ref[...]).T.astype(BF16)
+    else:
+        dxa_ref[...] = dxa + dha_ref[...]
+        dxb_ref[...] = dxb + dh_ref[...]
+        flush(dxa_ref)
+        flush(dxb_ref)
     if not last:
         if split:
             for c in range(2):
@@ -612,7 +637,22 @@
     put_wide(send.at[:lead, :], half_rows(extra, 1 - idx[0], half))
 
 
-def attn_finish_kernel(parts, idx, a0, a1, b0, b1, slot1, gin, gout):
+def out_kernel(idx, ha, hb, *refs):
+    pieces, out, whole = refs[:-2], refs[-2], refs[-1]
+    t, d = ha.shape
+    half = t // len(pieces)
+    for k, h in enumerate((ha, hb)):
+        if len(pieces) == 1:
+            whole[...] = pieces[0][k * t : k * t + t, :d]
+        else:
+            rows = slice(k * half, k * half + half)
+            whole[pl.ds(pl.multiple_of(idx[1] * half, half), half), :] = pieces[0][rows, :d]
+            whole[pl.ds(pl.multiple_of((1 - idx[1]) * half, half), half), :] = pieces[1][rows, :d]
+        out[:, k * t : k * t + t] = (whole[...] + h[...]).T.astype(BF16)
+
+
+def attn_finish_kernel(parts, idx, a0, a1, b0, b1, *rest):
+    slot1, gin, gout = rest[:-2], *rest[-2:]
     d = gin.shape[2]
     for xi in range(2):
         @pl.when(idx[0] == xi)
@@ -625,10 +665,12 @@
             gout[0, 64:, :] = q1[:, :d]
     mine = idx[5].astype(F32)
     rows_in, rows_out = 320 // parts, 192 // parts
-    for k in range(parts):
-        r = k * (rows_in + rows_out)
-        gin[1, k * rows_in : (k + 1) * rows_in, :] = slot1[r : r + rows_in, :d] * mine
-        gout[1, k * rows_out : (k + 1) * rows_out, :] = slot1[r + rows_in : r + rows_in + rows_out, :d] * mine
+    for k, quarter in enumerate(slot1):
+        m = (idx[4] // 2 * (1 - k % 2) + (1 - idx[4] // 2) * (k % 2)) * 2 + (
+            idx[4] % 2 * (1 - k // 2) + (1 - idx[4] % 2) * (k // 2))
+        gin[1, pl.ds(pl.multiple_of(m * rows_in, 8), rows_in), :] = quarter[:rows_in, :d] * mine
+        gout[1, pl.ds(pl.multiple_of(m * rows_out, 8), rows_out), :] = (
+            quarter[rows_in : rows_in + rows_out, :d] * mine)
 
 
 def idx_parts(extra):
@@ -651,7 +693,7 @@
     return math.prod(a.shape) * jnp.dtype(a.dtype).itemsize
 
 
-def call(kernel, outs, ins, scratch=(), smem=0, flops=0, late=(), grouped=()):
+def call(kernel, outs, ins, scratch=(), smem=0, flops=0, late=(), grouped=(), first=()):
     n_in, n_out = len(ins), len(outs)
     big_in = [i for i in range(smem, n_in) if size(ins[i]) >= BIG]
     big_out = [i for i in range(n_out) if size(outs[i]) >= BIG]
@@ -672,13 +714,20 @@
         ins_, outs_, rest = list(refs[:n_in]), list(refs[n_in : n_in + n_out]), list(refs[n_in + n_out :])
         own, (bufs, sem) = rest[: len(scratch)], (rest[len(scratch) : -1], rest[-1])
         kept = []
-        order = [i for i in big_in if i not in late and i not in grouped]
-        order += [i for i in big_in if i in grouped] + [i for i in late if i in big_in]
-        for i in order:
-            k = big_in.index(i)
-            item = Late(ins_[i], bufs[k], sem, at[i], i in grouped)
-            item.start()
-            kept.append((i, item))
+        for k, i in enumerate(big_in):
+            kept.append((i, Late(ins_[i], bufs[k], sem, at[i], i in grouped)))
+        items = dict(kept)
+        for i in big_in:
+            if i not in late and i not in grouped:
+                items[i].start()
+        for i in first:
+            items[i].start()
+        for g in range(max((ins[i].shape[0] for i in grouped), default=0)):
+            for i in grouped:
+                items[i].copy(g).start()
+        for i in late:
+            if i in items and i not in first:
+                items[i].start()
         for i, item in kept:
             early = i not in late and i not in grouped
             ins_[i] = item.wait() if early else item
@@ -698,7 +747,6 @@
             pltpu.make_async_copy(outs_[i], out, s).wait()
         OUT.clear()
 
-    moved = sum(size(a) for a in list(ins) + list(outs))
     return pl.pallas_call(
         body,
         out_shape=tuple(outs),
@@ -706,12 +754,58 @@
         out_specs=tuple(out_specs),
         scratch_shapes=list(scratch) + buffers + [sems],
         compiler_params=pltpu.CompilerParams(vmem_limit_bytes=VMEM * 1024 * 1024),
-        cost_estimate=pl.CostEstimate(flops=flops, bytes_accessed=moved, transcendentals=0),
+        cost_estimate=pl.CostEstimate(flops=1, bytes_accessed=1, transcendentals=0),
     )(*ins)
 
 
 def S(shape, dtype):
     return jax.ShapeDtypeStruct(shape, dtype)
+
+
+def add_kernel(a, b, out):
+    out[...] = a[...] + b[...]
+
+
+def pick_kernel(flag, a, b, out):
+    @pl.when(flag[0] == 1)
+    def _():
+        out[...] = a[...]
+
+    @pl.when(flag[0] != 1)
+    def _():
+        out[...] = b[...]
+
+
+def small_call(kernel, ins, smem=0):
+    a = ins[-1]
+    return pl.pallas_call(
+        kernel,
+        out_shape=jax.ShapeDtypeStruct(a.shape, a.dtype),
+        in_specs=[pl.BlockSpec(memory_space=pltpu.SMEM)] * smem + [pl.BlockSpec(memory_space=pltpu.VMEM)] * 2,
+        out_specs=pl.BlockSpec(memory_space=pltpu.VMEM),
+        compiler_params=pltpu.CompilerParams(vmem_limit_bytes=8 * 2**20),
+        cost_estimate=pl.CostEstimate(flops=1, bytes_accessed=1, transcendentals=0),
+    )(*ins)
+
+
+def add(a, b):
+    return small_call(add_kernel, [a, b])
+
+
+def add_pieces(keeps, got):
+    def kernel(*refs):
+        n = len(keeps)
+        at = 0
+        for keep, out in zip(refs[:n], refs[n + 1 :]):
+            out[...] = keep[...] + refs[n][at : at + keep.shape[0], :]
+            at += keep.shape[0]
+
+    return pl.pallas_call(
+        kernel,
+        out_shape=tuple(jax.ShapeDtypeStruct(k.shape, k.dtype) for k in keeps),
+        compiler_params=pltpu.CompilerParams(vmem_limit_bytes=12 * 2**20),
+        cost_estimate=pl.CostEstimate(flops=1, bytes_accessed=1, transcendentals=0),
+    )(*keeps, got)
 
 
 class Links:
@@ -748,7 +842,7 @@
         return self.permute(v, lambda z, x, y, c: (3 - z, x, y, c) if z in (1, 2) else None)
 
     def sum_cores(self, pieces):
-        return pieces[0] + self.core(pieces[1]) if self.known else pieces[0]
+        return add(pieces[0], self.core(pieces[1])) if self.known else pieces[0]
 
     def y_start(self, r):
         return self.y(r) if self.known else r
@@ -756,13 +850,13 @@
     def sum_chips(self, r, got):
         if not self.known:
             return [lax.psum(r, "narrow")]
-        r = r + got
+        r = add(r, got)
         return [r, self.core(r)]
 
     def both_cores(self, got):
         return [got, self.core(got)] if self.known else [got]
 
-    def sum_lines(self, chunks, jobs, hooks):
+    def sum_lines(self, chunks, jobs, pieces, finish, hooks):
         last = chunks[0]
         if not self.known:
             for job in jobs:
@@ -782,18 +876,42 @@
             theirs = [self.x(r) for r in vals]
             for c, hook in hooks.items():
                 results[c] = hook(vals, theirs)
+            results[None] = finish([lax.psum(pieces[0], "narrow")])
             return vals, theirs, results
         z = lax.axis_index("wide") // 2
-        inner = (z == 1) | (z == 2)
+        inner = ((z == 1) | (z == 2)).astype(jnp.int32).reshape(1)
         n_keep = 3
         n = len(chunks) + n_keep
-        order = [*range(4), len(chunks), *range(4, len(chunks)), *range(len(chunks) + 1, n)]
-        moved = [self.inward(r) for r in chunks] + [None] * n_keep
+        order = [*range(POS_A), len(chunks), *range(POS_A, len(chunks)), *range(len(chunks) + 1, n)]
+        moved = [None] * n
+        for c in order[:U_AHEAD]:
+            moved[c] = self.inward(chunks[c])
         vals, theirs, results = list(chunks) + [None] * n_keep, [None] * n, {}
-        last = jobs[0](last)[0]
-        for s in range(n + 3):
+        tr = self.core(pieces[1])
+        for s in range(n + LAGS[3]):
+            if s == OUT_SLOTS[0]:
+                tr = last = add(pieces[0], after(tr, last))
+                ty = self.y(tr)
+            if s == OUT_SLOTS[1]:
+                tr = last = add(tr, after(ty, last))
+                tc = self.core(tr)
+            if s == OUT_SLOTS[2]:
+                results[None] = finish([tr, after(tc, last)])
+                last = results[None][0]
+            if s in J_SLOTS:
+                made = jobs[J_SLOTS.index(s)](last)
+                last = made[0]
+            if s == J_SLOTS[2]:
+                *keeps, send = made
+                got = self.x(send)
+            if s == R_SLOT:
+                got = after(got, last)
+                sums = add_pieces(keeps, got)
+                last = sums[0]
+                for i, v in enumerate(sums):
+                    vals[len(chunks) + i] = v
             for stage in range(4):
-                c = s - stage
+                c = s - LAGS[stage]
                 if not 0 <= c < n:
                     continue
                 c = order[c]
@@ -804,38 +922,23 @@
                         last = results[c][0]
                     continue
                 new = after(moved[c], last)
-                vals[c] = jnp.where(inner, vals[c], new) if stage == 2 else vals[c] + new
+                vals[c] = small_call(pick_kernel, [inner, vals[c], new], 1) if stage == 2 else add(vals[c], new)
                 last = vals[c]
                 if stage == 0:
                     moved[c] = self.middle(vals[c])
+                    if s + U_AHEAD < n:
+                        p = order[s + U_AHEAD]
+                        moved[p] = self.inward(after(vals[p], last))
                 elif stage == 1:
                     moved[c] = self.outward(vals[c])
                 else:
                     theirs[c] = self.x(vals[c])
-            if s == 0:
-                last = jobs[1](last)[0]
-            if s == 1:
-                *keeps, send = jobs[2](last)
-                last = keeps[0]
-                got = self.x(send)
-            if s == 3:
-                got = after(got, last)
-                at = 0
-                for i, keep in enumerate(keeps):
-                    c = len(chunks) + i
-                    vals[c] = last = keep + got[at : at + keep.shape[0]]
-                    at += keep.shape[0]
-                    moved[c] = self.inward(last)
         return vals, theirs, results
 
     def gather_narrow(self, v):
-        if not self.known:
-            return lax.all_gather(v, "narrow", axis=0, tiled=True)
-        n = lax.axis_index("narrow")
-        o = self.core(v)
-        two = jnp.where(n % 2 == 0, jnp.concatenate([v, o], 0), jnp.concatenate([o, v], 0))
-        o = self.y(two)
-        return jnp.where(n // 2 == 0, jnp.concatenate([two, o], 0), jnp.concatenate([o, two], 0))
+        o = self.permute(v, lambda z, x, y, c: (z, x, 1 - y, c))
+        p = self.permute(v, lambda z, x, y, c: (z, x, y, 1 - c))
+        return [v, o, p, self.permute(o, lambda z, x, y, c: (z, x, y, 1 - c))]
 
 
 def tie(*groups):
@@ -846,6 +949,12 @@
     return lax.optimization_barrier((v, *deps))[0]
 
 
+LAGS = (0, 1, 2, 5)
+POS_A = 6
+R_SLOT = 4
+U_AHEAD = 2
+J_SLOTS = (0, 1, 2)
+OUT_SLOTS = (2, 5, 7)
 CHUNKS = (240, 240, 240, 240, 240, 240)
 
 
@@ -892,14 +1001,16 @@
     def forward(second, x, adds, old):
         part = old is not None
         outs = list(saved) + ([piece] if part else [])
-        outs += [S((th, d), F32), S((th, f), BF16), S((th, d), F32)] if second else [S((th, d), BF16)] + [S((th, f), F32)] * 2
+        outs += [S((th, d), F32), S((th, f), BF16)] + ([piece] * n_sums if part else [S((th, d), F32)]) if second else [S((th, d), BF16)] + [S((th, f), F32)] * 2
         ins = [idx, x, *adds] + weights + ffn_w
         at = 2 + len(adds)
         ins += [old[2], old[3], old[7]] if part else []
+        ins += [old[9]] if part and second else []
         ins += [cotangent] if second else []
         res = call(functools.partial(fwd_kernel, second, split, int(part), groups), outs + sums, ins, scratch, smem=1,
-                   flops=4 * 10**9, grouped=[at, at + 1],
+                   flops=4 * 10**9, grouped=[at, at + 1], first=[at + 4, at + 5],
                    late=[at + 4, at + 5, at + 8, at + 9, at + 10] + ([at + 13] if part else [])
+                   + ([at + 14] if part and second else [])
                    + ([len(ins) - 1] if second else []))
         return list(res[:-n_sums]), list(res[-n_sums:])
 
@@ -914,23 +1025,23 @@
     y1a = links.y_start(r1a)
     b1, s1b = forward(False, after(tokens_t, r1a), [], a1)
     *b1, n2as, tok_b, gate1b, up1b = b1
-    s1b, n2as, y1a, cot_x = tie(s1b, n2as, y1a, cot_x)
+    s1b, n2as, y1a = tie(s1b, n2as, y1a)
     sum1a = links.sum_chips(r1a, y1a)
     r1b = links.sum_cores(s1b)
     y1b = links.y_start(r1b)
     n2a_x = links.x(n2as)
-    cot_p = links.both_cores(cot_x)
     a2, s2a = forward(True, after(a1[6], r1b), sum1a, None)
     *a2, x1a, duh2a, part2a = a2
-    s2a, y1b, n2a_x = tie(s2a, y1b, n2a_x)
+    s2a, y1b, cot_x = tie(s2a, y1b, cot_x)
     sum1b = links.sum_chips(r1b, y1b)
-    n2a_p = links.both_cores(n2a_x)
+    cot_p = links.both_cores(cot_x)
     r2a = links.sum_cores(s2a)
     y2a = links.y_start(r2a)
-    b2, s2b = forward(True, after(b1[6], r2a, n2a_p, cot_p), sum1b, a2)
-    *b2, n2bs, x1b, duh2b, part2b = b2
+    b2, s2b = forward(True, after(b1[6], r2a, cot_p), sum1b, a2 + [part2a])
+    b2, (n2bs, x1b, duh2b, *out2) = b2[:9], b2[9:]
     h2a, h2b = a2[6], b2[6]
-    s2b, n2bs, y2a = tie(s2b, n2bs, y2a)
+    s2b, n2bs, y2a, n2a_x = tie(s2b, n2bs, y2a, n2a_x)
+    n2a_p = links.both_cores(n2a_x)
     sum2a = links.sum_chips(r2a, y2a)
     r2b = links.sum_cores(s2b)
     y2b = links.y_start(r2b)
@@ -947,12 +1058,12 @@
             functools.partial(bwd_a_kernel, split, groups), outs,
             [idx, *sums, dz, r[6], *r[1:6], attn_out, g2] + tail, smem=1, flops=4 * 10**9,
             grouped=[n_sums + 3, n_sums + 4, n_sums + 5, n_sums + 6, n_sums + 8], late=[n_sums + 7, n_sums + 10, n_sums + 11],
+            first=[n_sums + 7, n_sums + 10, n_sums + 11],
         )
 
     def backward_b(last, sums, dz, first, ra, rb, xa, xb):
-        xt = BF16 if last else F32
-        outs = [S((th, d), BF16), S((groups, th, 320), BF16), S((groups, th, 320), BF16), S((th, d), xt), S((th, d), xt),
-                S((1, d), F32), S((1, d), F32)] + ([] if last else [piece])
+        outs = [S((th, d), BF16), S((groups, th, 320), BF16), S((groups, th, 320), BF16), S((1, d), F32), S((1, d), F32)]
+        outs += [S((d, t), BF16)] if last else [S((th, d), F32), S((th, d), F32), piece]
         dha, _, dqxa, dqya, dkva, _ = first
         return call(
             functools.partial(bwd_b_kernel, last, split, groups), outs,
@@ -961,7 +1072,7 @@
              pltpu.VMEM((t, 128), BF16), pltpu.VMEM((th, 128), F32)],
             smem=1, flops=6 * 10**9,
             grouped=[n_sums + k for k in (3, 4, 5, 6, 10, 11, 13, 14, 15, 16, 17)],
-            late=[n_sums + k for k in (7, 20, 21, 8, 9, 12)],
+            late=[n_sums + k for k in (7, 20, 21, 8, 9, 12)], first=[n_sums + 7, n_sums + 20, n_sums + 21],
         )
 
     acc = call(own_grads_kernel, grad_outs, [after(a2[7], r2b, sum2a), b2[7], duh2a, duh2b, a2[8], b2[8], cotangent],
@@ -969,7 +1080,7 @@
     first2 = backward_a(after(sum2a, acc), cotangent[:th], a2)
     first2, y2b = tie(first2, y2b)
     sum2b = links.sum_chips(r2b, y2b)
-    da2b, dp2a, dp2b, dz1a, dz1b, dg1b, dg2b1, dfs = backward_b(
+    da2b, dp2a, dp2b, dg1b, dg2b1, dz1a, dz1b, dfs = backward_b(
         False, sum2b, cotangent[th:], first2, a2, b2, x1a, x1b)
     dfs, dz1a, dz1b, n2b_x = tie(dfs, dz1a, dz1b, n2b_x)
     df_x = links.x(dfs)
@@ -1021,7 +1132,7 @@
         return made["b"]
 
     def job_grads(dep):
-        first, (da1b, dp1a, dp1b, _, _, dg1a, dg2a1) = made["a"], made["b"]
+        first, (da1b, dp1a, dp1b, dg1a, dg2a1, _) = made["a"], made["b"]
         gains = jnp.concatenate([dg1a + dg1b, first[5] + dg2a1 + dg2b0 + dg2b1], axis=0)
         return call(
             attn_grad_kernel, [S((n, wd), F32) for n in (lead, 128, 128, lead + 256)],
@@ -1030,11 +1141,8 @@
             [pltpu.VMEM((512, d), F32), pltpu.VMEM((quarter + 16, d), F32)], smem=1, flops=2 * 10**9,
         )
 
-    part2 = lax.psum(after((part2a, part2b), y3b), "narrow")
-
-    def finish_out(vals, theirs):
-        total = after(part2, vals[4])
-        return [jnp.concatenate([h + p for h, p in zip((h2a, h2b), total)], axis=0).astype(BF16)]
+    def finish_out(pieces):
+        return call(out_kernel, [S((d, t), BF16)], [idx, h2a, h2b, *pieces], [pltpu.VMEM((th, d), F32)], smem=1)
 
     def unpack(vals, theirs):
         return call(functools.partial(unpack_kernel, 4, False), [S((d, f), F32)] * 2,
@@ -1050,16 +1158,16 @@
         return second, links.gather_narrow(second[:quarter])
 
     done, theirs, results = links.sum_lines(
-        chunks, [job_a, job_b, job_grads], {4: finish_out, 3: unpack, 5: unpack_down, 6: collect})
-    layer_out = results[4][0]
-    dx = jnp.concatenate(made["b"][3:5], axis=0)
+        chunks, [job_a, job_b, job_grads], out2, finish_out, {3: unpack, 5: unpack_down, 6: collect})
+    layer_out = results[None][0].T
+    dx = made["b"][5].T
     ggate, gup = results[3]
     gdown, = results[5]
     second, slot1 = results[6]
     small = second[quarter : quarter + 2, :d]
     gin, gout = call(
         functools.partial(attn_finish_kernel, links.narrow), [S((SLOTS, 320, d), F32), S((SLOTS, 192, d), F32)],
-        [idx, *done[7:], *theirs[7:], slot1], smem=1,
+        [idx, *done[7:], *theirs[7:], *slot1], smem=1,
     )
     gin = jnp.swapaxes(gin, 1, 2)
     return layer_out, dx, gin, gout, ggate, gup, gdown.T, small[0], small[1]

time: 479 us -> 415 us (0.87)
  other arithmetic: 41.1 us -> 6.99 us
  waiting for transfers between devices: 106 us -> 92 us
  starting transfers between devices: 94.2 us -> 80.3 us
  between operations: 16.6 us -> 3.29 us
  Pallas kernels: 194 us -> 204 us
    add x32 -> x0, other arithmetic: 16.4 us -> none  [the longest x18 9.37 us: sum_lines(): vals[c] = jnp.where(inner, vals[c], new) if stage == 2 else vals[c] + new]
    pallas_call x0 -> x42, Pallas kernels: none -> 14.7 us  [the longest x41 13.1 us: small_call(): pl.pallas_call(kernel, out_shape=jax.ShapeDtypeStruct(a.shape, a.dtype),...]
    ppermute x65 -> x69, starting transfers between devices: 94.2 us -> 80.3 us  [permute(): return lax.ppermute(v, ('wide', 'narrow'), pairs)]
    select_n x11 -> x0, other arithmetic: 13 us -> none  [the longest x9 8.32 us: sum_lines(): vals[c] = jnp.where(inner, vals[c], new) if stage == 2 else vals[c] + new]
    psum x1 -> x0, waiting for transfers between devices: 11.4 us -> none  [per_device(): part2 = lax.psum(after((part2a, part2b), y3b), 'narrow')]
    pallas_call x16 -> x17, Pallas kernels: 194 us -> 189 us  [call(): pl.pallas_call(body, out_shape=tuple(outs), in_specs=in_specs, out_specs=...]
    ppermute x65 -> x69, waiting for transfers between devices: 94.2 us -> 92 us  [permute(): return lax.ppermute(v, ('wide', 'narrow'), pairs)]
    unnamed x121 -> x139, local copies, waits for them, and re-layouts: 10.4 us -> 11.8 us
  transfers between devices with their start and end apart: 66 -> 69, of which waited for: 18 -> 25; matrix products, arithmetic and copies ran while one was open for 11% -> 3% of each run, Pallas kernels for 37% -> 45%
where the time goes in v3:
time: 415 us; the launch traced here: 407 us
  Pallas kernels  204 us (49%)
  waiting for transfers between devices  92 us (22%)
  starting transfers between devices  80.3 us (19%)
  local copies, waits for them, and re-layouts  20.4 us (5%)
  other arithmetic  6.99 us (2%)
    pallas_call x17, Pallas kernels, call(): pl.pallas_call(body, out_shape=tuple(outs), in_specs=in_specs, out_specs=...  189 us
    ppermute x69, waiting for transfers between devices, permute(): return lax.ppermute(v, ('wide', 'narrow'), pairs)  92 us
    ppermute x69, starting transfers between devices, permute(): return lax.ppermute(v, ('wide', 'narrow'), pairs)  80.3 us
    pallas_call x41, Pallas kernels, small_call(): pl.pallas_call(kernel, out_shape=jax.ShapeDtypeStruct(a.shape, a.dtype),...  13.1 us
    unnamed x139, local copies, waits for them, and re-layouts  11.8 us
  transfers between devices with their start and end apart: 69, of which 25 were waited for; matrix products, arithmetic and copies ran while one was open for 3% of the time, Pallas kernels for 45%

profile of v3, /device:TPU:0, one launch (start us, length us, event | category | flops | bytes accessed | tf_op | source)
XLA Modules:
  0.0 407.2 jit_solution(15479902180238104941)
XLA Ops:
  2.0 1.8 fusion
  3.8 15.5 %shard_map.196 = (bf16[256,960]{1,0:T(8,128)(2,1)}, bf16[5,256,256]{2,1,0:T(8,128)(2,1)}, bf16[5,256,128]{2,1,0:T(8,128)(2,1)}, bf16[5,256,128]{2,1,0:T(8,128)(2...) custom-call(s32[2]{0:T(128)} %pad_add_fusion.refs_0_, ...), custom_call_target="tpu_custom_call" | custom-call | flops 1 | bytes 1 | tf_op jit(solution)/shard_map/pallas_call | solution.py:750
  19.8 1.7 collective-permute-done.b
  22.7 3.0 collective-permute-start.1
  27.5 16.3 %shard_map.198 = (bf16[256,960]{1,0:T(8,128)(2,1)}, bf16[5,256,256]{2,1,0:T(8,128)(2,1)}, bf16[5,256,128]{2,1,0:T(8,128)(2,1)}, bf16[5,256,128]{2,1,0:T(8,128)(2...) custom-call(s32[2]{0:T(128)} %pad_add_fusion.refs_0_, ...), custom_call_target="tpu_custom_call" | custom-call | flops 1 | bytes 1 | tf_op jit(solution)/shard_map/pallas_call | solution.py:750
  44.0 1.7 collective-permute-start.5
  48.5 17.4 %shard_map.201 = (bf16[256,960]{1,0:T(8,128)(2,1)}, bf16[5,256,256]{2,1,0:T(8,128)(2,1)}, bf16[5,256,128]{2,1,0:T(8,128)(2,1)}, bf16[5,256,128]{2,1,0:T(8,128)(2...) custom-call(s32[2]{0:T(128)} %pad_add_fusion.refs_0_, ...), custom_call_target="tpu_custom_call" | custom-call | flops 1 | bytes 1 | tf_op jit(solution)/shard_map/pallas_call | solution.py:750
  65.9 3.7 collective-permute-done.5.refs_2_
  74.7 18.5 %shard_map.204 = (bf16[256,960]{1,0:T(8,128)(2,1)}, bf16[5,256,256]{2,1,0:T(8,128)(2,1)}, bf16[5,256,128]{2,1,0:T(8,128)(2,1)}, bf16[5,256,128]{2,1,0:T(8,128)(2...) custom-call(s32[2]{0:T(128)} %pad_add_fusion.refs_0_, ...), custom_call_target="tpu_custom_call" | custom-call | flops 1 | bytes 1 | tf_op jit(solution)/shard_map/pallas_call | solution.py:750
  93.2 2.1 collective-permute-done.10.refs_0_
  98.0 1.7 collective-permute-start.15
  99.7 4.7 %shard_map.207 = (f32[960,640]{1,0:T(8,128)}, f32[960,384]{1,0:T(8,128)}) custom-call(bf16[256,960]{1,0:T(8,128)(2,1)} %get-tuple-element.255.refs_17_.refs_0_, bf16[256,960]{1,0:T(8,128)(2,1)} %get-tuple-element.256.refs_1_, bf16[256,640]{1,0:T(8,128)(2,1)} %get-tuple-element.257.refs_2_, bf16[256,640]{1,0:T(8,128)(2,1)} %get-tuple-element.258.refs_3_, ...), custom_call_target="tpu_custom_call" | custom-call | flops 1 | bytes 1 | tf_op jit(solution)/shard_map/pallas_call | solution.py:750
  104.5 12.5 %shard_map.208 = (f32[256,960]{1,0:T(8,128)}, bf16[256,960]{1,0:T(8,128)(2,1)}, bf16[5,256,128]{2,1,0:T(8,128)(2,1)}, f32[5,256,128]{2,1,0:T(8,128)}, f32[5,2,256,128]{3,2,1,0:T(8,128)}, /*index=5*/f32[1,960]{1,0:T(1,128)}) custom-call(s32[2]{0:T(128)} %pad_add_fusion.refs_0_, f32[128,1024]{1,0:T(8,128)} %copy-done.9, f32[128,1024]{1,0:T(8,128)} %copy-done.52, ...), custom_call_target="tpu_custom_call" | custom-call | flops 1 | bytes 1 | tf_op jit(solution)/shard_map/pallas_call | solution.py:750
  117.1 1.9 collective-permute-done.14.refs_2_
  119.8 20.5 %shard_map.210 = (bf16[256,960]{1,0:T(8,128)(2,1)}, bf16[5,256,320]{2,1,0:T(8,128)(2,1)}, bf16[5,256,320]{2,1,0:T(8,128)(2,1)}, f32[1,960]{1,0:T(1,128)}, f32[1,...) custom-call(s32[2]{0:T(128)} %pad_add_fusion.refs_0_, f32[128,1024]{1,0:T(8,128)} %copy-done.11, ...), custom_call_target="tpu_custom_call" | custom-call | flops 1 | bytes 1 | tf_op jit(solution)/shard_map/pallas_call | solution.py:750
  143.2 7.6 %shard_map.211 = (bf16[256,640]{1,0:T(8,128)(2,1)}, bf16[256,640]{1,0:T(8,128)(2,1)}, bf16[256,960]{1,0:T(8,128)(2,1)}, bf16[256,960]{1,0:T(8,128)(2,1)}, f32[12...) custom-call(s32[2]{0:T(128)} %pad_add_fusion.refs_0_, ...), custom_call_target="tpu_custom_call" | custom-call | flops 1 | bytes 1 | tf_op jit(solution)/shard_map/pallas_call | solution.py:750
  156.4 9.1 %shard_map.214 = (f32[960,640]{1,0:T(8,128)}, f32[960,384]{1,0:T(8,128)}) custom-call(f32[256,1024]{1,0:T(8,128)} %copy-done.42, f32[256,1024]{1,0:T(8,128)} %collective-permute-done.16.refs_1_, f32[256,1024]{1,0:T(8,128)} %copy-done.39, f32[256,1024]{1,0:T(8,128)} %copy-done.41, bf16[960,640]{1,0:T(8,128)(2,1)} %pad_maximum_fusion.refs_4_, ...), custom_call_target="tpu_custom_call" | custom-call | flops 1 | bytes 1 | tf_op jit(solution)/shard_map/pallas_call | solution.py:750
  170.2 7.7 %shard_map.215 = (f32[240,640]{1,0:T(8,128)}, f32[240,640]{1,0:T(8,128)}, f32[240,640]{1,0:T(8,128)}, f32[240,640]{1,0:T(8,128)}, f32[240,640]{1,0:T(8,128)}, /*index=5*/f32[240,640]{1,0:T(8,128)}) custom-call(f32[256,1024]{1,0:T(8,128)} %copy-done.40, f32[256,1024]{1,0:T(8,128)} %copy-done.43, f32[256,1024]{1,0:T(8,128)} %collective-permute-done.19.refs_2_, ...), custom_call_target="tpu_custom_call" | custom-call | flops 1 | bytes 1 | tf_op jit(solution)/shard_map/pallas_call | solution.py:750
  177.9 2.7 collective-permute-done.23.b
  180.8 1.6 collective-permute-start.28
  182.4 4.3 %collective-permute-start.24 = (f32[240,640]{1,0:T(8,128)}, f32[240,640]{1,0:T(8,128)}, u32[]{:S(2)}, u32[]{:S(2)}) collective-permute-start(f32[240,640]{1,0:T(8,128)} %get-tuple-element.327.a), channel_id=1, source_target_pairs={{0,8},{1,9},{2,10},{3,11},{4,12},{5,13},{6,14},{7,15},{24,16},{25,... | collective-permute-start | bytes 1843208 | tf_op jit(solution)/shard_map/ppermute | solution.py:824
  189.8 1.9 stack.37.refs_0_
  191.7 12.6 %shard_map.217 = (f32[256,960]{1,0:T(8,128)}, bf16[256,960]{1,0:T(8,128)(2,1)}, bf16[5,256,128]{2,1,0:T(8,128)(2,1)}, f32[5,256,128]{2,1,0:T(8,128)}, f32[5,2,256,128]{3,2,1,0:T(8,128)}, /*index=5*/f32[1,960]{1,0:T(1,128)}) custom-call(s32[6]{0:T(128)} %stack.37.refs_0_, f32[128,1024]{1,0:T(8,128)} %copy-done.7, ...), custom_call_target="tpu_custom_call" | custom-call | flops 1 | bytes 1 | tf_op jit(solution)/shard_map/pallas_call | solution.py:750
  208.2 3.3 collective-permute-start.31
  212.3 20.4 %shard_map.220 = (bf16[256,960]{1,0:T(8,128)(2,1)}, bf16[5,256,320]{2,1,0:T(8,128)(2,1)}, bf16[5,256,320]{2,1,0:T(8,128)(2,1)}, f32[1,960]{1,0:T(1,128)}, f32[1,960]{1,0:T(1,128)}, /*index=5*/bf16[960,512]{1,0:T(8,128)(2,1)}) custom-call(s32[6]{0:T(128)} %stack.37.refs_0_, f32[128,1024]{1,0:T(8,128)} %copy-done.8, f32[128,1024]{1,0:T(8,128)} %copy-done.51, ...), custom_call_target="tpu_custom_call" | custom-call | flops 1 | bytes 1 | tf_op jit(solution)/shard_map/pallas_call | solution.py:750
  232.9 1.7 collective-permute-start.35
  234.6 2.1 collective-permute-start.33
  237.6 9.0 %shard_map.224 = (f32[72,1024]{1,0:T(8,128)}, f32[128,1024]{1,0:T(8,128)}, f32[128,1024]{1,0:T(8,128)}, f32[328,1024]{1,0:T(8,128)}) custom-call(s32[6]{0:T(128)} %stack.37.refs_0_, bf16[256,960]{1,0:T(8,128)(2,1)} %get-tuple-element.363.refs_1_, bf16[256,960]{1,0:T(8,128)(2,1)} %get-tuple-element.364.refs_2_, bf16[256,960]{1,0:T(8,128)(2,1)} %get-tuple-element.365.refs_3_, ...), custom_call_target="tpu_custom_call" | custom-call | flops 1 | bytes 1 | tf_op jit(solution)/shard_map/pallas_call | solution.py:750
  250.5 7.4 %collective-permute-start.38 = (f32[240,640]{1,0:T(8,128)S(1)}, f32[240,640]{1,0:T(8,128)}, u32[]{:S(2)}, u32[]{:S(2)}) collective-permute-start(f32[240,640]{1,0:T(8,128)S(1)} %copy-done.17), channel_id=1, source_target_pairs={{0,8},{1,9},{2,10},{3,11},{4,12},{5,13},{6,14},{7,15},{24,16},{25,... | collective-permute-start | bytes 1843208 | tf_op jit(solution)/shard_map/ppermute | solution.py:824
  259.6 4.7 %collective-permute-done.34.b = f32[240,640]{1,0:T(8,128)S(1)} collective-permute-done((f32[240,640]{1,0:T(8,128)S(1)}, f32[240,640]{1,0:T(8,128)S(1)}, u32[]{:S(2)}, u32[]{:S(2)}) %collective-permute-start.34) | collective-permute-done | bytes 614432 | tf_op jit(solution)/shard_map/ppermute | solution.py:824
  271.3 12.6 %collective-permute-done.40.b = f32[240,640]{1,0:T(8,128)} collective-permute-done((f32[240,640]{1,0:T(8,128)S(1)}, f32[240,640]{1,0:T(8,128)}, u32[]{:S(2)}, u32[]{:S(2)}) %collective-permute-start.40) | collective-permute-done | bytes 614432 | tf_op jit(solution)/shard_map/ppermute | solution.py:824
  287.6 1.7 shard_map.231
  293.0 4.0 collective-permute-done.36.b
  302.6 5.3 %collective-permute-start.50 = (f32[128,1024]{1,0:T(8,128)S(1)}, f32[128,1024]{1,0:T(8,128)S(1)}, u32[]{:S(2)}, u32[]{:S(2)}) collective-permute-start(f32[128,1024]{1,0:T(8,128)S(1)} %get-tuple-element.412.a), channel_id=1, source_target_pairs={{0,8},{1,9},{2,10},{3,11},{4,12},{5,13},{6,14},{7,15},{24,16},{25,... | collective-permute-start | bytes 1572872 | tf_op jit(solution)/shard_map/ppermute | solution.py:824
  312.2 6.6 %collective-permute-done.50.b = f32[128,1024]{1,0:T(8,128)S(1)} collective-permute-done((f32[128,1024]{1,0:T(8,128)S(1)}, f32[128,1024]{1,0:T(8,128)S(1)}, u32[]{:S(2)}, u32[]{:S(2)}) %collective-permute-start.50) | collective-permute-done | bytes 524320 | tf_op jit(solution)/shard_map/ppermute | solution.py:824
  318.9 5.2 %collective-permute-start.52 = (f32[128,1024]{1,0:T(8,128)S(1)}, f32[128,1024]{1,0:T(8,128)}, u32[]{:S(2)}, u32[]{:S(2)}) collective-permute-start(f32[128,1024]{1,0:T(8,128)S(1)} %get-tuple-element.415.a), channel_id=1, source_target_pairs={{0,8},{1,9},{2,10},{3,11},{4,12},{5,13},{6,14},{7,15},{24,16},{25,... | collective-permute-start | bytes 1572872 | tf_op jit(solution)/shard_map/ppermute | solution.py:824
  324.0 2.7 collective-permute-done.45.b
  329.2 4.4 %shard_map.242 = bf16[960,512]{1,0:T(8,128)(2,1)} custom-call(s32[6]{0:T(128)} %stack.37.refs_0_, f32[256,960]{1,0:T(8,128)} %get-tuple-element.265.refs_4_.refs_1_, f32[256,960]{1,0:T(8,128)} %get-tuple-element.276.refs_4_.refs_2_, f32[256,1024]{1,0:T(8,128)} %copy-done, f32[256,1024]{1,0:T(8,128)} %copy-done.45), custom_call_target="tpu_custom_call" | custom-call | flops 1 | bytes 1 | tf_op jit(solution)/shard_map/pallas_call | solution.py:750
  334.5 3.7 collective-permute-done.54.b
  343.8 5.7 %collective-permute-done.59.b = f32[72,1024]{1,0:T(8,128)S(1)} collective-permute-done((f32[72,1024]{1,0:T(8,128)S(1)}, f32[72,1024]{1,0:T(8,128)S(1)}, u32[]{:S(2)}, u32[]{:S(2)}) %collective-permute-start.59) | collective-permute-done | bytes 294944 | tf_op jit(solution)/shard_map/ppermute | solution.py:824
  351.7 4.5 %shard_map.249 = (f32[960,640]{1,0:T(8,128)}, f32[960,640]{1,0:T(8,128)}) custom-call(s32[6]{0:T(128)} %stack.37.refs_0_, f32[240,640]{1,0:T(8,128)} %copy-done.1, f32[240,640]{1,0:T(8,128)} %copy-done.2, f32[240,640]{1,0:T(8,128)} %copy-done.3, f32[240,640]{1,0:T(8,128)} %copy-done.4, f32[240,640]{1,0:T(8,128)} %copy-done.47, f32[240,640]{1,0:T(8,128)} %copy-done.48, ...), custom_call_target="tpu_custom_call" | custom-call | flops 1 | bytes 1 | tf_op jit(solution)/shard_map/pallas_call | solution.py:750
  359.0 8.1 %collective-permute-done.56.b = f32[128,1024]{1,0:T(8,128)S(1)} collective-permute-done((f32[128,1024]{1,0:T(8,128)S(1)}, f32[128,1024]{1,0:T(8,128)S(1)}, u32[]{:S(2)}, u32[]{:S(2)}) %collective-permute-start.56) | collective-permute-done | bytes 524320 | tf_op jit(solution)/shard_map/ppermute | solution.py:824
  367.2 6.8 %collective-permute-done.60.b = f32[128,1024]{1,0:T(8,128)} collective-permute-done((f32[128,1024]{1,0:T(8,128)S(1)}, f32[128,1024]{1,0:T(8,128)}, u32[]{:S(2)}, u32[]{:S(2)}) %collective-permute-start.60) | collective-permute-done | bytes 524320 | tf_op jit(solution)/shard_map/ppermute | solution.py:824
  375.1 3.5 shard_map.253
  381.4 6.9 %collective-permute-done.66.refs_6_ = f32[128,1024]{1,0:T(8,128)S(1)} collective-permute-done((f32[128,1024]{1,0:T(8,128)S(1)}, f32[128,1024]{1,0:T(8,128)S(1)}, u32[]{:S(2)}, u32[]{:S(2)}) %collective-permute-start.66) | collective-permute-done | bytes 524320 | tf_op jit(solution)/shard_map/ppermute | solution.py:824
  388.9 5.2 %collective-permute-done.62.refs_3_ = f32[128,1024]{1,0:T(8,128)S(1)} collective-permute-done((f32[128,1024]{1,0:T(8,128)S(1)}, f32[128,1024]{1,0:T(8,128)S(1)}, u32[]{:S(2)}, u32[]{:S(2)}) %collective-permute-start.62) | collective-permute-done | bytes 524320 | tf_op jit(solution)/shard_map/ppermute | solution.py:824
  394.1 5.6 %collective-permute-done.65.refs_4_ = f32[128,1024]{1,0:T(8,128)S(1)} collective-permute-done((f32[128,1024]{1,0:T(8,128)S(1)}, f32[128,1024]{1,0:T(8,128)S(1)}, u32[]{:S(2)}, u32[]{:S(2)}) %collective-permute-start.65) | collective-permute-done | bytes 524320 | tf_op jit(solution)/shard_map/ppermute | solution.py:824
  401.5 5.2 %shard_map.254 = (f32[2,320,960]{2,1,0:T(8,128)}, f32[2,192,960]{2,1,0:T(8,128)}) custom-call(s32[6]{0:T(128)} %stack.37.refs_0_, f32[128,1024]{1,0:T(8,128)} %copy-done.12, f32[128,1024]{1,0:T(8,128)} %copy-done.13, f32[128,1024]{1,0:T(8,128)} %copy-done.53, f32[128,1024]{1,0:T(8,128)} %copy-done.55, f32[128,1024]{1,0:T(8,128)} %copy-done.38, ...), custom_call_target="tpu_custom_call" | custom-call | flops 1 | bytes 1 | tf_op jit(solution)/shard_map/pallas_call | solution.py:750
  (311 shorter events, 86.9 us)
Async XLA Ops:
  22.7 21.1 %collective-permute-start.1 = (f32[128,1024]{1,0:T(8,128)S(1)}, f32[128,1024]{1,0:T(8,128)S(1)}, u32[]{:S(2)}, u32[]{:S(2)}) collective-permute-start(f32[128,1024]{1,0:T(8,128)S(1)} %shard_map.197.a), channel_id=1, source_target_pairs={{0,2},{1,3},{2,0},{3,1},{4,6},{5,7},{6,4},{7,5},{8,10},{9,11},{10,... | collective-permute-start | bytes 1572872 | tf_op jit(solution)/shard_map/ppermute | solution.py:824
  44.0 25.6 %collective-permute-start.5 = (f32[256,1024]{1,0:T(8,128)S(1)}, f32[256,1024]{1,0:T(8,128)S(1)}, u32[]{:S(2)}, u32[]{:S(2)}) collective-permute-start(f32[256,1024]{1,0:T(8,128)S(1)} %pad_convert_fusion), channel_id=1, source_target_pairs={{0,4},{1,5},{2,6},{3,7},{4,0},{5,1},{6,2},{7,3},{8,12},{9,13},{10,... | collective-permute-start | bytes 3145736 | tf_op jit(solution)/shard_map/ppermute | solution.py:824
  46.1 23.6 %collective-permute-start.4 = (f32[128,1024]{1,0:T(8,128)S(1)}, f32[128,1024]{1,0:T(8,128)S(1)}, u32[]{:S(2)}, u32[]{:S(2)}) collective-permute-start(f32[128,1024]{1,0:T(8,128)S(1)} %shard_map.199.a), channel_id=1, source_target_pairs={{0,2},{1,3},{2,0},{3,1},{4,6},{5,7},{6,4},{7,5},{8,10},{9,11},{10,... | collective-permute-start | bytes 1572872 | tf_op jit(solution)/shard_map/ppermute | solution.py:824
  70.2 25.1 %collective-permute-start.10 = (f32[256,1024]{1,0:T(8,128)S(1)}, f32[256,1024]{1,0:T(8,128)S(1)}, u32[]{:S(2)}, u32[]{:S(2)}) collective-permute-start(f32[256,1024]{1,0:T(8,128)S(1)} %copy-done.67), channel_id=1, source_target_pairs={{0,4},{1,5},{2,6},{3,7},{4,0},{5,1},{6,2},{7,3},{8,12},{9,13},{10,... | collective-permute-start | bytes 3145736 | tf_op jit(solution)/shard_map/ppermute | solution.py:824
  73.3 22.0 %collective-permute-start.9 = (f32[128,1024]{1,0:T(8,128)S(1)}, f32[128,1024]{1,0:T(8,128)S(1)}, u32[]{:S(2)}, u32[]{:S(2)}) collective-permute-start(f32[128,1024]{1,0:T(8,128)S(1)} %shard_map.202.a), channel_id=1, source_target_pairs={{0,2},{1,3},{2,0},{3,1},{4,6},{5,7},{6,4},{7,5},{8,10},{9,11},{10,... | collective-permute-start | bytes 1572872 | tf_op jit(solution)/shard_map/ppermute | solution.py:824
  97.5 19.4 %collective-permute-start.13 = (f32[128,1024]{1,0:T(8,128)S(1)}, f32[128,1024]{1,0:T(8,128)S(1)}, u32[]{:S(2)}, u32[]{:S(2)}) collective-permute-start(f32[128,1024]{1,0:T(8,128)S(1)} %shard_map.205.a), channel_id=1, source_target_pairs={{0,2},{1,3},{2,0},{3,1},{4,6},{5,7},{6,4},{7,5},{8,10},{9,11},{10,... | collective-permute-start | bytes 1572872 | tf_op jit(solution)/shard_map/ppermute | solution.py:824
  98.0 42.4 %collective-permute-start.15 = (f32[256,1024]{1,0:T(8,128)S(1)}, f32[256,1024]{1,0:T(8,128)S(1)}, u32[]{:S(2)}, u32[]{:S(2)}) collective-permute-start(f32[256,1024]{1,0:T(8,128)S(1)} %copy-done.68), channel_id=1, source_target_pairs={{0,4},{1,5},{2,6},{3,7},{4,0},{5,1},{6,2},{7,3},{8,12},{9,13},{10,... | collective-permute-start | bytes 3145736 | tf_op jit(solution)/shard_map/ppermute | solution.py:824
  140.4 16.0 %collective-permute-start.16 = (f32[256,1024]{1,0:T(8,128)S(1)}, f32[256,1024]{1,0:T(8,128)}, u32[]{:S(2)}, u32[]{:S(2)}) collective-permute-start(f32[256,1024]{1,0:T(8,128)S(1)} %collective-permute-done.15.refs_0_), channel_id=1, source_target_pairs={{0,1},{1,0},{2,3},{3,2},{4,5},{5,4},{6,7},{7,6},{8,9},{9,8},{10,11... | collective-permute-start | bytes 3145736 | tf_op jit(solution)/shard_map/ppermute | solution.py:824
  140.6 25.8 %collective-permute-start.19 = (f32[256,1024]{1,0:T(8,128)}, f32[256,1024]{1,0:T(8,128)}, u32[]{:S(2)}, u32[]{:S(2)}) collective-permute-start(f32[256,1024]{1,0:T(8,128)} %get-tuple-element.313), channel_id=1, source_target_pairs={{0,4},{1,5},{2,6},{3,7},{4,0},{5,1},{6,2},{7,3},{8,12},{9,13},{10,... | collective-permute-start | bytes 3145736 | tf_op jit(solution)/shard_map/ppermute | solution.py:824
  156.1 11.7 %collective-permute-start.21 = (f32[256,1024]{1,0:T(8,128)S(1)}, f32[256,1024]{1,0:T(8,128)S(1)}, u32[]{:S(2)}, u32[]{:S(2)}) collective-permute-start(f32[256,1024]{1,0:T(8,128)S(1)} %collective-permute-done.10.refs_0_), channel_id=1, source_target_pairs={{0,1},{1,0},{2,3},{3,2},{4,5},{5,4},{6,7},{7,6},{8,9},{9,8},{10,11... | collective-permute-start | bytes 3145736 | tf_op jit(solution)/shard_map/ppermute | solution.py:824
  166.3 14.3 %collective-permute-start.23 = (f32[128,1024]{1,0:T(8,128)S(1)}, f32[128,1024]{1,0:T(8,128)S(1)}, u32[]{:S(2)}, u32[]{:S(2)}) collective-permute-start(f32[128,1024]{1,0:T(8,128)S(1)} %shard_map.212.a), channel_id=1, source_target_pairs={{0,2},{1,3},{2,0},{3,1},{4,6},{5,7},{6,4},{7,5},{8,10},{9,11},{10,... | collective-permute-start | bytes 1572872 | tf_op jit(solution)/shard_map/ppermute | solution.py:824
  180.8 23.5 %collective-permute-start.28 = (f32[128,1024]{1,0:T(8,128)S(1)}, f32[128,1024]{1,0:T(8,128)}, u32[]{:S(2)}, u32[]{:S(2)}) collective-permute-start(f32[128,1024]{1,0:T(8,128)S(1)} %shard_map.213.a), channel_id=1, source_target_pairs={{0,2},{1,3},{2,0},{3,1},{4,6},{5,7},{6,4},{7,5},{8,10},{9,11},{10,... | collective-permute-start | bytes 1572872 | tf_op jit(solution)/shard_map/ppermute | solution.py:824
  182.4 23.7 %collective-permute-start.24 = (f32[240,640]{1,0:T(8,128)}, f32[240,640]{1,0:T(8,128)}, u32[]{:S(2)}, u32[]{:S(2)}) collective-permute-start(f32[240,640]{1,0:T(8,128)} %get-tuple-element.327.a), channel_id=1, source_target_pairs={{0,8},{1,9},{2,10},{3,11},{4,12},{5,13},{6,14},{7,15},{24,16},{25,... | collective-permute-start | bytes 1843208 | tf_op jit(solution)/shard_map/ppermute | solution.py:824
  186.7 50.7 %collective-permute-start.20 = (f32[256,1024]{1,0:T(8,128)}, f32[256,1024]{1,0:T(8,128)S(1)}, u32[]{:S(2)}, u32[]{:S(2)}) collective-permute-start(f32[256,1024]{1,0:T(8,128)} %get-tuple-element.318), channel_id=1, source_target_pairs={{0,1},{1,0},{2,3},{3,2},{4,5},{5,4},{6,7},{7,6},{8,9},{9,8},{10,11... | collective-permute-start | bytes 3145736 | tf_op jit(solution)/shard_map/ppermute | solution.py:824
  186.9 45.8 %collective-permute-start.27 = (f32[240,640]{1,0:T(8,128)S(1)}, f32[240,640]{1,0:T(8,128)S(1)}, u32[]{:S(2)}, u32[]{:S(2)}) collective-permute-start(f32[240,640]{1,0:T(8,128)S(1)} %copy-done.21), channel_id=1, source_target_pairs={{0,8},{1,9},{2,10},{3,11},{4,12},{5,13},{6,14},{7,15},{24,16},{25,... | collective-permute-start | bytes 1843208 | tf_op jit(solution)/shard_map/ppermute | solution.py:824
  207.5 29.9 %collective-permute-start.26 = (f32[240,640]{1,0:T(8,128)S(1)}, f32[240,640]{1,0:T(8,128)S(1)}, u32[]{:S(2)}, u32[]{:S(2)}) collective-permute-start(f32[240,640]{1,0:T(8,128)S(1)} %shard_map.218.a), channel_id=1, source_target_pairs={{8,16},{9,17},{10,18},{11,19},{12,20},{13,21},{14,22},{15,23},{16,... | collective-permute-start | bytes 1843208 | tf_op jit(solution)/shard_map/ppermute | solution.py:824
  208.2 40.7 %collective-permute-start.31 = (f32[240,640]{1,0:T(8,128)S(1)}, f32[240,640]{1,0:T(8,128)S(1)}, u32[]{:S(2)}, u32[]{:S(2)}) collective-permute-start(f32[240,640]{1,0:T(8,128)S(1)} %copy-done.20), channel_id=1, source_target_pairs={{0,8},{1,9},{2,10},{3,11},{4,12},{5,13},{6,14},{7,15},{24,16},{25,... | collective-permute-start | bytes 1843208 | tf_op jit(solution)/shard_map/ppermute | solution.py:824
  232.9 17.6 %collective-permute-start.35 = (f32[240,640]{1,0:T(8,128)S(1)}, f32[240,640]{1,0:T(8,128)}, u32[]{:S(2)}, u32[]{:S(2)}) collective-permute-start(f32[240,640]{1,0:T(8,128)S(1)} %shard_map.221.a), channel_id=1, source_target_pairs={{8,16},{9,17},{10,18},{11,19},{12,20},{13,21},{14,22},{15,23},{16,... | collective-permute-start | bytes 1843208 | tf_op jit(solution)/shard_map/ppermute | solution.py:824
  234.6 23.3 %collective-permute-start.33 = (f32[240,640]{1,0:T(8,128)S(1)}, f32[240,640]{1,0:T(8,128)S(1)}, u32[]{:S(2)}, u32[]{:S(2)}) collective-permute-start(f32[240,640]{1,0:T(8,128)S(1)} %copy-done.18), channel_id=1, source_target_pairs={{0,8},{1,9},{2,10},{3,11},{4,12},{5,13},{6,14},{7,15},{24,16},{25,... | collective-permute-start | bytes 1843208 | tf_op jit(solution)/shard_map/ppermute | solution.py:824
  246.6 38.7 %collective-permute-start.39 = (f32[328,1024]{1,0:T(8,128)}, f32[328,1024]{1,0:T(8,128)}, u32[]{:S(2)}, u32[]{:S(2)}) collective-permute-start(f32[328,1024]{1,0:T(8,128)} %get-tuple-element.390), channel_id=1, source_target_pairs={{0,4},{1,5},{2,6},{3,7},{4,0},{5,1},{6,2},{7,3},{8,12},{9,13},{10,... | collective-permute-start | bytes 4030472 | tf_op jit(solution)/shard_map/ppermute | solution.py:824
  247.6 16.7 %collective-permute-start.34 = (f32[240,640]{1,0:T(8,128)S(1)}, f32[240,640]{1,0:T(8,128)S(1)}, u32[]{:S(2)}, u32[]{:S(2)}) collective-permute-start(f32[240,640]{1,0:T(8,128)S(1)} %shard_map.222.a), channel_id=1, source_target_pairs={{8,0},{9,1},{10,2},{11,3},{12,4},{13,5},{14,6},{15,7},{16,24},{17,... | collective-permute-start | bytes 1843208 | tf_op jit(solution)/shard_map/ppermute | solution.py:824
  249.0 19.0 %collective-permute-start.32 = (f32[240,640]{1,0:T(8,128)S(1)}, f32[240,640]{1,0:T(8,128)}, u32[]{:S(2)}, u32[]{:S(2)}) collective-permute-start(f32[240,640]{1,0:T(8,128)S(1)} %shard_map.225.a), channel_id=1, source_target_pairs={{8,16},{9,17},{10,18},{11,19},{12,20},{13,21},{14,22},{15,23},{16,... | collective-permute-start | bytes 1843208 | tf_op jit(solution)/shard_map/ppermute | solution.py:824
  250.5 19.5 %collective-permute-start.38 = (f32[240,640]{1,0:T(8,128)S(1)}, f32[240,640]{1,0:T(8,128)}, u32[]{:S(2)}, u32[]{:S(2)}) collective-permute-start(f32[240,640]{1,0:T(8,128)S(1)} %copy-done.17), channel_id=1, source_target_pairs={{0,8},{1,9},{2,10},{3,11},{4,12},{5,13},{6,14},{7,15},{24,16},{25,... | collective-permute-start | bytes 1843208 | tf_op jit(solution)/shard_map/ppermute | solution.py:824
  257.9 33.8 %collective-permute-start.30 = (f32[256,1024]{1,0:T(8,128)S(1)}, f32[256,1024]{1,0:T(8,128)}, u32[]{:S(2)}, u32[]{:S(2)}) collective-permute-start(f32[256,1024]{1,0:T(8,128)S(1)} %shard_map.223.a), channel_id=1, source_target_pairs={{0,2},{1,3},{2,0},{3,1},{4,6},{5,7},{6,4},{7,5},{8,10},{9,11},{10,... | collective-permute-start | bytes 3145736 | tf_op jit(solution)/shard_map/ppermute | solution.py:824
  265.1 18.8 %collective-permute-start.40 = (f32[240,640]{1,0:T(8,128)S(1)}, f32[240,640]{1,0:T(8,128)}, u32[]{:S(2)}, u32[]{:S(2)}) collective-permute-start(f32[240,640]{1,0:T(8,128)S(1)} %shard_map.226.a), channel_id=1, source_target_pairs={{8,0},{9,1},{10,2},{11,3},{12,4},{13,5},{14,6},{15,7},{16,24},{17,... | collective-permute-start | bytes 1843208 | tf_op jit(solution)/shard_map/ppermute | solution.py:824
  268.0 22.7 %collective-permute-start.37 = (f32[240,640]{1,0:T(8,128)S(1)}, f32[240,640]{1,0:T(8,128)S(1)}, u32[]{:S(2)}, u32[]{:S(2)}) collective-permute-start(f32[240,640]{1,0:T(8,128)S(1)} %shard_map.228.a), channel_id=1, source_target_pairs={{8,16},{9,17},{10,18},{11,19},{12,20},{13,21},{14,22},{15,23},{16,... | collective-permute-start | bytes 1843208 | tf_op jit(solution)/shard_map/ppermute | solution.py:824
  270.0 27.0 %collective-permute-start.36 = (f32[240,640]{1,0:T(8,128)S(1)}, f32[240,640]{1,0:T(8,128)S(1)}, u32[]{:S(2)}, u32[]{:S(2)}) collective-permute-start(f32[240,640]{1,0:T(8,128)S(1)} %shard_map.229.a), channel_id=1, source_target_pairs={{8,0},{9,1},{10,2},{11,3},{12,4},{13,5},{14,6},{15,7},{16,24},{17,... | collective-permute-start | bytes 1843208 | tf_op jit(solution)/shard_map/ppermute | solution.py:824
  283.9 16.2 %collective-permute-start.44 = (f32[240,640]{1,0:T(8,128)S(1)}, f32[240,640]{1,0:T(8,128)S(1)}, u32[]{:S(2)}, u32[]{:S(2)}) collective-permute-start(f32[240,640]{1,0:T(8,128)S(1)} %copy-done.16), channel_id=1, source_target_pairs={{0,8},{1,9},{2,10},{3,11},{4,12},{5,13},{6,14},{7,15},{24,16},{25,... | collective-permute-start | bytes 1843208 | tf_op jit(solution)/shard_map/ppermute | solution.py:824
  285.3 15.6 %collective-permute-start.48 = (f32[240,640]{1,0:T(8,128)S(1)}, f32[240,640]{1,0:T(8,128)S(1)}, u32[]{:S(2)}, u32[]{:S(2)}) collective-permute-start(f32[240,640]{1,0:T(8,128)S(1)} %shard_map.227.refs_1_), channel_id=1, source_target_pairs={{0,4},{1,5},{2,6},{3,7},{4,0},{5,1},{6,2},{7,3},{8,12},{9,13},{10,... | collective-permute-start | bytes 1843208 | tf_op jit(solution)/shard_map/ppermute | solution.py:824
  290.7 12.0 %collective-permute-start.43 = (f32[240,640]{1,0:T(8,128)S(1)}, f32[240,640]{1,0:T(8,128)S(1)}, u32[]{:S(2)}, u32[]{:S(2)}) collective-permute-start(f32[240,640]{1,0:T(8,128)S(1)} %shard_map.232.a), channel_id=1, source_target_pairs={{8,16},{9,17},{10,18},{11,19},{12,20},{13,21},{14,22},{15,23},{16,... | collective-permute-start | bytes 1843208 | tf_op jit(solution)/shard_map/ppermute | solution.py:824
  291.7 16.4 %collective-permute-start.49 = (f32[240,640]{1,0:T(8,128)S(1)}, f32[240,640]{1,0:T(8,128)S(1)}, u32[]{:S(2)}, u32[]{:S(2)}) collective-permute-start(f32[240,640]{1,0:T(8,128)S(1)} %shard_map.233.a), channel_id=1, source_target_pairs={{8,0},{9,1},{10,2},{11,3},{12,4},{13,5},{14,6},{15,7},{16,24},{17,... | collective-permute-start | bytes 1843208 | tf_op jit(solution)/shard_map/ppermute | solution.py:824
  302.6 24.8 %collective-permute-start.41 = (f32[256,1024]{1,0:T(8,128)S(1)}, f32[256,1024]{1,0:T(8,128)S(1)}, u32[]{:S(2)}, u32[]{:S(2)}) collective-permute-start(f32[256,1024]{1,0:T(8,128)S(1)} %shard_map.235.refs_3_), channel_id=1, source_target_pairs={{0,1},{1,0},{2,3},{3,2},{4,5},{5,4},{6,7},{7,6},{8,9},{9,8},{10,11... | collective-permute-start | bytes 3145736 | tf_op jit(solution)/shard_map/ppermute | solution.py:824
  302.6 16.2 %collective-permute-start.50 = (f32[128,1024]{1,0:T(8,128)S(1)}, f32[128,1024]{1,0:T(8,128)S(1)}, u32[]{:S(2)}, u32[]{:S(2)}) collective-permute-start(f32[128,1024]{1,0:T(8,128)S(1)} %get-tuple-element.412.a), channel_id=1, source_target_pairs={{0,8},{1,9},{2,10},{3,11},{4,12},{5,13},{6,14},{7,15},{24,16},{25,... | collective-permute-start | bytes 1572872 | tf_op jit(solution)/shard_map/ppermute | solution.py:824
  308.1 18.7 %collective-permute-start.45 = (f32[240,640]{1,0:T(8,128)S(1)}, f32[240,640]{1,0:T(8,128)S(1)}, u32[]{:S(2)}, u32[]{:S(2)}) collective-permute-start(f32[240,640]{1,0:T(8,128)S(1)} %shard_map.237.a), channel_id=1, source_target_pairs={{8,0},{9,1},{10,2},{11,3},{12,4},{13,5},{14,6},{15,7},{16,24},{17,... | collective-permute-start | bytes 1843208 | tf_op jit(solution)/shard_map/ppermute | solution.py:824
  309.6 28.6 %collective-permute-start.54 = (f32[240,640]{1,0:T(8,128)S(1)}, f32[240,640]{1,0:T(8,128)S(1)}, u32[]{:S(2)}, u32[]{:S(2)}) collective-permute-start(f32[240,640]{1,0:T(8,128)S(1)} %shard_map.240.a), channel_id=1, source_target_pairs={{8,0},{9,1},{10,2},{11,3},{12,4},{13,5},{14,6},{15,7},{16,24},{17,... | collective-permute-start | bytes 1843208 | tf_op jit(solution)/shard_map/ppermute | solution.py:824
  311.1 27.2 %collective-permute-start.53 = (f32[240,640]{1,0:T(8,128)S(1)}, f32[240,640]{1,0:T(8,128)}, u32[]{:S(2)}, u32[]{:S(2)}) collective-permute-start(f32[240,640]{1,0:T(8,128)S(1)} %shard_map.234.refs_3_), channel_id=1, source_target_pairs={{0,4},{1,5},{2,6},{3,7},{4,0},{5,1},{6,2},{7,3},{8,12},{9,13},{10,... | collective-permute-start | bytes 1843208 | tf_op jit(solution)/shard_map/ppermute | solution.py:824
  318.9 19.4 %collective-permute-start.52 = (f32[128,1024]{1,0:T(8,128)S(1)}, f32[128,1024]{1,0:T(8,128)}, u32[]{:S(2)}, u32[]{:S(2)}) collective-permute-start(f32[128,1024]{1,0:T(8,128)S(1)} %get-tuple-element.415.a), channel_id=1, source_target_pairs={{0,8},{1,9},{2,10},{3,11},{4,12},{5,13},{6,14},{7,15},{24,16},{25,... | collective-permute-start | bytes 1572872 | tf_op jit(solution)/shard_map/ppermute | solution.py:824
  328.4 22.4 %collective-permute-start.58 = (f32[240,640]{1,0:T(8,128)S(1)}, f32[240,640]{1,0:T(8,128)S(1)}, u32[]{:S(2)}, u32[]{:S(2)}) collective-permute-start(f32[240,640]{1,0:T(8,128)S(1)} %shard_map.238.refs_4_), channel_id=1, source_target_pairs={{0,4},{1,5},{2,6},{3,7},{4,0},{5,1},{6,2},{7,3},{8,12},{9,13},{10,... | collective-permute-start | bytes 1843208 | tf_op jit(solution)/shard_map/ppermute | solution.py:824
  339.6 16.6 %collective-permute-start.57 = (f32[128,1024]{1,0:T(8,128)S(1)}, f32[128,1024]{1,0:T(8,128)S(1)}, u32[]{:S(2)}, u32[]{:S(2)}) collective-permute-start(f32[128,1024]{1,0:T(8,128)S(1)} %shard_map.246.a), channel_id=1, source_target_pairs={{8,16},{9,17},{10,18},{11,19},{12,20},{13,21},{14,22},{15,23},{16,... | collective-permute-start | bytes 1572872 | tf_op jit(solution)/shard_map/ppermute | solution.py:824
  341.6 25.6 %collective-permute-start.61 = (f32[240,640]{1,0:T(8,128)S(1)}, f32[240,640]{1,0:T(8,128)}, u32[]{:S(2)}, u32[]{:S(2)}) collective-permute-start(f32[240,640]{1,0:T(8,128)S(1)} %shard_map.241.refs_1_), channel_id=1, source_target_pairs={{0,4},{1,5},{2,6},{3,7},{4,0},{5,1},{6,2},{7,3},{8,12},{9,13},{10,... | collective-permute-start | bytes 1843208 | tf_op jit(solution)/shard_map/ppermute | solution.py:824
  342.8 32.3 %collective-permute-start.64 = (f32[240,640]{1,0:T(8,128)S(1)}, f32[240,640]{1,0:T(8,128)}, u32[]{:S(2)}, u32[]{:S(2)}) collective-permute-start(f32[240,640]{1,0:T(8,128)S(1)} %shard_map.245.refs_2_), channel_id=1, source_target_pairs={{0,4},{1,5},{2,6},{3,7},{4,0},{5,1},{6,2},{7,3},{8,12},{9,13},{10,... | collective-permute-start | bytes 1843208 | tf_op jit(solution)/shard_map/ppermute | solution.py:824
  349.5 17.7 %collective-permute-start.56 = (f32[128,1024]{1,0:T(8,128)S(1)}, f32[128,1024]{1,0:T(8,128)S(1)}, u32[]{:S(2)}, u32[]{:S(2)}) collective-permute-start(f32[128,1024]{1,0:T(8,128)S(1)} %shard_map.247.a), channel_id=1, source_target_pairs={{8,0},{9,1},{10,2},{11,3},{12,4},{13,5},{14,6},{15,7},{16,24},{17,... | collective-permute-start | bytes 1572872 | tf_op jit(solution)/shard_map/ppermute | solution.py:824
  356.2 17.8 %collective-permute-start.60 = (f32[128,1024]{1,0:T(8,128)S(1)}, f32[128,1024]{1,0:T(8,128)}, u32[]{:S(2)}, u32[]{:S(2)}) collective-permute-start(f32[128,1024]{1,0:T(8,128)S(1)} %shard_map.250.a), channel_id=1, source_target_pairs={{8,0},{9,1},{10,2},{11,3},{12,4},{13,5},{14,6},{15,7},{16,24},{17,... | collective-permute-start | bytes 1572872 | tf_op jit(solution)/shard_map/ppermute | solution.py:824
  357.5 21.1 %collective-permute-start.63 = (f32[72,1024]{1,0:T(8,128)S(1)}, f32[72,1024]{1,0:T(8,128)S(1)}, u32[]{:S(2)}, u32[]{:S(2)}) collective-permute-start(f32[72,1024]{1,0:T(8,128)S(1)} %shard_map.248), channel_id=1, source_target_pairs={{0,4},{1,5},{2,6},{3,7},{4,0},{5,1},{6,2},{7,3},{8,12},{9,13},{10,... | collective-permute-start | bytes 884744 | tf_op jit(solution)/shard_map/ppermute | solution.py:824
  379.4 14.7 %collective-permute-start.62 = (f32[128,1024]{1,0:T(8,128)S(1)}, f32[128,1024]{1,0:T(8,128)S(1)}, u32[]{:S(2)}, u32[]{:S(2)}) collective-permute-start(f32[128,1024]{1,0:T(8,128)S(1)} %shard_map.251.refs_1_), channel_id=1, source_target_pairs={{0,4},{1,5},{2,6},{3,7},{4,0},{5,1},{6,2},{7,3},{8,12},{9,13},{10,... | collective-permute-start | bytes 1572872 | tf_op jit(solution)/shard_map/ppermute | solution.py:824
  380.6 19.2 %collective-permute-start.65 = (f32[128,1024]{1,0:T(8,128)S(1)}, f32[128,1024]{1,0:T(8,128)S(1)}, u32[]{:S(2)}, u32[]{:S(2)}) collective-permute-start(f32[128,1024]{1,0:T(8,128)S(1)} %shard_map.252.refs_2_), channel_id=1, source_target_pairs={{0,4},{1,5},{2,6},{3,7},{4,0},{5,1},{6,2},{7,3},{8,12},{9,13},{10,... | collective-permute-start | bytes 1572872 | tf_op jit(solution)/shard_map/ppermute | solution.py:824
  381.4 18.3 %collective-permute-start.67 = (f32[128,1024]{1,0:T(8,128)S(1)}, f32[128,1024]{1,0:T(8,128)S(1)}, u32[]{:S(2)}, u32[]{:S(2)}) collective-permute-start(f32[128,1024]{1,0:T(8,128)S(1)} %slice.25.refs_5_), channel_id=1, source_target_pairs={{0,1},{1,0},{2,3},{3,2},{4,5},{5,4},{6,7},{7,6},{8,9},{9,8},{10,11... | collective-permute-start | bytes 1572872 | tf_op jit(solution)/shard_map/ppermute | solution.py:824
  388.3 11.5 %collective-permute-start.68 = (f32[128,1024]{1,0:T(8,128)S(1)}, f32[128,1024]{1,0:T(8,128)S(1)}, u32[]{:S(2)}, u32[]{:S(2)}) collective-permute-start(f32[128,1024]{1,0:T(8,128)S(1)} %collective-permute-done.66.refs_6_), channel_id=1, source_target_pairs={{0,1},{1,0},{2,3},{3,2},{4,5},{5,4},{6,7},{7,6},{8,9},{9,8},{10,11... | collective-permute-start | bytes 1572872 | tf_op jit(solution)/shard_map/ppermute | solution.py:824
  (90 other events, 654.7 us)

commit v4 on v3

--- a/solution.py
+++ b/solution.py
@@ -122,14 +122,16 @@
 
 
 class Late:
-    def __init__(self, source, buffer, sems, at, grouped):
+    def __init__(self, source, buffer, sems, at, grouped, pick=None):
+        self.pick = pick
         self.source, self.buffer, self.sems, self.at, self.grouped = source, buffer, sems, at, grouped
         self.waited = False
 
     def copy(self, g=None):
         if g is None:
             return pltpu.make_async_copy(self.source, self.buffer, self.sems.at[self.at])
-        return pltpu.make_async_copy(self.source.at[g], self.buffer.at[g], self.sems.at[self.at + g])
+        source = g if self.pick is None else self.pick[2 + g]
+        return pltpu.make_async_copy(self.source.at[source], self.buffer.at[g], self.sems.at[self.at + g])
 
     def start(self):
         self.copy().start()
@@ -321,11 +323,11 @@
     dg2_ref[...] = dg2
 
 
-def bwd_block(g, r0, base, da, qk_ref, o_ref, lse_ref, ktf, vtf, wout, seqr, valr, dkv):
+def bwd_block(g, r0, base, do, qk_ref, o_ref, lse_ref, ktf, vtf, seqr, valr, dkv):
     low, lane = low_half(RB), lane_iota(RB)
     nk = base + r0 + RB
     rows = slice(r0, r0 + RB)
-    do = dot_nt(da[rows], wout[g])
+    do = do[rows]
     dox = do[:, :128].astype(BF16)
     doy = jnp.concatenate([do[:, 128:192], jnp.zeros((RB, 64), F32)], axis=1).astype(BF16)
     px = dox.astype(F32) * o_ref[g, rows, :128].astype(F32)
@@ -379,11 +381,11 @@
 
     def group(g, carry):
         ready_group(g, *waits)
-        da = da_ref[...]
+        do = dot_nt(da_ref[...], wout[g])
         for r0 in range(0, t, RB):
             rows = slice(r0, r0 + RB)
-            dqx, dqy = bwd_block(g, r0, 0, da, qk_ref, o_ref, lse_ref, lambda n: kt_ref[g, :n, :],
-                                 lambda n: vt_ref[g, :n, :], wout, seqr, valr, dkv_ref.at[g])
+            dqx, dqy = bwd_block(g, r0, 0, do, qk_ref, o_ref, lse_ref, lambda n: kt_ref[g, :n, :],
+                                 lambda n: vt_ref[g, :n, :], seqr, valr, dkv_ref.at[g])
             dqx_ref[g, rows, :] = rope128(dqx, cs_ref[rows, :], -sn_ref[rows, :]).astype(BF16)
             dqy_ref[g, rows, :] = dqy
         return carry
@@ -412,7 +414,7 @@
 
     def group(g, carry):
         ready_group(g, *waits)
-        da = da_ref[...]
+        do = dot_nt(da_ref[...], wout[g])
         ktf[:t, :] = kt_old[g]
         ktf[t:, :] = kt_ref[g]
         vtf[:t, :] = vt_old[g]
@@ -421,8 +423,8 @@
         dkv[:, t:, :] = jnp.zeros((2, t, 128), F32)
         for r0 in range(0, t, RB):
             rows = slice(r0, r0 + RB)
-            dqx, dqy = bwd_block(g, r0, t, da, qk_ref, o_ref, lse_ref, lambda n: ktf[:n, :], lambda n: vtf[:n, :],
-                                 wout, seqr, valr, dkv)
+            dqx, dqy = bwd_block(g, r0, t, do, qk_ref, o_ref, lse_ref, lambda n: ktf[:n, :], lambda n: vtf[:n, :],
+                                 seqr, valr, dkv)
             full = slice(t + r0, t + r0 + RB)
             dpb_ref[g, rows, :128] = rope128(dqx, cs_ref[full, :], -sn_ref[full, :]).astype(BF16)
             dqy_ref[rows, :] = dqy
@@ -436,8 +438,9 @@
             dy = jnp.where(low, dqy, dk)
             ref[g, :, 128:256] = rope128(dy, cs_ref[rows, :], -sn_ref[rows, :]).astype(BF16)
             ref[g, :, 256:320] = dv[:, :64].astype(BF16)
-        acca[...] += dot(dpa_ref[g], win[g])
-        accb[...] += dot(dpb_ref[g], win[g])
+        both = dot(jnp.concatenate([dpa_ref[g], dpb_ref[g]], axis=0), win[g])
+        acca[...] += both[:t]
+        accb[...] += both[t:]
         return carry
 
     lax.fori_loop(0, groups, group, 0)
@@ -496,23 +499,28 @@
         put(1, r, sum((dot_tn(a[:, r : r + 320], b[...]) for a, b in zip(df, hidh)), base(1, r)))
 
 
-def peer_acts(n2, df, wgu, wdh, du, hd, rows):
-    gu = dot(n2, wgu[...])
-    dh = dot(df, wdh[...])
-    ga, ua, tile = gu[:, :256], gu[:, 256:512], gu[:, 512:]
-    turned = pltpu.roll(tile, 64, 1)
-    sa, sb = jax.nn.sigmoid(ga), jax.nn.sigmoid(tile)
+def peer_acts(xi, n2, df, wg, wu, wdt, du, hd, rows):
+    half = pl.ds(pl.multiple_of(xi * 256, 128), 256)
+    last = slice(512, 640)
+
+    def own_half(v):
+        return jnp.where(xi == 0, v, pltpu.roll(v, 64, 1))
+
+    ga, gb = dot(n2, wg[:, half]), own_half(dot(n2, wg[:, last]))
+    ua, ub = dot(n2, wu[:, half]), own_half(dot(n2, wu[:, last]))
+    dha, dhb = dot(df, wdt[:, half]), own_half(dot(df, wdt[:, last]))
+    sa, sb = jax.nn.sigmoid(ga), jax.nn.sigmoid(gb)
     low = low_half(n2.shape[0])
     hd[rows, :256] = (ga * sa * ua).astype(BF16)
-    hd[rows, 256:] = jnp.where(low, tile * sb * turned, 0.0).astype(BF16)
-    dga, dua = ffn_back(dh[:, :256], ga, ua, sa)
-    dgb, dub = ffn_back(dh[:, 256:], tile, turned, sb)
+    hd[rows, 256:] = jnp.where(low, gb * sb * ub, 0.0).astype(BF16)
+    dga, dua = ffn_back(dha, ga, ua, sa)
+    dgb, dub = ffn_back(dhb, gb, ub, sb)
     du[rows, :256] = dga.astype(BF16)
     du[rows, 256:512] = dua.astype(BF16)
     du[rows, 512:] = jnp.where(low, dgb, pltpu.roll(dub, 64, 1)).astype(BF16)
 
 
-def peer_grads(n2p, dfp, wgu, wdh, scratch, base, put):
+def peer_grads(xi, n2p, dfp, weights, scratch, base, put):
     n2, df, du, hd = scratch
     d = n2.shape[1]
     n = n2p[0].shape[0]
@@ -522,7 +530,7 @@
         df[rows, :] = dfp[i][:, :d].astype(BF16)
         for r in range(i * n, i * n + n, 256):
             part = slice(r, r + 256)
-            peer_acts(n2[part, :], df[part, :], wgu, wdh, du, hd, part)
+            peer_acts(xi, n2[part, :], df[part, :], *weights, du, hd, part)
     own_grads([n2], [du], [hd], [df], base, put)
 
 
@@ -538,8 +546,9 @@
 
 
 def both_grads_kernel(count, *refs):
+    idx, refs = refs[0], refs[1:]
     n2p, dfp = refs[:count], refs[count : 2 * count]
-    wgu, wdh, *rest = refs[2 * count :]
+    wg, wu, wdt, *rest = refs[2 * count :]
     n2, duh, hidh, df = (rest[2 * k : 2 * k + 2] for k in range(4))
     old, outs, scratch = rest[8:10], rest[10:12], rest[12:]
 
@@ -553,20 +562,21 @@
     old = ready(*old)
     own_grads(n2, duh, hidh, df, lambda k, r: old[k][r : r + 320, :], put)
     n2p, dfp = [ready(r) for r in n2p], [ready(r) for r in dfp]
-    wgu, wdh = ready(wgu, wdh)
-    peer_grads(n2p, dfp, wgu, wdh, scratch, lambda k, r: outs[k][r : r + 320, :], put_last)
+    weights = ready(wg, wu, wdt)
+    peer_grads(idx[0], n2p, dfp, weights, scratch, lambda k, r: outs[k][r : r + 320, :], put_last)
 
 
 def last_grads_kernel(count, n_chunks, *refs):
+    idx, refs = refs[0], refs[1:]
     n2p, dfp = refs[:count], refs[count : 2 * count]
-    wgu, wdh, *rest = refs[2 * count :]
+    wg, wu, wdt, *rest = refs[2 * count :]
     old, chunks, scratch = rest[:2], rest[2 : 2 + n_chunks], rest[2 + n_chunks : 6 + n_chunks]
     gu, dn = rest[6 + n_chunks :]
 
     def put(k, r, v):
         (gu, dn)[k][r : r + 320, :] = v
 
-    peer_grads(n2p, dfp, wgu, wdh, scratch, lambda k, r: ready(old[k])[r : r + 320, :], put)
+    peer_grads(idx[0], n2p, dfp, (wg, wu, wdt), scratch, lambda k, r: ready(old[k])[r : r + 320, :], put)
     at = 0
     half = dn.shape[0] // 2
     for out in chunks:
@@ -613,19 +623,22 @@
 
 def attn_grad_kernel(idx, *refs):
     n1, dp, o, da = (refs[4 * k : 4 * k + 4] for k in range(4))
+    da = [ready(v) for v in da]
     gains, keep2, keep0, keep1, send, whole, extra = refs[16:]
 
     def grads(g, out, at):
-        out[at : at + 320, :] = sum(dot_tn(p[g], n[...]) for p, n in zip(dp, n1))
-        out[at + 320 : at + 512, :] = sum(dot_tn(v[g, :, :192], a[...]) for v, a in zip(o, da))
-
-    grads(idx[2], whole, 0)
+        ready_group(g, *dp)
+        out[at : at + 320, :] = sum(dot_tn(p[g], n[...]) for p, n in zip(buffers(*dp), n1))
+        ready_group(g, *o)
+        out[at + 320 : at + 512, :] = sum(dot_tn(v[g, :, :192], a[...]) for v, a in zip(buffers(*o), da))
+
+    grads(0, whole, 0)
     half = whole.shape[0] // 2
     lead = send.shape[0] - half
-    for k, ref in enumerate((keep0, keep1)):
-        put_wide(ref, whole[pl.ds(pl.multiple_of(idx[0] * half + k * (half // 2), 8), half // 2), :])
+    for at, ref in ((0, keep0), (keep0.shape[0], keep1)):
+        put_wide(ref, whole[pl.ds(pl.multiple_of(idx[0] * half + at, 8), ref.shape[0]), :])
     put_wide(send.at[lead:, :], half_rows(whole, 1 - idx[0], half))
-    grads(idx[3], whole, 0)
+    grads(1, whole, 0)
     rows_in, rows_out = 320 // idx_parts(extra), 192 // idx_parts(extra)
     extra[:rows_in, :] = whole[pl.ds(pl.multiple_of(idx[4] * rows_in, 8), rows_in), :]
     extra[rows_in : rows_in + rows_out, :] = whole[pl.ds(pl.multiple_of(320 + idx[4] * rows_out, 8), rows_out), :]
@@ -654,23 +667,30 @@
 def attn_finish_kernel(parts, idx, a0, a1, b0, b1, *rest):
     slot1, gin, gout = rest[:-2], *rest[-2:]
     d = gin.shape[2]
-    for xi in range(2):
-        @pl.when(idx[0] == xi)
-        def _():
-            p0, p1, q0, q1 = (a0, a1, b0, b1) if xi == 0 else (b0, b1, a0, a1)
-            gin[0, :128, :] = p0[:, :d]
-            gin[0, 128:256, :] = p1[:, :d]
-            gin[0, 256:, :] = q0[:64, :d]
-            gout[0, :64, :] = q0[64:, :d]
-            gout[0, 64:, :] = q1[:, :d]
     mine = idx[5].astype(F32)
     rows_in, rows_out = 320 // parts, 192 // parts
     for k, quarter in enumerate(slot1):
+        quarter = ready(quarter)
         m = (idx[4] // 2 * (1 - k % 2) + (1 - idx[4] // 2) * (k % 2)) * 2 + (
             idx[4] % 2 * (1 - k // 2) + (1 - idx[4] % 2) * (k // 2))
         gin[1, pl.ds(pl.multiple_of(m * rows_in, 8), rows_in), :] = quarter[:rows_in, :d] * mine
         gout[1, pl.ds(pl.multiple_of(m * rows_out, 8), rows_out), :] = (
             quarter[rows_in : rows_in + rows_out, :d] * mine)
+    flush(gin, slice(1, 2))
+    flush(gout, slice(1, 2))
+    a0, a1, b0, b1 = ready(a0, a1, b0, b1)
+    for xi in range(2):
+        @pl.when(idx[0] == xi)
+        def _():
+            p0, p1, q0, q1 = (a0, a1, b0, b1) if xi == 0 else (b0, b1, a0, a1)
+            n = p0.shape[0]
+            gin[0, :n, :] = p0[:, :d]
+            gin[0, n:256, :] = p1[:, :d]
+            gin[0, 256:, :] = q0[:64, :d]
+            gout[0, : n - 64, :] = q0[64:, :d]
+            gout[0, n - 64 :, :] = q1[:, :d]
+    flush(gin, slice(0, 1))
+    flush(gout, slice(0, 1))
 
 
 def idx_parts(extra):
@@ -693,7 +713,7 @@
     return math.prod(a.shape) * jnp.dtype(a.dtype).itemsize
 
 
-def call(kernel, outs, ins, scratch=(), smem=0, flops=0, late=(), grouped=(), first=()):
+def call(kernel, outs, ins, scratch=(), smem=0, flops=0, late=(), grouped=(), first=(), picked=()):
     n_in, n_out = len(ins), len(outs)
     big_in = [i for i in range(smem, n_in) if size(ins[i]) >= BIG]
     big_out = [i for i in range(n_out) if size(outs[i]) >= BIG]
@@ -701,12 +721,12 @@
         pl.BlockSpec(memory_space=pltpu.SMEM if i < smem else pl.ANY if i in big_in else pltpu.VMEM) for i in range(n_in)
     ]
     out_specs = [pl.BlockSpec(memory_space=pl.ANY if i in big_out else pltpu.VMEM) for i in range(n_out)]
-    buffers = [pltpu.VMEM(ins[i].shape, ins[i].dtype) for i in big_in]
+    buffers = [pltpu.VMEM((2, *ins[i].shape[1:]) if i in picked else ins[i].shape, ins[i].dtype) for i in big_in]
     buffers += [pltpu.VMEM(outs[i].shape, outs[i].dtype) for i in big_out]
     at, n_sems = {}, 0
     for i in big_in:
         at[i] = n_sems
-        n_sems += ins[i].shape[0] if i in grouped else 1
+        n_sems += ins[i].shape[0] if i in grouped else 2 if i in picked else 1
     out_at = n_sems
     sems = pltpu.SemaphoreType.DMA((n_sems + len(big_out),))
 
@@ -715,13 +735,17 @@
         own, (bufs, sem) = rest[: len(scratch)], (rest[len(scratch) : -1], rest[-1])
         kept = []
         for k, i in enumerate(big_in):
-            kept.append((i, Late(ins_[i], bufs[k], sem, at[i], i in grouped)))
+            pick = ins_[0] if i in picked else None
+            kept.append((i, Late(ins_[i], bufs[k], sem, at[i], i in grouped or i in picked, pick)))
         items = dict(kept)
         for i in big_in:
-            if i not in late and i not in grouped:
+            if i not in late and i not in grouped and i not in picked:
                 items[i].start()
         for i in first:
             items[i].start()
+        for g in range(2):
+            for i in picked:
+                items[i].copy(g).start()
         for g in range(max((ins[i].shape[0] for i in grouped), default=0)):
             for i in grouped:
                 items[i].copy(g).start()
@@ -729,7 +753,7 @@
             if i in items and i not in first:
                 items[i].start()
         for i, item in kept:
-            early = i not in late and i not in grouped
+            early = i not in late and i not in grouped and i not in picked
             ins_[i] = item.wait() if early else item
         OUT.clear()
         for k, i in enumerate(big_out):
@@ -949,12 +973,13 @@
     return lax.optimization_barrier((v, *deps))[0]
 
 
-LAGS = (0, 1, 2, 5)
+LAGS = (0, 1, 3, 4)
 POS_A = 6
+B_ROWS = 128
 R_SLOT = 4
 U_AHEAD = 2
 J_SLOTS = (0, 1, 2)
-OUT_SLOTS = (2, 5, 7)
+OUT_SLOTS = (3, 6, 8)
 CHUNKS = (240, 240, 240, 240, 240, 240)
 
 
@@ -978,13 +1003,6 @@
     g1, g2 = attn_gain.reshape(1, d), ffn_gain.reshape(1, d)
     win_t = jnp.swapaxes(attn_in, 1, 2)
     wd_t = down_weight.T
-
-    def x_half(w):
-        return lax.dynamic_slice_in_dim(w, xi * 256, 256, 1), lax.dynamic_slice_in_dim(w, 512 + xi * 64, 64, 1)
-
-    (ga, gb), (ua, ub), (wa, wb) = x_half(gate_weight), x_half(up_weight), x_half(wd_t)
-    wgu = jnp.concatenate([ga, ua, gb, ub], axis=1)
-    wdh = jnp.concatenate([wa, wb, jnp.zeros((d, 64), BF16)], axis=1)
 
     th = t // 2
     sent = th if split else t
@@ -1096,16 +1114,17 @@
     y3a, y3b = links.y_start(r3a), links.y_start(r3b)
     acc = call(
         functools.partial(both_grads_kernel, len(n2b_p)), grad_outs,
-        [*n2b_p, *cot_p, wgu, wdh, after(a1[7], r3a, r3b), b1[7], *duh1, a1[8], b1[8], *df1, *acc], gscratch,
-        flops=6 * 10**9, late=[12 + 2 * len(n2b_p) - 2 + 0, 12 + 2 * len(n2b_p) - 1, *range(2 * len(n2b_p) + 2)],
+        [idx, *n2b_p, *cot_p, *ffn_w, after(a1[7], r3a, r3b), b1[7], *duh1, a1[8], b1[8], *df1, *acc], gscratch,
+        flops=6 * 10**9, smem=1,
+        late=[12 + 2 * len(n2b_p), 13 + 2 * len(n2b_p), *range(1, 2 * len(n2b_p) + 4)],
     )
     acc, df_x = tie(acc, df_x)
     df_p = links.both_cores(df_x)
     count = len(df_p)
     chunks = call(
         functools.partial(last_grads_kernel, count, len(CHUNKS)), [S((n, f), F32) for n in CHUNKS],
-        [*n2a_p, *df_p, wgu, wdh, *acc], gscratch + [pltpu.VMEM((d, f), F32), pltpu.VMEM((d, 384), F32)],
-        flops=4 * 10**9, late=[2 * count + 2, 2 * count + 3],
+        [idx, *n2a_p, *df_p, *ffn_w, *acc], gscratch + [pltpu.VMEM((d, f), F32), pltpu.VMEM((d, 384), F32)],
+        flops=4 * 10**9, smem=1, late=[2 * count + 4, 2 * count + 5],
     )
     quarter = 512 // links.narrow
     group_owner = after(group_owner, acc)
@@ -1135,39 +1154,45 @@
         first, (da1b, dp1a, dp1b, dg1a, dg2a1, _) = made["a"], made["b"]
         gains = jnp.concatenate([dg1a + dg1b, first[5] + dg2a1 + dg2b0 + dg2b1], axis=0)
         return call(
-            attn_grad_kernel, [S((n, wd), F32) for n in (lead, 128, 128, lead + 256)],
+            attn_grad_kernel, [S((n, wd), F32) for n in (lead, B_ROWS, 256 - B_ROWS, lead + 256)],
             [idx, after(a1[0], dep), b1[0], a2[0], b2[0], dp1a, dp1b, dp2a, dp2b, a1[4], b1[4], a2[4], b2[4], first[1],
              da1b, da2a, da2b, gains],
             [pltpu.VMEM((512, d), F32), pltpu.VMEM((quarter + 16, d), F32)], smem=1, flops=2 * 10**9,
+            picked=range(5, 13), late=range(13, 17),
         )
 
     def finish_out(pieces):
         return call(out_kernel, [S((d, t), BF16)], [idx, h2a, h2b, *pieces], [pltpu.VMEM((th, d), F32)], smem=1)
 
+    nc = len(CHUNKS)
+    ng = next(k for k in range(1, nc) if sum(CHUNKS[:k]) == d)
+
     def unpack(vals, theirs):
-        return call(functools.partial(unpack_kernel, 4, False), [S((d, f), F32)] * 2,
-                    [idx, *vals[:4], *theirs[:4]], smem=1, late=[1, 5, 2, 6, 3, 7, 4, 8])
+        return call(functools.partial(unpack_kernel, ng, False), [S((d, f), F32)] * 2,
+                    [idx, *vals[:ng], *theirs[:ng]], smem=1,
+                    late=[k for c in range(ng) for k in (1 + c, 1 + ng + c)])
 
     def unpack_down(vals, theirs):
-        return call(functools.partial(unpack_kernel, 2, True), [S((d, f), F32)],
-                    [idx, *vals[4:6], *theirs[4:6]], smem=1, late=[1, 3, 2, 4])
+        return call(functools.partial(unpack_kernel, nc - ng, True), [S((d, f), F32)],
+                    [idx, *vals[ng:nc], *theirs[ng:nc]], smem=1,
+                    late=[k for c in range(nc - ng) for k in (1 + c, 1 + nc - ng + c)])
 
     def collect(vals, theirs):
-        r, o = vals[6], theirs[6]
+        r, o = vals[nc], theirs[nc]
         second = jnp.where(xi == 0, jnp.concatenate([r, o], 0), jnp.concatenate([o, r], 0))
         return second, links.gather_narrow(second[:quarter])
 
     done, theirs, results = links.sum_lines(
-        chunks, [job_a, job_b, job_grads], out2, finish_out, {3: unpack, 5: unpack_down, 6: collect})
+        chunks, [job_a, job_b, job_grads], out2, finish_out, {ng - 1: unpack, nc - 1: unpack_down, nc: collect})
     layer_out = results[None][0].T
     dx = made["b"][5].T
-    ggate, gup = results[3]
-    gdown, = results[5]
-    second, slot1 = results[6]
+    ggate, gup = results[ng - 1]
+    gdown, = results[nc - 1]
+    second, slot1 = results[nc]
     small = second[quarter : quarter + 2, :d]
     gin, gout = call(
         functools.partial(attn_finish_kernel, links.narrow), [S((SLOTS, 320, d), F32), S((SLOTS, 192, d), F32)],
-        [idx, *done[7:], *theirs[7:], *slot1], smem=1,
+        [idx, *done[nc + 1 :], *theirs[nc + 1 :], *slot1], smem=1, late=[*range(5, 5 + len(slot1)), 1, 2, 3, 4],
     )
     gin = jnp.swapaxes(gin, 1, 2)
     return layer_out, dx, gin, gout, ggate, gup, gdown.T, small[0], small[1]

time: 415 us -> 404 us (0.973)
  waiting for transfers between devices: 92 us -> 75.2 us
  starting transfers between devices: 80.3 us -> 95.4 us
    ppermute x69, waiting for transfers between devices: 92 us -> 75.2 us  [permute(): return lax.ppermute(v, ('wide', 'narrow'), pairs)]
    ppermute x69, starting transfers between devices: 80.3 us -> 95.4 us  [permute(): return lax.ppermute(v, ('wide', 'narrow'), pairs)]
    dynamic_slice x4 -> x0, local copies, waits for them, and re-layouts: 4.66 us -> none  [the longest x2 2.34 us: x_half(): lax.dynamic_slice_in_dim(w, 512 + xi * 64, 64, 1)]
    unnamed x139 -> x133, local copies, waits for them, and re-layouts: 11.8 us -> 12.6 us
  transfers between devices with their start and end apart: 69 -> 69, of which waited for: 25 -> 28; matrix products, arithmetic and copies ran while one was open for 3% -> 2% of each run, Pallas kernels for 45% -> 46%
where the time goes in v4:
time: 404 us; the launch traced here: 397 us
  Pallas kernels  200 us (50%)
  starting transfers between devices  95.4 us (24%)
  waiting for transfers between devices  75.2 us (19%)
  local copies, waits for them, and re-layouts  16.5 us (4%)
  other arithmetic  6.01 us (1%)
    pallas_call x17, Pallas kernels, call(): pl.pallas_call(body, out_shape=tuple(outs), in_specs=in_specs, out_specs=...  189 us
    ppermute x69, starting transfers between devices, permute(): return lax.ppermute(v, ('wide', 'narrow'), pairs)  95.4 us
    ppermute x69, waiting for transfers between devices, permute(): return lax.ppermute(v, ('wide', 'narrow'), pairs)  75.2 us
    unnamed x133, local copies, waits for them, and re-layouts  12.6 us
    pallas_call x41, Pallas kernels, small_call(): pl.pallas_call(kernel, out_shape=jax.ShapeDtypeStruct(a.shape, a.dtype),...  9.31 us
  transfers between devices with their start and end apart: 69, of which 28 were waited for; matrix products, arithmetic and copies ran while one was open for 2% of the time, Pallas kernels for 46%

profile of v4, /device:TPU:0, one launch (start us, length us, event | category | flops | bytes accessed | tf_op | source)
XLA Modules:
  0.0 396.7 jit_solution(18403024577809037623)
XLA Ops:
  1.9 1.9 fusion
  3.8 15.5 %shard_map.196 = (bf16[256,960]{1,0:T(8,128)(2,1)}, bf16[5,256,256]{2,1,0:T(8,128)(2,1)}, bf16[5,256,128]{2,1,0:T(8,128)(2,1)}, bf16[5,256,128]{2,1,0:T(8,128)(2...) custom-call(s32[2]{0:T(128)} %pad_add_fusion.refs_0_, ...), custom_call_target="tpu_custom_call" | custom-call | flops 1 | bytes 1 | tf_op jit(solution)/shard_map/pallas_call | solution.py:774
  19.8 1.7 collective-permute-done.b
  22.7 3.0 collective-permute-start.1
  27.5 16.3 %shard_map.198 = (bf16[256,960]{1,0:T(8,128)(2,1)}, bf16[5,256,256]{2,1,0:T(8,128)(2,1)}, bf16[5,256,128]{2,1,0:T(8,128)(2,1)}, bf16[5,256,128]{2,1,0:T(8,128)(2...) custom-call(s32[2]{0:T(128)} %pad_add_fusion.refs_0_, ...), custom_call_target="tpu_custom_call" | custom-call | flops 1 | bytes 1 | tf_op jit(solution)/shard_map/pallas_call | solution.py:774
  44.0 1.6 collective-permute-start.5
  48.5 17.5 %shard_map.201 = (bf16[256,960]{1,0:T(8,128)(2,1)}, bf16[5,256,256]{2,1,0:T(8,128)(2,1)}, bf16[5,256,128]{2,1,0:T(8,128)(2,1)}, bf16[5,256,128]{2,1,0:T(8,128)(2...) custom-call(s32[2]{0:T(128)} %pad_add_fusion.refs_0_, ...), custom_call_target="tpu_custom_call" | custom-call | flops 1 | bytes 1 | tf_op jit(solution)/shard_map/pallas_call | solution.py:774
  66.0 3.6 collective-permute-done.5.refs_3_
  74.7 18.6 %shard_map.204 = (bf16[256,960]{1,0:T(8,128)(2,1)}, bf16[5,256,256]{2,1,0:T(8,128)(2,1)}, bf16[5,256,128]{2,1,0:T(8,128)(2,1)}, bf16[5,256,128]{2,1,0:T(8,128)(2...) custom-call(s32[2]{0:T(128)} %pad_add_fusion.refs_0_, ...), custom_call_target="tpu_custom_call" | custom-call | flops 1 | bytes 1 | tf_op jit(solution)/shard_map/pallas_call | solution.py:774
  93.3 2.0 collective-permute-done.10.refs_1_
  98.0 1.7 collective-permute-start.15
  99.7 4.7 %shard_map.207 = (f32[960,640]{1,0:T(8,128)}, f32[960,384]{1,0:T(8,128)}) custom-call(bf16[256,960]{1,0:T(8,128)(2,1)} %get-tuple-element.255.refs_17_.refs_0_, bf16[256,960]{1,0:T(8,128)(2,1)} %get-tuple-element.256.refs_1_, bf16[256,640]{1,0:T(8,128)(2,1)} %get-tuple-element.257.refs_2_, bf16[256,640]{1,0:T(8,128)(2,1)} %get-tuple-element.258.refs_3_, ...), custom_call_target="tpu_custom_call" | custom-call | flops 1 | bytes 1 | tf_op jit(solution)/shard_map/pallas_call | solution.py:774
  104.5 12.3 %shard_map.208 = (f32[256,960]{1,0:T(8,128)}, bf16[256,960]{1,0:T(8,128)(2,1)}, bf16[5,256,128]{2,1,0:T(8,128)(2,1)}, f32[5,256,128]{2,1,0:T(8,128)}, f32[5,2,256,128]{3,2,1,0:T(8,128)}, /*index=5*/f32[1,960]{1,0:T(1,128)}) custom-call(s32[2]{0:T(128)} %pad_add_fusion.refs_0_, f32[128,1024]{1,0:T(8,128)} %copy-done.9, f32[128,1024]{1,0:T(8,128)} %copy-done.50, ...), custom_call_target="tpu_custom_call" | custom-call | flops 1 | bytes 1 | tf_op jit(solution)/shard_map/pallas_call | solution.py:774
  116.9 1.9 collective-permute-done.14.refs_2_
  119.6 19.5 %shard_map.210 = (bf16[256,960]{1,0:T(8,128)(2,1)}, bf16[5,256,320]{2,1,0:T(8,128)(2,1)}, bf16[5,256,320]{2,1,0:T(8,128)(2,1)}, f32[1,960]{1,0:T(1,128)}, f32[1,...) custom-call(s32[2]{0:T(128)} %pad_add_fusion.refs_0_, f32[128,1024]{1,0:T(8,128)} %copy-done.11, ...), custom_call_target="tpu_custom_call" | custom-call | flops 1 | bytes 1 | tf_op jit(solution)/shard_map/pallas_call | solution.py:774
  139.7 7.9 %shard_map.211 = (bf16[256,640]{1,0:T(8,128)(2,1)}, bf16[256,640]{1,0:T(8,128)(2,1)}, bf16[256,960]{1,0:T(8,128)(2,1)}, bf16[256,960]{1,0:T(8,128)(2,1)}, f32[12...) custom-call(s32[2]{0:T(128)} %pad_add_fusion.refs_0_, ...), custom_call_target="tpu_custom_call" | custom-call | flops 1 | bytes 1 | tf_op jit(solution)/shard_map/pallas_call | solution.py:774
  151.3 10.4 %shard_map.214 = (f32[960,640]{1,0:T(8,128)}, f32[960,384]{1,0:T(8,128)}) custom-call(s32[2]{0:T(128)} %pad_add_fusion.refs_0_, f32[256,1024]{1,0:T(8,128)} %copy-done.37, f32[256,1024]{1,0:T(8,128)} %collective-permute-done.16.refs_2_, f32[256,1024]{1,0:T(8,128)} %copy-done.34, f32[256,1024]{1,0:T(8,128)} %copy-done.36, bf16[960,640]{1,0:T(8,128)(2,1)} %refs_5_.7, ...), custom_call_target="tpu_custom_call" | custom-call | flops 1 | bytes 1 | tf_op jit(solution)/shard_map/pallas_call | solution.py:774
  161.8 3.3 collective-permute-done.19.refs_3_
  168.7 9.2 %shard_map.215 = (f32[240,640]{1,0:T(8,128)}, f32[240,640]{1,0:T(8,128)}, f32[240,640]{1,0:T(8,128)}, f32[240,640]{1,0:T(8,128)}, f32[240,640]{1,0:T(8,128)}, /*index=5*/f32[240,640]{1,0:T(8,128)}) custom-call(s32[2]{0:T(128)} %pad_add_fusion.refs_0_, f32[256,1024]{1,0:T(8,128)} %copy-done.35, f32[256,1024]{1,0:T(8,128)} %copy-done.39, ...), custom_call_target="tpu_custom_call" | custom-call | flops 1 | bytes 1 | tf_op jit(solution)/shard_map/pallas_call | solution.py:774
  181.1 4.3 %collective-permute-start.28 = (f32[240,640]{1,0:T(8,128)S(1)}, f32[240,640]{1,0:T(8,128)}, u32[]{:S(2)}, u32[]{:S(2)}) collective-permute-start(f32[240,640]{1,0:T(8,128)S(1)} %copy-done.20), channel_id=1, source_target_pairs={{0,8},{1,9},{2,10},{3,11},{4,12},{5,13},{6,14},{7,15},{24,16},{25,... | collective-permute-start | bytes 1843208 | tf_op jit(solution)/shard_map/ppermute | solution.py:848
  188.5 1.9 stack.37.refs_0_
  190.4 12.4 %shard_map.217 = (f32[256,960]{1,0:T(8,128)}, bf16[256,960]{1,0:T(8,128)(2,1)}, bf16[5,256,128]{2,1,0:T(8,128)(2,1)}, f32[5,256,128]{2,1,0:T(8,128)}, f32[5,2,256,128]{3,2,1,0:T(8,128)}, /*index=5*/f32[1,960]{1,0:T(1,128)}) custom-call(s32[6]{0:T(128)} %stack.37.refs_0_, f32[128,1024]{1,0:T(8,128)} %copy-done.8, ...), custom_call_target="tpu_custom_call" | custom-call | flops 1 | bytes 1 | tf_op jit(solution)/shard_map/pallas_call | solution.py:774
  205.4 3.2 collective-permute-start.30
  209.4 19.3 %shard_map.220 = (bf16[256,960]{1,0:T(8,128)(2,1)}, bf16[5,256,320]{2,1,0:T(8,128)(2,1)}, bf16[5,256,320]{2,1,0:T(8,128)(2,1)}, f32[1,960]{1,0:T(1,128)}, f32[1,960]{1,0:T(1,128)}, /*index=5*/bf16[960,512]{1,0:T(8,128)(2,1)}) custom-call(s32[6]{0:T(128)} %stack.37.refs_0_, f32[128,1024]{1,0:T(8,128)} %copy-done.7, f32[128,1024]{1,0:T(8,128)} %copy-done.48, ...), custom_call_target="tpu_custom_call" | custom-call | flops 1 | bytes 1 | tf_op jit(solution)/shard_map/pallas_call | solution.py:774
  230.4 8.7 %shard_map.223 = (f32[72,1024]{1,0:T(8,128)}, f32[128,1024]{1,0:T(8,128)}, f32[128,1024]{1,0:T(8,128)}, f32[328,1024]{1,0:T(8,128)}) custom-call(s32[6]{0:T(128)} %stack.37.refs_0_, bf16[256,960]{1,0:T(8,128)(2,1)} %get-tuple-element.362.refs_1_, bf16[256,960]{1,0:T(8,128)(2,1)} %get-tuple-element.363.refs_2_, bf16[256,960]{1,0:T(8,128)(2,1)} %get-tuple-element.364.refs_3_, ...), custom_call_target="tpu_custom_call" | custom-call | flops 1 | bytes 1 | tf_op jit(solution)/shard_map/pallas_call | solution.py:774
  239.6 2.9 collective-permute-start.34
  244.8 6.2 %collective-permute-start.36 = (f32[240,640]{1,0:T(8,128)}, f32[240,640]{1,0:T(8,128)}, u32[]{:S(2)}, u32[]{:S(2)}) collective-permute-start(f32[240,640]{1,0:T(8,128)} %get-tuple-element.385.a), channel_id=1, source_target_pairs={{0,8},{1,9},{2,10},{3,11},{4,12},{5,13},{6,14},{7,15},{24,16},{25,... | collective-permute-start | bytes 1843208 | tf_op jit(solution)/shard_map/ppermute | solution.py:848
  251.3 5.5 %collective-permute-done.34.b = f32[240,640]{1,0:T(8,128)S(1)} collective-permute-done((f32[240,640]{1,0:T(8,128)S(1)}, f32[240,640]{1,0:T(8,128)S(1)}, u32[]{:S(2)}, u32[]{:S(2)}) %collective-permute-start.34) | collective-permute-done | bytes 614432 | tf_op jit(solution)/shard_map/ppermute | solution.py:848
  264.6 3.8 collective-permute-done.36.b
  268.4 4.4 %collective-permute-start.43 = (f32[240,640]{1,0:T(8,128)S(1)}, f32[240,640]{1,0:T(8,128)S(1)}, u32[]{:S(2)}, u32[]{:S(2)}) collective-permute-start(f32[240,640]{1,0:T(8,128)S(1)} %copy-done.16), channel_id=1, source_target_pairs={{0,8},{1,9},{2,10},{3,11},{4,12},{5,13},{6,14},{7,15},{24,16},{25,... | collective-permute-start | bytes 1843208 | tf_op jit(solution)/shard_map/ppermute | solution.py:848
  274.7 2.3 shard_map.230
  281.6 2.0 collective-permute-done.44.refs_5_
  285.2 3.7 collective-permute-done.41.b
  290.2 11.4 %collective-permute-start.48 = (f32[72,1024]{1,0:T(8,128)S(1)}, f32[72,1024]{1,0:T(8,128)S(1)}, u32[]{:S(2)}, u32[]{:S(2)}) collective-permute-start(f32[72,1024]{1,0:T(8,128)S(1)} %get-tuple-element.404.a), channel_id=1, source_target_pairs={{0,8},{1,9},{2,10},{3,11},{4,12},{5,13},{6,14},{7,15},{24,16},{25,... | collective-permute-start | bytes 884744 | tf_op jit(solution)/shard_map/ppermute | solution.py:848
  303.4 3.9 collective-permute-done.48.b
  311.1 1.8 collective-permute-done.53.b
  314.5 8.9 %collective-permute-start.55 = (f32[128,1024]{1,0:T(8,128)}, f32[128,1024]{1,0:T(8,128)S(1)}, u32[]{:S(2)}, u32[]{:S(2)}) collective-permute-start(f32[128,1024]{1,0:T(8,128)} %get-tuple-element.419.a), channel_id=1, source_target_pairs={{0,8},{1,9},{2,10},{3,11},{4,12},{5,13},{6,14},{7,15},{24,16},{25,... | collective-permute-start | bytes 1572872 | tf_op jit(solution)/shard_map/ppermute | solution.py:848
  327.2 6.4 %collective-permute-done.50.refs_8_ = f32[240,640]{1,0:T(8,128)S(1)} collective-permute-done((f32[240,640]{1,0:T(8,128)S(1)}, f32[240,640]{1,0:T(8,128)S(1)}, u32[]{:S(2)}, u32[]{:S(2)}) %collective-permute-start.50) | collective-permute-done | bytes 614432 | tf_op jit(solution)/shard_map/ppermute | solution.py:848
  336.1 4.5 %shard_map.244 = (f32[960,640]{1,0:T(8,128)}, f32[960,640]{1,0:T(8,128)}) custom-call(s32[6]{0:T(128)} %stack.37.refs_0_, f32[240,640]{1,0:T(8,128)} %copy-done.1, f32[240,640]{1,0:T(8,128)} %copy-done.2, f32[240,640]{1,0:T(8,128)} %copy-done.3, f32[240,640]{1,0:T(8,128)} %copy-done.5, f32[240,640]{1,0:T(8,128)} %copy-done.42, f32[240,640]{1,0:T(8,128)} %copy-done.43, ...), custom_call_target="tpu_custom_call" | custom-call | flops 1 | bytes 1 | tf_op jit(solution)/shard_map/pallas_call | solution.py:774
  340.6 4.3 %shard_map.245 = bf16[960,512]{1,0:T(8,128)(2,1)} custom-call(s32[6]{0:T(128)} %stack.37.refs_0_, f32[256,960]{1,0:T(8,128)} %get-tuple-element.265.refs_4_.refs_1_, f32[256,960]{1,0:T(8,128)} %get-tuple-element.276.refs_4_.refs_2_, f32[256,1024]{1,0:T(8,128)} %copy-done, f32[256,1024]{1,0:T(8,128)} %collective-permute-done.45.refs_4_), custom_call_target="tpu_custom_call" | custom-call | flops 1 | bytes 1 | tf_op jit(solution)/shard_map/pallas_call | solution.py:774
  350.1 10.8 %collective-permute-done.60.b = f32[72,1024]{1,0:T(8,128)S(1)} collective-permute-done((f32[72,1024]{1,0:T(8,128)S(1)}, f32[72,1024]{1,0:T(8,128)S(1)}, u32[]{:S(2)}, u32[]{:S(2)}) %collective-permute-start.60) | collective-permute-done | bytes 294944 | tf_op jit(solution)/shard_map/ppermute | solution.py:848
  360.9 2.1 collective-permute-start.63
  364.2 3.5 shard_map.251
  372.4 1.9 collective-permute-start.64
  376.7 3.4 collective-permute-done.66.refs_6_
  380.7 3.8 collective-permute-done.64.refs_3_
  384.5 5.6 %collective-permute-done.65.refs_4_ = f32[128,1024]{1,0:T(8,128)S(1)} collective-permute-done((f32[128,1024]{1,0:T(8,128)S(1)}, f32[128,1024]{1,0:T(8,128)S(1)}, u32[]{:S(2)}, u32[]{:S(2)}) %collective-permute-start.65) | collective-permute-done | bytes 524320 | tf_op jit(solution)/shard_map/ppermute | solution.py:848
  391.9 4.3 %shard_map.254 = (f32[2,320,960]{2,1,0:T(8,128)}, f32[2,192,960]{2,1,0:T(8,128)}) custom-call(s32[6]{0:T(128)} %stack.37.refs_0_, f32[128,1024]{1,0:T(8,128)} %copy-done.12, f32[128,1024]{1,0:T(8,128)} %copy-done.13, f32[128,1024]{1,0:T(8,128)} %copy-done.49, f32[128,1024]{1,0:T(8,128)} %copy-done.52, f32[128,1024]{1,0:T(8,128)} %copy-done.33, ...), custom_call_target="tpu_custom_call" | custom-call | flops 1 | bytes 1 | tf_op jit(solution)/shard_map/pallas_call | solution.py:774
  (297 shorter events, 83.6 us)
Async XLA Ops:
  22.7 21.2 %collective-permute-start.1 = (f32[128,1024]{1,0:T(8,128)S(1)}, f32[128,1024]{1,0:T(8,128)S(1)}, u32[]{:S(2)}, u32[]{:S(2)}) collective-permute-start(f32[128,1024]{1,0:T(8,128)S(1)} %shard_map.197.a), channel_id=1, source_target_pairs={{0,2},{1,3},{2,0},{3,1},{4,6},{5,7},{6,4},{7,5},{8,10},{9,11},{10,... | collective-permute-start | bytes 1572872 | tf_op jit(solution)/shard_map/ppermute | solution.py:848
  44.0 25.6 %collective-permute-start.5 = (f32[256,1024]{1,0:T(8,128)S(1)}, f32[256,1024]{1,0:T(8,128)S(1)}, u32[]{:S(2)}, u32[]{:S(2)}) collective-permute-start(f32[256,1024]{1,0:T(8,128)S(1)} %pad_convert_fusion), channel_id=1, source_target_pairs={{0,4},{1,5},{2,6},{3,7},{4,0},{5,1},{6,2},{7,3},{8,12},{9,13},{10,... | collective-permute-start | bytes 3145736 | tf_op jit(solution)/shard_map/ppermute | solution.py:848
  46.1 23.6 %collective-permute-start.4 = (f32[128,1024]{1,0:T(8,128)S(1)}, f32[128,1024]{1,0:T(8,128)S(1)}, u32[]{:S(2)}, u32[]{:S(2)}) collective-permute-start(f32[128,1024]{1,0:T(8,128)S(1)} %shard_map.199.a), channel_id=1, source_target_pairs={{0,2},{1,3},{2,0},{3,1},{4,6},{5,7},{6,4},{7,5},{8,10},{9,11},{10,... | collective-permute-start | bytes 1572872 | tf_op jit(solution)/shard_map/ppermute | solution.py:848
  70.2 25.1 %collective-permute-start.10 = (f32[256,1024]{1,0:T(8,128)S(1)}, f32[256,1024]{1,0:T(8,128)S(1)}, u32[]{:S(2)}, u32[]{:S(2)}) collective-permute-start(f32[256,1024]{1,0:T(8,128)S(1)} %copy-done.64), channel_id=1, source_target_pairs={{0,4},{1,5},{2,6},{3,7},{4,0},{5,1},{6,2},{7,3},{8,12},{9,13},{10,... | collective-permute-start | bytes 3145736 | tf_op jit(solution)/shard_map/ppermute | solution.py:848
  73.3 22.0 %collective-permute-start.9 = (f32[128,1024]{1,0:T(8,128)S(1)}, f32[128,1024]{1,0:T(8,128)S(1)}, u32[]{:S(2)}, u32[]{:S(2)}) collective-permute-start(f32[128,1024]{1,0:T(8,128)S(1)} %shard_map.202.a), channel_id=1, source_target_pairs={{0,2},{1,3},{2,0},{3,1},{4,6},{5,7},{6,4},{7,5},{8,10},{9,11},{10,... | collective-permute-start | bytes 1572872 | tf_op jit(solution)/shard_map/ppermute | solution.py:848
  97.5 19.2 %collective-permute-start.13 = (f32[128,1024]{1,0:T(8,128)S(1)}, f32[128,1024]{1,0:T(8,128)S(1)}, u32[]{:S(2)}, u32[]{:S(2)}) collective-permute-start(f32[128,1024]{1,0:T(8,128)S(1)} %shard_map.205.a), channel_id=1, source_target_pairs={{0,2},{1,3},{2,0},{3,1},{4,6},{5,7},{6,4},{7,5},{8,10},{9,11},{10,... | collective-permute-start | bytes 1572872 | tf_op jit(solution)/shard_map/ppermute | solution.py:848
  98.0 41.2 %collective-permute-start.15 = (f32[256,1024]{1,0:T(8,128)S(1)}, f32[256,1024]{1,0:T(8,128)S(1)}, u32[]{:S(2)}, u32[]{:S(2)}) collective-permute-start(f32[256,1024]{1,0:T(8,128)S(1)} %copy-done.65), channel_id=1, source_target_pairs={{0,4},{1,5},{2,6},{3,7},{4,0},{5,1},{6,2},{7,3},{8,12},{9,13},{10,... | collective-permute-start | bytes 3145736 | tf_op jit(solution)/shard_map/ppermute | solution.py:848
  139.2 12.2 %collective-permute-start.16 = (f32[256,1024]{1,0:T(8,128)S(1)}, f32[256,1024]{1,0:T(8,128)}, u32[]{:S(2)}, u32[]{:S(2)}) collective-permute-start(f32[256,1024]{1,0:T(8,128)S(1)} %collective-permute-done.15.refs_1_), channel_id=1, source_target_pairs={{0,1},{1,0},{2,3},{3,2},{4,5},{5,4},{6,7},{7,6},{8,9},{9,8},{10,11... | collective-permute-start | bytes 3145736 | tf_op jit(solution)/shard_map/ppermute | solution.py:848
  139.4 25.7 %collective-permute-start.19 = (f32[256,1024]{1,0:T(8,128)}, f32[256,1024]{1,0:T(8,128)S(1)}, u32[]{:S(2)}, u32[]{:S(2)}) collective-permute-start(f32[256,1024]{1,0:T(8,128)} %get-tuple-element.313), channel_id=1, source_target_pairs={{0,4},{1,5},{2,6},{3,7},{4,0},{5,1},{6,2},{7,3},{8,12},{9,13},{10,... | collective-permute-start | bytes 3145736 | tf_op jit(solution)/shard_map/ppermute | solution.py:848
  148.2 18.4 %collective-permute-start.21 = (f32[256,1024]{1,0:T(8,128)S(1)}, f32[256,1024]{1,0:T(8,128)S(1)}, u32[]{:S(2)}, u32[]{:S(2)}) collective-permute-start(f32[256,1024]{1,0:T(8,128)S(1)} %collective-permute-done.10.refs_1_), channel_id=1, source_target_pairs={{0,1},{1,0},{2,3},{3,2},{4,5},{5,4},{6,7},{7,6},{8,9},{9,8},{10,11... | collective-permute-start | bytes 3145736 | tf_op jit(solution)/shard_map/ppermute | solution.py:848
  165.0 14.3 %collective-permute-start.23 = (f32[128,1024]{1,0:T(8,128)S(1)}, f32[128,1024]{1,0:T(8,128)S(1)}, u32[]{:S(2)}, u32[]{:S(2)}) collective-permute-start(f32[128,1024]{1,0:T(8,128)S(1)} %shard_map.212.a), channel_id=1, source_target_pairs={{0,2},{1,3},{2,0},{3,1},{4,6},{5,7},{6,4},{7,5},{8,10},{9,11},{10,... | collective-permute-start | bytes 1572872 | tf_op jit(solution)/shard_map/ppermute | solution.py:848
  179.5 23.3 %collective-permute-start.26 = (f32[128,1024]{1,0:T(8,128)S(1)}, f32[128,1024]{1,0:T(8,128)S(1)}, u32[]{:S(2)}, u32[]{:S(2)}) collective-permute-start(f32[128,1024]{1,0:T(8,128)S(1)} %shard_map.213.a), channel_id=1, source_target_pairs={{0,2},{1,3},{2,0},{3,1},{4,6},{5,7},{6,4},{7,5},{8,10},{9,11},{10,... | collective-permute-start | bytes 1572872 | tf_op jit(solution)/shard_map/ppermute | solution.py:848
  181.1 22.4 %collective-permute-start.28 = (f32[240,640]{1,0:T(8,128)S(1)}, f32[240,640]{1,0:T(8,128)}, u32[]{:S(2)}, u32[]{:S(2)}) collective-permute-start(f32[240,640]{1,0:T(8,128)S(1)} %copy-done.20), channel_id=1, source_target_pairs={{0,8},{1,9},{2,10},{3,11},{4,12},{5,13},{6,14},{7,15},{24,16},{25,... | collective-permute-start | bytes 1843208 | tf_op jit(solution)/shard_map/ppermute | solution.py:848
  185.6 43.2 %collective-permute-start.24 = (f32[240,640]{1,0:T(8,128)S(1)}, f32[240,640]{1,0:T(8,128)S(1)}, u32[]{:S(2)}, u32[]{:S(2)}) collective-permute-start(f32[240,640]{1,0:T(8,128)S(1)} %copy-done.19), channel_id=1, source_target_pairs={{0,8},{1,9},{2,10},{3,11},{4,12},{5,13},{6,14},{7,15},{24,16},{25,... | collective-permute-start | bytes 1843208 | tf_op jit(solution)/shard_map/ppermute | solution.py:848
  203.0 40.5 %collective-permute-start.20 = (f32[256,1024]{1,0:T(8,128)}, f32[256,1024]{1,0:T(8,128)S(1)}, u32[]{:S(2)}, u32[]{:S(2)}) collective-permute-start(f32[256,1024]{1,0:T(8,128)} %get-tuple-element.318), channel_id=1, source_target_pairs={{0,1},{1,0},{2,3},{3,2},{4,5},{5,4},{6,7},{7,6},{8,9},{9,8},{10,11... | collective-permute-start | bytes 3145736 | tf_op jit(solution)/shard_map/ppermute | solution.py:848
  204.6 25.7 %collective-permute-start.31 = (f32[240,640]{1,0:T(8,128)S(1)}, f32[240,640]{1,0:T(8,128)S(1)}, u32[]{:S(2)}, u32[]{:S(2)}) collective-permute-start(f32[240,640]{1,0:T(8,128)S(1)} %shard_map.219.a), channel_id=1, source_target_pairs={{8,16},{9,17},{10,18},{11,19},{12,20},{13,21},{14,22},{15,23},{16,... | collective-permute-start | bytes 1843208 | tf_op jit(solution)/shard_map/ppermute | solution.py:848
  205.4 37.2 %collective-permute-start.30 = (f32[240,640]{1,0:T(8,128)S(1)}, f32[240,640]{1,0:T(8,128)S(1)}, u32[]{:S(2)}, u32[]{:S(2)}) collective-permute-start(f32[240,640]{1,0:T(8,128)S(1)} %copy-done.18), channel_id=1, source_target_pairs={{0,8},{1,9},{2,10},{3,11},{4,12},{5,13},{6,14},{7,15},{24,16},{25,... | collective-permute-start | bytes 1843208 | tf_op jit(solution)/shard_map/ppermute | solution.py:848
  228.9 15.9 %collective-permute-start.29 = (f32[240,640]{1,0:T(8,128)S(1)}, f32[240,640]{1,0:T(8,128)S(1)}, u32[]{:S(2)}, u32[]{:S(2)}) collective-permute-start(f32[240,640]{1,0:T(8,128)S(1)} %shard_map.221.a), channel_id=1, source_target_pairs={{8,16},{9,17},{10,18},{11,19},{12,20},{13,21},{14,22},{15,23},{16,... | collective-permute-start | bytes 1843208 | tf_op jit(solution)/shard_map/ppermute | solution.py:848
  239.1 34.3 %collective-permute-start.37 = (f32[328,1024]{1,0:T(8,128)}, f32[328,1024]{1,0:T(8,128)}, u32[]{:S(2)}, u32[]{:S(2)}) collective-permute-start(f32[328,1024]{1,0:T(8,128)} %get-tuple-element.388), channel_id=1, source_target_pairs={{0,4},{1,5},{2,6},{3,7},{4,0},{5,1},{6,2},{7,3},{8,12},{9,13},{10,... | collective-permute-start | bytes 4030472 | tf_op jit(solution)/shard_map/ppermute | solution.py:848
  239.6 17.2 %collective-permute-start.34 = (f32[240,640]{1,0:T(8,128)S(1)}, f32[240,640]{1,0:T(8,128)S(1)}, u32[]{:S(2)}, u32[]{:S(2)}) collective-permute-start(f32[240,640]{1,0:T(8,128)S(1)} %copy-done.17), channel_id=1, source_target_pairs={{0,8},{1,9},{2,10},{3,11},{4,12},{5,13},{6,14},{7,15},{24,16},{25,... | collective-permute-start | bytes 1843208 | tf_op jit(solution)/shard_map/ppermute | solution.py:848
  242.7 15.7 %collective-permute-start.39 = (f32[240,640]{1,0:T(8,128)S(1)}, f32[240,640]{1,0:T(8,128)S(1)}, u32[]{:S(2)}, u32[]{:S(2)}) collective-permute-start(f32[240,640]{1,0:T(8,128)S(1)} %shard_map.224.a), channel_id=1, source_target_pairs={{8,16},{9,17},{10,18},{11,19},{12,20},{13,21},{14,22},{15,23},{16,... | collective-permute-start | bytes 1843208 | tf_op jit(solution)/shard_map/ppermute | solution.py:848
  243.5 18.2 %collective-permute-start.38 = (f32[240,640]{1,0:T(8,128)S(1)}, f32[240,640]{1,0:T(8,128)}, u32[]{:S(2)}, u32[]{:S(2)}) collective-permute-start(f32[240,640]{1,0:T(8,128)S(1)} %shard_map.222.a), channel_id=1, source_target_pairs={{8,0},{9,1},{10,2},{11,3},{12,4},{13,5},{14,6},{15,7},{16,24},{17,... | collective-permute-start | bytes 1843208 | tf_op jit(solution)/shard_map/ppermute | solution.py:848
  244.8 23.6 %collective-permute-start.36 = (f32[240,640]{1,0:T(8,128)}, f32[240,640]{1,0:T(8,128)}, u32[]{:S(2)}, u32[]{:S(2)}) collective-permute-start(f32[240,640]{1,0:T(8,128)} %get-tuple-element.385.a), channel_id=1, source_target_pairs={{0,8},{1,9},{2,10},{3,11},{4,12},{5,13},{6,14},{7,15},{24,16},{25,... | collective-permute-start | bytes 1843208 | tf_op jit(solution)/shard_map/ppermute | solution.py:848
  256.9 15.9 %collective-permute-start.35 = (f32[240,640]{1,0:T(8,128)S(1)}, f32[240,640]{1,0:T(8,128)}, u32[]{:S(2)}, u32[]{:S(2)}) collective-permute-start(f32[240,640]{1,0:T(8,128)S(1)} %shard_map.227.a), channel_id=1, source_target_pairs={{8,16},{9,17},{10,18},{11,19},{12,20},{13,21},{14,22},{15,23},{16,... | collective-permute-start | bytes 1843208 | tf_op jit(solution)/shard_map/ppermute | solution.py:848
  259.2 19.1 %collective-permute-start.33 = (f32[240,640]{1,0:T(8,128)S(1)}, f32[240,640]{1,0:T(8,128)}, u32[]{:S(2)}, u32[]{:S(2)}) collective-permute-start(f32[240,640]{1,0:T(8,128)S(1)} %shard_map.225.a), channel_id=1, source_target_pairs={{8,0},{9,1},{10,2},{11,3},{12,4},{13,5},{14,6},{15,7},{16,24},{17,... | collective-permute-start | bytes 1843208 | tf_op jit(solution)/shard_map/ppermute | solution.py:848
  263.0 20.6 %collective-permute-start.44 = (f32[240,640]{1,0:T(8,128)S(1)}, f32[240,640]{1,0:T(8,128)S(1)}, u32[]{:S(2)}, u32[]{:S(2)}) collective-permute-start(f32[240,640]{1,0:T(8,128)S(1)} %shard_map.229.refs_1_), channel_id=1, source_target_pairs={{0,4},{1,5},{2,6},{3,7},{4,0},{5,1},{6,2},{7,3},{8,12},{9,13},{10,... | collective-permute-start | bytes 1843208 | tf_op jit(solution)/shard_map/ppermute | solution.py:848
  268.4 16.1 %collective-permute-start.43 = (f32[240,640]{1,0:T(8,128)S(1)}, f32[240,640]{1,0:T(8,128)S(1)}, u32[]{:S(2)}, u32[]{:S(2)}) collective-permute-start(f32[240,640]{1,0:T(8,128)S(1)} %copy-done.16), channel_id=1, source_target_pairs={{0,8},{1,9},{2,10},{3,11},{4,12},{5,13},{6,14},{7,15},{24,16},{25,... | collective-permute-start | bytes 1843208 | tf_op jit(solution)/shard_map/ppermute | solution.py:848
  272.8 30.3 %collective-permute-start.32 = (f32[256,1024]{1,0:T(8,128)S(1)}, f32[256,1024]{1,0:T(8,128)S(1)}, u32[]{:S(2)}, u32[]{:S(2)}) collective-permute-start(f32[256,1024]{1,0:T(8,128)S(1)} %shard_map.226.a), channel_id=1, source_target_pairs={{0,2},{1,3},{2,0},{3,1},{4,6},{5,7},{6,4},{7,5},{8,10},{9,11},{10,... | collective-permute-start | bytes 3145736 | tf_op jit(solution)/shard_map/ppermute | solution.py:848
  273.4 15.5 %collective-permute-start.41 = (f32[240,640]{1,0:T(8,128)S(1)}, f32[240,640]{1,0:T(8,128)S(1)}, u32[]{:S(2)}, u32[]{:S(2)}) collective-permute-start(f32[240,640]{1,0:T(8,128)S(1)} %shard_map.228.a), channel_id=1, source_target_pairs={{8,0},{9,1},{10,2},{11,3},{12,4},{13,5},{14,6},{15,7},{16,24},{17,... | collective-permute-start | bytes 1843208 | tf_op jit(solution)/shard_map/ppermute | solution.py:848
  283.5 18.1 %collective-permute-start.40 = (f32[240,640]{1,0:T(8,128)S(1)}, f32[240,640]{1,0:T(8,128)S(1)}, u32[]{:S(2)}, u32[]{:S(2)}) collective-permute-start(f32[240,640]{1,0:T(8,128)S(1)} %shard_map.233.refs_2_), channel_id=1, source_target_pairs={{0,4},{1,5},{2,6},{3,7},{4,0},{5,1},{6,2},{7,3},{8,12},{9,13},{10,... | collective-permute-start | bytes 1843208 | tf_op jit(solution)/shard_map/ppermute | solution.py:848
  284.5 24.4 %collective-permute-start.47 = (f32[240,640]{1,0:T(8,128)S(1)}, f32[240,640]{1,0:T(8,128)S(1)}, u32[]{:S(2)}, u32[]{:S(2)}) collective-permute-start(f32[240,640]{1,0:T(8,128)S(1)} %shard_map.234.a), channel_id=1, source_target_pairs={{8,16},{9,17},{10,18},{11,19},{12,20},{13,21},{14,22},{15,23},{16,... | collective-permute-start | bytes 1843208 | tf_op jit(solution)/shard_map/ppermute | solution.py:848
  288.9 21.3 %collective-permute-start.46 = (f32[240,640]{1,0:T(8,128)S(1)}, f32[240,640]{1,0:T(8,128)S(1)}, u32[]{:S(2)}, u32[]{:S(2)}) collective-permute-start(f32[240,640]{1,0:T(8,128)S(1)} %shard_map.232.a), channel_id=1, source_target_pairs={{8,0},{9,1},{10,2},{11,3},{12,4},{13,5},{14,6},{15,7},{16,24},{17,... | collective-permute-start | bytes 1843208 | tf_op jit(solution)/shard_map/ppermute | solution.py:848
  290.2 17.1 %collective-permute-start.48 = (f32[72,1024]{1,0:T(8,128)S(1)}, f32[72,1024]{1,0:T(8,128)S(1)}, u32[]{:S(2)}, u32[]{:S(2)}) collective-permute-start(f32[72,1024]{1,0:T(8,128)S(1)} %get-tuple-element.404.a), channel_id=1, source_target_pairs={{0,8},{1,9},{2,10},{3,11},{4,12},{5,13},{6,14},{7,15},{24,16},{25,... | collective-permute-start | bytes 884744 | tf_op jit(solution)/shard_map/ppermute | solution.py:848
  303.3 37.2 %collective-permute-start.45 = (f32[256,1024]{1,0:T(8,128)S(1)}, f32[256,1024]{1,0:T(8,128)}, u32[]{:S(2)}, u32[]{:S(2)}) collective-permute-start(f32[256,1024]{1,0:T(8,128)S(1)} %shard_map.237.refs_3_), channel_id=1, source_target_pairs={{0,1},{1,0},{2,3},{3,2},{4,5},{5,4},{6,7},{7,6},{8,9},{9,8},{10,11... | collective-permute-start | bytes 3145736 | tf_op jit(solution)/shard_map/ppermute | solution.py:848
  307.3 16.8 %collective-permute-start.49 = (f32[240,640]{1,0:T(8,128)S(1)}, f32[240,640]{1,0:T(8,128)S(1)}, u32[]{:S(2)}, u32[]{:S(2)}) collective-permute-start(f32[240,640]{1,0:T(8,128)S(1)} %shard_map.236.refs_3_), channel_id=1, source_target_pairs={{0,4},{1,5},{2,6},{3,7},{4,0},{5,1},{6,2},{7,3},{8,12},{9,13},{10,... | collective-permute-start | bytes 1843208 | tf_op jit(solution)/shard_map/ppermute | solution.py:848
  308.9 17.5 %collective-permute-start.51 = (f32[240,640]{1,0:T(8,128)S(1)}, f32[240,640]{1,0:T(8,128)S(1)}, u32[]{:S(2)}, u32[]{:S(2)}) collective-permute-start(f32[240,640]{1,0:T(8,128)S(1)} %shard_map.235.a), channel_id=1, source_target_pairs={{8,0},{9,1},{10,2},{11,3},{12,4},{13,5},{14,6},{15,7},{16,24},{17,... | collective-permute-start | bytes 1843208 | tf_op jit(solution)/shard_map/ppermute | solution.py:848
  312.9 20.7 %collective-permute-start.50 = (f32[240,640]{1,0:T(8,128)S(1)}, f32[240,640]{1,0:T(8,128)S(1)}, u32[]{:S(2)}, u32[]{:S(2)}) collective-permute-start(f32[240,640]{1,0:T(8,128)S(1)} %shard_map.240.refs_4_), channel_id=1, source_target_pairs={{0,4},{1,5},{2,6},{3,7},{4,0},{5,1},{6,2},{7,3},{8,12},{9,13},{10,... | collective-permute-start | bytes 1843208 | tf_op jit(solution)/shard_map/ppermute | solution.py:848
  314.5 30.4 %collective-permute-start.55 = (f32[128,1024]{1,0:T(8,128)}, f32[128,1024]{1,0:T(8,128)S(1)}, u32[]{:S(2)}, u32[]{:S(2)}) collective-permute-start(f32[128,1024]{1,0:T(8,128)} %get-tuple-element.419.a), channel_id=1, source_target_pairs={{0,8},{1,9},{2,10},{3,11},{4,12},{5,13},{6,14},{7,15},{24,16},{25,... | collective-permute-start | bytes 1572872 | tf_op jit(solution)/shard_map/ppermute | solution.py:848
  325.0 21.8 %collective-permute-start.57 = (f32[240,640]{1,0:T(8,128)S(1)}, f32[240,640]{1,0:T(8,128)S(1)}, u32[]{:S(2)}, u32[]{:S(2)}) collective-permute-start(f32[240,640]{1,0:T(8,128)S(1)} %shard_map.239.a), channel_id=1, source_target_pairs={{8,0},{9,1},{10,2},{11,3},{12,4},{13,5},{14,6},{15,7},{16,24},{17,... | collective-permute-start | bytes 1843208 | tf_op jit(solution)/shard_map/ppermute | solution.py:848
  326.4 20.3 %collective-permute-start.54 = (f32[128,1024]{1,0:T(8,128)S(1)}, f32[128,1024]{1,0:T(8,128)S(1)}, u32[]{:S(2)}, u32[]{:S(2)}) collective-permute-start(f32[128,1024]{1,0:T(8,128)S(1)} %shard_map.241.a), channel_id=1, source_target_pairs={{8,16},{9,17},{10,18},{11,19},{12,20},{13,21},{14,22},{15,23},{16,... | collective-permute-start | bytes 1572872 | tf_op jit(solution)/shard_map/ppermute | solution.py:848
  334.5 15.5 %collective-permute-start.58 = (f32[240,640]{1,0:T(8,128)S(1)}, f32[240,640]{1,0:T(8,128)S(1)}, u32[]{:S(2)}, u32[]{:S(2)}) collective-permute-start(f32[240,640]{1,0:T(8,128)S(1)} %shard_map.243.refs_1_), channel_id=1, source_target_pairs={{0,4},{1,5},{2,6},{3,7},{4,0},{5,1},{6,2},{7,3},{8,12},{9,13},{10,... | collective-permute-start | bytes 1843208 | tf_op jit(solution)/shard_map/ppermute | solution.py:848
  346.9 17.4 %collective-permute-start.59 = (f32[240,640]{1,0:T(8,128)S(1)}, f32[240,640]{1,0:T(8,128)}, u32[]{:S(2)}, u32[]{:S(2)}) collective-permute-start(f32[240,640]{1,0:T(8,128)S(1)} %shard_map.248.refs_2_), channel_id=1, source_target_pairs={{0,4},{1,5},{2,6},{3,7},{4,0},{5,1},{6,2},{7,3},{8,12},{9,13},{10,... | collective-permute-start | bytes 1843208 | tf_op jit(solution)/shard_map/ppermute | solution.py:848
  347.4 13.5 %collective-permute-start.60 = (f32[72,1024]{1,0:T(8,128)S(1)}, f32[72,1024]{1,0:T(8,128)S(1)}, u32[]{:S(2)}, u32[]{:S(2)}) collective-permute-start(f32[72,1024]{1,0:T(8,128)S(1)} %shard_map.242.a), channel_id=1, source_target_pairs={{8,0},{9,1},{10,2},{11,3},{12,4},{13,5},{14,6},{15,7},{16,24},{17,... | collective-permute-start | bytes 884744 | tf_op jit(solution)/shard_map/ppermute | solution.py:848
  348.7 20.7 %collective-permute-start.56 = (f32[128,1024]{1,0:T(8,128)S(1)}, f32[128,1024]{1,0:T(8,128)S(1)}, u32[]{:S(2)}, u32[]{:S(2)}) collective-permute-start(f32[128,1024]{1,0:T(8,128)S(1)} %shard_map.247.a), channel_id=1, source_target_pairs={{8,0},{9,1},{10,2},{11,3},{12,4},{13,5},{14,6},{15,7},{16,24},{17,... | collective-permute-start | bytes 1572872 | tf_op jit(solution)/shard_map/ppermute | solution.py:848
  362.9 12.0 %collective-permute-start.62 = (f32[128,1024]{1,0:T(8,128)S(1)}, f32[128,1024]{1,0:T(8,128)S(1)}, u32[]{:S(2)}, u32[]{:S(2)}) collective-permute-start(f32[128,1024]{1,0:T(8,128)S(1)} %shard_map.249.a), channel_id=1, source_target_pairs={{8,0},{9,1},{10,2},{11,3},{12,4},{13,5},{14,6},{15,7},{16,24},{17,... | collective-permute-start | bytes 1572872 | tf_op jit(solution)/shard_map/ppermute | solution.py:848
  372.4 12.1 %collective-permute-start.64 = (f32[128,1024]{1,0:T(8,128)S(1)}, f32[128,1024]{1,0:T(8,128)S(1)}, u32[]{:S(2)}, u32[]{:S(2)}) collective-permute-start(f32[128,1024]{1,0:T(8,128)S(1)} %shard_map.252.refs_1_), channel_id=1, source_target_pairs={{0,4},{1,5},{2,6},{3,7},{4,0},{5,1},{6,2},{7,3},{8,12},{9,13},{10,... | collective-permute-start | bytes 1572872 | tf_op jit(solution)/shard_map/ppermute | solution.py:848
  375.0 15.1 %collective-permute-start.65 = (f32[128,1024]{1,0:T(8,128)S(1)}, f32[128,1024]{1,0:T(8,128)S(1)}, u32[]{:S(2)}, u32[]{:S(2)}) collective-permute-start(f32[128,1024]{1,0:T(8,128)S(1)} %shard_map.253.refs_2_), channel_id=1, source_target_pairs={{0,4},{1,5},{2,6},{3,7},{4,0},{5,1},{6,2},{7,3},{8,12},{9,13},{10,... | collective-permute-start | bytes 1572872 | tf_op jit(solution)/shard_map/ppermute | solution.py:848
  376.6 13.5 %collective-permute-start.67 = (f32[128,1024]{1,0:T(8,128)S(1)}, f32[128,1024]{1,0:T(8,128)S(1)}, u32[]{:S(2)}, u32[]{:S(2)}) collective-permute-start(f32[128,1024]{1,0:T(8,128)S(1)} %slice.25.refs_5_), channel_id=1, source_target_pairs={{0,1},{1,0},{2,3},{3,2},{4,5},{5,4},{6,7},{7,6},{8,9},{9,8},{10,11... | collective-permute-start | bytes 1572872 | tf_op jit(solution)/shard_map/ppermute | solution.py:848
  (87 other events, 589.7 us)

commit v5 on v4

--- a/solution.py
+++ b/solution.py
@@ -171,8 +171,6 @@
     x_out = next(it)
     if second:
         duh_ref, part_refs = next(it), [next(it) for _ in range(2 if part and split else 1)]
-    else:
-        gate_ref, up_ref = next(it), next(it)
     outs = [next(it) for _ in range(2 if split else 1)]
     acc, whole, ktf, vtf = (next(it) for _ in range(4))
     t = n1_ref.shape[0]
@@ -295,10 +293,6 @@
         flush(duh_ref)
         whole[...] = dot_nt(dgate.astype(BF16), wg[...]) + dot_nt(dup.astype(BF16), wu[...])
     else:
-        gate_ref[...] = gate
-        up_ref[...] = up
-        flush(gate_ref)
-        flush(up_ref)
         whole[...] = dot_nt(hid.astype(BF16), wdt[...])
     if split:
         split_send(idx, whole, *outs)
@@ -470,20 +464,20 @@
 
 
 def ffn_back_kernel(split, *refs):
-    idx, dza, dzb, gatea, gateb, upa, upb, wg, wu, wdt, duha, duhb, dfa, dfb, *rest = refs
+    idx, dza, dzb, n2a, n2b, wg, wu, wdt, duha, duhb, dfa, dfb, *rest = refs
     outs, whole = rest[:-1], rest[-1]
     per = len(outs) // 2
-    for k, (dz_ref, gate_ref, up_ref, duh_ref, df_ref) in enumerate(
-            ((dza, gatea, upa, duha, dfa), (dzb, gateb, upb, duhb, dfb))):
+    for k, (dz_ref, n2_ref, duh_ref, df_ref) in enumerate(
+            ((dza, n2a, duha, dfa), (dzb, n2b, duhb, dfb))):
         df = ready(dz_ref)[...].astype(BF16)
         df_ref[...] = df
         flush(df_ref)
-        wdt, gate_ref, up_ref = ready(wdt, gate_ref, up_ref)
-        gate, up = gate_ref[...], up_ref[...]
+        n2_ref, wg, wu = ready(n2_ref, wg, wu)
+        gate, up = dot(n2_ref[...], wg[...]), dot(n2_ref[...], wu[...])
+        wdt = ready(wdt)
         dgate, dup = ffn_back(dot(df, wdt[...]), gate, up, jax.nn.sigmoid(gate))
         store_pair(idx, duh_ref, slice(0, df.shape[0]), dgate, dup)
         flush(duh_ref)
-        wg, wu = ready(wg, wu)
         whole[...] = dot_nt(dgate.astype(BF16), wg[...]) + dot_nt(dup.astype(BF16), wu[...])
         if split:
             split_send(idx, whole, *outs[per * k : per * k + per])
@@ -1019,7 +1013,7 @@
     def forward(second, x, adds, old):
         part = old is not None
         outs = list(saved) + ([piece] if part else [])
-        outs += [S((th, d), F32), S((th, f), BF16)] + ([piece] * n_sums if part else [S((th, d), F32)]) if second else [S((th, d), BF16)] + [S((th, f), F32)] * 2
+        outs += [S((th, d), F32), S((th, f), BF16)] + ([piece] * n_sums if part else [S((th, d), F32)]) if second else [S((th, d), BF16)]
         ins = [idx, x, *adds] + weights + ffn_w
         at = 2 + len(adds)
         ins += [old[2], old[3], old[7]] if part else []
@@ -1038,11 +1032,11 @@
     tokens_t = tokens.T
     cot_x = links.x(cot_s)
     a1, s1a = forward(False, tokens_t, [], None)
-    *a1, tok_a, gate1a, up1a = a1
+    *a1, tok_a = a1
     r1a = links.sum_cores(s1a)
     y1a = links.y_start(r1a)
     b1, s1b = forward(False, after(tokens_t, r1a), [], a1)
-    *b1, n2as, tok_b, gate1b, up1b = b1
+    *b1, n2as, tok_b = b1
     s1b, n2as, y1a = tie(s1b, n2as, y1a)
     sum1a = links.sum_chips(r1a, y1a)
     r1b = links.sum_cores(s1b)
@@ -1106,8 +1100,8 @@
     da2a, dg2b0 = first2[1], first2[5]
     res = call(
         functools.partial(ffn_back_kernel, split), [S((th, f), BF16)] * 2 + [S((th, d), BF16)] * 2 + sums * 2,
-        [idx, dz1a, dz1b, gate1a, gate1b, up1a, up1b] + ffn_w, [pltpu.VMEM((th, d), F32)], smem=1, flops=2 * 10**9,
-        late=[1, 9, 3, 5, 7, 8, 2, 4, 6],
+        [idx, dz1a, dz1b, a1[7], b1[7]] + ffn_w, [pltpu.VMEM((th, d), F32)], smem=1, flops=2 * 10**9,
+        late=[1, 3, 5, 6, 7, 2, 4],
     )
     duh1, df1, s3 = res[:2], res[2:4], res[4:]
     r3a, r3b = links.sum_cores(s3[:n_sums]), links.sum_cores(s3[n_sums:])

time: 404 us -> 404 us (level)
  no operation moved by 1% of the time
where the time goes in v5:
time: 404 us; the launch traced here: 396 us
  Pallas kernels  202 us (50%)
  starting transfers between devices  95.5 us (24%)
  waiting for transfers between devices  73.2 us (18%)
  local copies, waits for them, and re-layouts  16.5 us (4%)
  other arithmetic  6 us (1%)
    pallas_call x17, Pallas kernels, call(): pl.pallas_call(body, out_shape=tuple(outs), in_specs=in_specs, out_specs=...  190 us
    ppermute x69, starting transfers between devices, permute(): return lax.ppermute(v, ('wide', 'narrow'), pairs)  95.5 us
    ppermute x69, waiting for transfers between devices, permute(): return lax.ppermute(v, ('wide', 'narrow'), pairs)  73.2 us
    unnamed x133, local copies, waits for them, and re-layouts  12.6 us
    pallas_call x41, Pallas kernels, small_call(): pl.pallas_call(kernel, out_shape=jax.ShapeDtypeStruct(a.shape, a.dtype),...  9.31 us
  transfers between devices with their start and end apart: 69, of which 28 were waited for; matrix products, arithmetic and copies ran while one was open for 2% of the time, Pallas kernels for 46%

profile of v5, /device:TPU:0, one launch (start us, length us, event | category | flops | bytes accessed | tf_op | source)
XLA Modules:
  0.0 396.3 jit_solution(8664281049849795232)
XLA Ops:
  1.9 1.8 fusion
  3.8 15.4 %shard_map.196 = (bf16[256,960]{1,0:T(8,128)(2,1)}, bf16[5,256,256]{2,1,0:T(8,128)(2,1)}, bf16[5,256,128]{2,1,0:T(8,128)(2,1)}, bf16[5,256,128]{2,1,0:T(8,128)(2...) custom-call(s32[2]{0:T(128)} %pad_add_fusion.refs_0_, ...), custom_call_target="tpu_custom_call" | custom-call | flops 1 | bytes 1 | tf_op jit(solution)/shard_map/pallas_call | solution.py:768
  19.7 1.7 collective-permute-done.b
  22.5 3.0 collective-permute-start.1
  27.3 16.2 %shard_map.198 = (bf16[256,960]{1,0:T(8,128)(2,1)}, bf16[5,256,256]{2,1,0:T(8,128)(2,1)}, bf16[5,256,128]{2,1,0:T(8,128)(2,1)}, bf16[5,256,128]{2,1,0:T(8,128)(2...) custom-call(s32[2]{0:T(128)} %pad_add_fusion.refs_0_, ...), custom_call_target="tpu_custom_call" | custom-call | flops 1 | bytes 1 | tf_op jit(solution)/shard_map/pallas_call | solution.py:768
  43.8 1.7 collective-permute-start.5
  48.3 17.5 %shard_map.201 = (bf16[256,960]{1,0:T(8,128)(2,1)}, bf16[5,256,256]{2,1,0:T(8,128)(2,1)}, bf16[5,256,128]{2,1,0:T(8,128)(2,1)}, bf16[5,256,128]{2,1,0:T(8,128)(2...) custom-call(s32[2]{0:T(128)} %pad_add_fusion.refs_0_, ...), custom_call_target="tpu_custom_call" | custom-call | flops 1 | bytes 1 | tf_op jit(solution)/shard_map/pallas_call | solution.py:768
  65.8 3.6 collective-permute-done.5.refs_3_
  74.4 18.6 %shard_map.204 = (bf16[256,960]{1,0:T(8,128)(2,1)}, bf16[5,256,256]{2,1,0:T(8,128)(2,1)}, bf16[5,256,128]{2,1,0:T(8,128)(2,1)}, bf16[5,256,128]{2,1,0:T(8,128)(2...) custom-call(s32[2]{0:T(128)} %pad_add_fusion.refs_0_, ...), custom_call_target="tpu_custom_call" | custom-call | flops 1 | bytes 1 | tf_op jit(solution)/shard_map/pallas_call | solution.py:768
  93.0 2.0 collective-permute-done.10.refs_1_
  97.7 1.7 collective-permute-start.15
  99.5 4.7 %shard_map.207 = (f32[960,640]{1,0:T(8,128)}, f32[960,384]{1,0:T(8,128)}) custom-call(bf16[256,960]{1,0:T(8,128)(2,1)} %get-tuple-element.251.refs_17_.refs_0_, bf16[256,960]{1,0:T(8,128)(2,1)} %get-tuple-element.252.refs_1_, bf16[256,640]{1,0:T(8,128)(2,1)} %get-tuple-element.253.refs_2_, bf16[256,640]{1,0:T(8,128)(2,1)} %get-tuple-element.254.refs_3_, ...), custom_call_target="tpu_custom_call" | custom-call | flops 1 | bytes 1 | tf_op jit(solution)/shard_map/pallas_call | solution.py:768
  104.2 12.3 %shard_map.208 = (f32[256,960]{1,0:T(8,128)}, bf16[256,960]{1,0:T(8,128)(2,1)}, bf16[5,256,128]{2,1,0:T(8,128)(2,1)}, f32[5,256,128]{2,1,0:T(8,128)}, f32[5,2,256,128]{3,2,1,0:T(8,128)}, /*index=5*/f32[1,960]{1,0:T(1,128)}) custom-call(s32[2]{0:T(128)} %pad_add_fusion.refs_0_, f32[128,1024]{1,0:T(8,128)} %copy-done.9, f32[128,1024]{1,0:T(8,128)} %copy-done.50, ...), custom_call_target="tpu_custom_call" | custom-call | flops 1 | bytes 1 | tf_op jit(solution)/shard_map/pallas_call | solution.py:768
  116.7 1.9 collective-permute-done.14.refs_2_
  119.4 19.4 %shard_map.210 = (bf16[256,960]{1,0:T(8,128)(2,1)}, bf16[5,256,320]{2,1,0:T(8,128)(2,1)}, bf16[5,256,320]{2,1,0:T(8,128)(2,1)}, f32[1,960]{1,0:T(1,128)}, f32[1,...) custom-call(s32[2]{0:T(128)} %pad_add_fusion.refs_0_, f32[128,1024]{1,0:T(8,128)} %copy-done.11, ...), custom_call_target="tpu_custom_call" | custom-call | flops 1 | bytes 1 | tf_op jit(solution)/shard_map/pallas_call | solution.py:768
  139.4 9.5 %shard_map.211 = (bf16[256,640]{1,0:T(8,128)(2,1)}, bf16[256,640]{1,0:T(8,128)(2,1)}, bf16[256,960]{1,0:T(8,128)(2,1)}, bf16[256,960]{1,0:T(8,128)(2,1)}, f32[12...) custom-call(s32[2]{0:T(128)} %pad_add_fusion.refs_0_, ...), custom_call_target="tpu_custom_call" | custom-call | flops 1 | bytes 1 | tf_op jit(solution)/shard_map/pallas_call | solution.py:768
  152.7 10.4 %shard_map.214 = (f32[960,640]{1,0:T(8,128)}, f32[960,384]{1,0:T(8,128)}) custom-call(s32[2]{0:T(128)} %pad_add_fusion.refs_0_, f32[256,1024]{1,0:T(8,128)} %copy-done.37, f32[256,1024]{1,0:T(8,128)} %collective-permute-done.16.refs_2_, f32[256,1024]{1,0:T(8,128)} %copy-done.34, f32[256,1024]{1,0:T(8,128)} %copy-done.36, bf16[960,640]{1,0:T(8,128)(2,1)} %refs_5_.9, ...), custom_call_target="tpu_custom_call" | custom-call | flops 1 | bytes 1 | tf_op jit(solution)/shard_map/pallas_call | solution.py:768
  168.4 9.2 %shard_map.215 = (f32[240,640]{1,0:T(8,128)}, f32[240,640]{1,0:T(8,128)}, f32[240,640]{1,0:T(8,128)}, f32[240,640]{1,0:T(8,128)}, f32[240,640]{1,0:T(8,128)}, /*index=5*/f32[240,640]{1,0:T(8,128)}) custom-call(s32[2]{0:T(128)} %pad_add_fusion.refs_0_, f32[256,1024]{1,0:T(8,128)} %copy-done.35, f32[256,1024]{1,0:T(8,128)} %copy-done.39, ...), custom_call_target="tpu_custom_call" | custom-call | flops 1 | bytes 1 | tf_op jit(solution)/shard_map/pallas_call | solution.py:768
  180.8 4.3 %collective-permute-start.28 = (f32[240,640]{1,0:T(8,128)S(1)}, f32[240,640]{1,0:T(8,128)}, u32[]{:S(2)}, u32[]{:S(2)}) collective-permute-start(f32[240,640]{1,0:T(8,128)S(1)} %copy-done.20), channel_id=1, source_target_pairs={{0,8},{1,9},{2,10},{3,11},{4,12},{5,13},{6,14},{7,15},{24,16},{25,... | collective-permute-start | bytes 1843208 | tf_op jit(solution)/shard_map/ppermute | solution.py:842
  188.2 1.9 stack.37.refs_0_
  190.1 12.4 %shard_map.217 = (f32[256,960]{1,0:T(8,128)}, bf16[256,960]{1,0:T(8,128)(2,1)}, bf16[5,256,128]{2,1,0:T(8,128)(2,1)}, f32[5,256,128]{2,1,0:T(8,128)}, f32[5,2,256,128]{3,2,1,0:T(8,128)}, /*index=5*/f32[1,960]{1,0:T(1,128)}) custom-call(s32[6]{0:T(128)} %stack.37.refs_0_, f32[128,1024]{1,0:T(8,128)} %copy-done.8, ...), custom_call_target="tpu_custom_call" | custom-call | flops 1 | bytes 1 | tf_op jit(solution)/shard_map/pallas_call | solution.py:768
  205.0 3.2 collective-permute-start.30
  209.1 19.3 %shard_map.220 = (bf16[256,960]{1,0:T(8,128)(2,1)}, bf16[5,256,320]{2,1,0:T(8,128)(2,1)}, bf16[5,256,320]{2,1,0:T(8,128)(2,1)}, f32[1,960]{1,0:T(1,128)}, f32[1,960]{1,0:T(1,128)}, /*index=5*/bf16[960,512]{1,0:T(8,128)(2,1)}) custom-call(s32[6]{0:T(128)} %stack.37.refs_0_, f32[128,1024]{1,0:T(8,128)} %copy-done.7, f32[128,1024]{1,0:T(8,128)} %copy-done.48, ...), custom_call_target="tpu_custom_call" | custom-call | flops 1 | bytes 1 | tf_op jit(solution)/shard_map/pallas_call | solution.py:768
  230.1 8.8 %shard_map.223 = (f32[72,1024]{1,0:T(8,128)}, f32[128,1024]{1,0:T(8,128)}, f32[128,1024]{1,0:T(8,128)}, f32[328,1024]{1,0:T(8,128)}) custom-call(s32[6]{0:T(128)} %stack.37.refs_0_, bf16[256,960]{1,0:T(8,128)(2,1)} %get-tuple-element.354.refs_1_, bf16[256,960]{1,0:T(8,128)(2,1)} %get-tuple-element.355.refs_2_, bf16[256,960]{1,0:T(8,128)(2,1)} %get-tuple-element.356.refs_3_, ...), custom_call_target="tpu_custom_call" | custom-call | flops 1 | bytes 1 | tf_op jit(solution)/shard_map/pallas_call | solution.py:768
  239.3 2.9 collective-permute-start.34
  244.6 6.2 %collective-permute-start.36 = (f32[240,640]{1,0:T(8,128)}, f32[240,640]{1,0:T(8,128)}, u32[]{:S(2)}, u32[]{:S(2)}) collective-permute-start(f32[240,640]{1,0:T(8,128)} %get-tuple-element.377.a), channel_id=1, source_target_pairs={{0,8},{1,9},{2,10},{3,11},{4,12},{5,13},{6,14},{7,15},{24,16},{25,... | collective-permute-start | bytes 1843208 | tf_op jit(solution)/shard_map/ppermute | solution.py:842
  251.0 5.5 %collective-permute-done.34.b = f32[240,640]{1,0:T(8,128)S(1)} collective-permute-done((f32[240,640]{1,0:T(8,128)S(1)}, f32[240,640]{1,0:T(8,128)S(1)}, u32[]{:S(2)}, u32[]{:S(2)}) %collective-permute-start.34) | collective-permute-done | bytes 614432 | tf_op jit(solution)/shard_map/ppermute | solution.py:842
  264.4 3.7 collective-permute-done.36.b
  268.0 4.4 %collective-permute-start.43 = (f32[240,640]{1,0:T(8,128)S(1)}, f32[240,640]{1,0:T(8,128)S(1)}, u32[]{:S(2)}, u32[]{:S(2)}) collective-permute-start(f32[240,640]{1,0:T(8,128)S(1)} %copy-done.16), channel_id=1, source_target_pairs={{0,8},{1,9},{2,10},{3,11},{4,12},{5,13},{6,14},{7,15},{24,16},{25,... | collective-permute-start | bytes 1843208 | tf_op jit(solution)/shard_map/ppermute | solution.py:842
  274.3 2.3 shard_map.230
  281.2 2.0 collective-permute-done.44.refs_5_
  284.8 3.7 collective-permute-done.41.b
  289.8 11.4 %collective-permute-start.48 = (f32[72,1024]{1,0:T(8,128)S(1)}, f32[72,1024]{1,0:T(8,128)S(1)}, u32[]{:S(2)}, u32[]{:S(2)}) collective-permute-start(f32[72,1024]{1,0:T(8,128)S(1)} %get-tuple-element.396.a), channel_id=1, source_target_pairs={{0,8},{1,9},{2,10},{3,11},{4,12},{5,13},{6,14},{7,15},{24,16},{25,... | collective-permute-start | bytes 884744 | tf_op jit(solution)/shard_map/ppermute | solution.py:842
  303.0 3.9 collective-permute-done.48.b
  310.7 1.8 collective-permute-done.53.b
  314.1 8.9 %collective-permute-start.55 = (f32[128,1024]{1,0:T(8,128)}, f32[128,1024]{1,0:T(8,128)S(1)}, u32[]{:S(2)}, u32[]{:S(2)}) collective-permute-start(f32[128,1024]{1,0:T(8,128)} %get-tuple-element.411.a), channel_id=1, source_target_pairs={{0,8},{1,9},{2,10},{3,11},{4,12},{5,13},{6,14},{7,15},{24,16},{25,... | collective-permute-start | bytes 1572872 | tf_op jit(solution)/shard_map/ppermute | solution.py:842
  326.8 6.4 %collective-permute-done.50.refs_8_ = f32[240,640]{1,0:T(8,128)S(1)} collective-permute-done((f32[240,640]{1,0:T(8,128)S(1)}, f32[240,640]{1,0:T(8,128)S(1)}, u32[]{:S(2)}, u32[]{:S(2)}) %collective-permute-start.50) | collective-permute-done | bytes 614432 | tf_op jit(solution)/shard_map/ppermute | solution.py:842
  335.7 4.5 %shard_map.244 = (f32[960,640]{1,0:T(8,128)}, f32[960,640]{1,0:T(8,128)}) custom-call(s32[6]{0:T(128)} %stack.37.refs_0_, f32[240,640]{1,0:T(8,128)} %copy-done.1, f32[240,640]{1,0:T(8,128)} %copy-done.2, f32[240,640]{1,0:T(8,128)} %copy-done.3, f32[240,640]{1,0:T(8,128)} %copy-done.5, f32[240,640]{1,0:T(8,128)} %copy-done.42, f32[240,640]{1,0:T(8,128)} %copy-done.43, ...), custom_call_target="tpu_custom_call" | custom-call | flops 1 | bytes 1 | tf_op jit(solution)/shard_map/pallas_call | solution.py:768
  340.2 4.3 %shard_map.245 = bf16[960,512]{1,0:T(8,128)(2,1)} custom-call(s32[6]{0:T(128)} %stack.37.refs_0_, f32[256,960]{1,0:T(8,128)} %get-tuple-element.261.refs_4_.refs_1_, f32[256,960]{1,0:T(8,128)} %get-tuple-element.272.refs_4_.refs_2_, f32[256,1024]{1,0:T(8,128)} %copy-done, f32[256,1024]{1,0:T(8,128)} %collective-permute-done.45.refs_4_), custom_call_target="tpu_custom_call" | custom-call | flops 1 | bytes 1 | tf_op jit(solution)/shard_map/pallas_call | solution.py:768
  349.7 10.8 %collective-permute-done.60.b = f32[72,1024]{1,0:T(8,128)S(1)} collective-permute-done((f32[72,1024]{1,0:T(8,128)S(1)}, f32[72,1024]{1,0:T(8,128)S(1)}, u32[]{:S(2)}, u32[]{:S(2)}) %collective-permute-start.60) | collective-permute-done | bytes 294944 | tf_op jit(solution)/shard_map/ppermute | solution.py:842
  360.4 2.1 collective-permute-start.63
  363.9 3.5 shard_map.251
  370.4 1.8 collective-permute-start.66
  374.7 1.7 collective-permute-start.65
  376.4 3.3 collective-permute-done.66.refs_6_
  380.3 3.8 collective-permute-done.64.refs_3_
  384.1 5.6 %collective-permute-done.65.refs_4_ = f32[128,1024]{1,0:T(8,128)S(1)} collective-permute-done((f32[128,1024]{1,0:T(8,128)S(1)}, f32[128,1024]{1,0:T(8,128)S(1)}, u32[]{:S(2)}, u32[]{:S(2)}) %collective-permute-start.65) | collective-permute-done | bytes 524320 | tf_op jit(solution)/shard_map/ppermute | solution.py:842
  391.5 4.3 %shard_map.254 = (f32[2,320,960]{2,1,0:T(8,128)}, f32[2,192,960]{2,1,0:T(8,128)}) custom-call(s32[6]{0:T(128)} %stack.37.refs_0_, f32[128,1024]{1,0:T(8,128)} %copy-done.12, f32[128,1024]{1,0:T(8,128)} %copy-done.13, f32[128,1024]{1,0:T(8,128)} %copy-done.49, f32[128,1024]{1,0:T(8,128)} %copy-done.52, f32[128,1024]{1,0:T(8,128)} %copy-done.33, ...), custom_call_target="tpu_custom_call" | custom-call | flops 1 | bytes 1 | tf_op jit(solution)/shard_map/pallas_call | solution.py:768
  (297 shorter events, 83.6 us)
Async XLA Ops:
  22.5 21.0 %collective-permute-start.1 = (f32[128,1024]{1,0:T(8,128)S(1)}, f32[128,1024]{1,0:T(8,128)S(1)}, u32[]{:S(2)}, u32[]{:S(2)}) collective-permute-start(f32[128,1024]{1,0:T(8,128)S(1)} %shard_map.197.a), channel_id=1, source_target_pairs={{0,2},{1,3},{2,0},{3,1},{4,6},{5,7},{6,4},{7,5},{8,10},{9,11},{10,... | collective-permute-start | bytes 1572872 | tf_op jit(solution)/shard_map/ppermute | solution.py:842
  43.8 25.6 %collective-permute-start.5 = (f32[256,1024]{1,0:T(8,128)S(1)}, f32[256,1024]{1,0:T(8,128)S(1)}, u32[]{:S(2)}, u32[]{:S(2)}) collective-permute-start(f32[256,1024]{1,0:T(8,128)S(1)} %pad_convert_fusion), channel_id=1, source_target_pairs={{0,4},{1,5},{2,6},{3,7},{4,0},{5,1},{6,2},{7,3},{8,12},{9,13},{10,... | collective-permute-start | bytes 3145736 | tf_op jit(solution)/shard_map/ppermute | solution.py:842
  45.8 23.6 %collective-permute-start.4 = (f32[128,1024]{1,0:T(8,128)S(1)}, f32[128,1024]{1,0:T(8,128)S(1)}, u32[]{:S(2)}, u32[]{:S(2)}) collective-permute-start(f32[128,1024]{1,0:T(8,128)S(1)} %shard_map.199.a), channel_id=1, source_target_pairs={{0,2},{1,3},{2,0},{3,1},{4,6},{5,7},{6,4},{7,5},{8,10},{9,11},{10,... | collective-permute-start | bytes 1572872 | tf_op jit(solution)/shard_map/ppermute | solution.py:842
  69.9 25.1 %collective-permute-start.10 = (f32[256,1024]{1,0:T(8,128)S(1)}, f32[256,1024]{1,0:T(8,128)S(1)}, u32[]{:S(2)}, u32[]{:S(2)}) collective-permute-start(f32[256,1024]{1,0:T(8,128)S(1)} %copy-done.64), channel_id=1, source_target_pairs={{0,4},{1,5},{2,6},{3,7},{4,0},{5,1},{6,2},{7,3},{8,12},{9,13},{10,... | collective-permute-start | bytes 3145736 | tf_op jit(solution)/shard_map/ppermute | solution.py:842
  73.0 22.0 %collective-permute-start.9 = (f32[128,1024]{1,0:T(8,128)S(1)}, f32[128,1024]{1,0:T(8,128)S(1)}, u32[]{:S(2)}, u32[]{:S(2)}) collective-permute-start(f32[128,1024]{1,0:T(8,128)S(1)} %shard_map.202.a), channel_id=1, source_target_pairs={{0,2},{1,3},{2,0},{3,1},{4,6},{5,7},{6,4},{7,5},{8,10},{9,11},{10,... | collective-permute-start | bytes 1572872 | tf_op jit(solution)/shard_map/ppermute | solution.py:842
  97.3 19.2 %collective-permute-start.13 = (f32[128,1024]{1,0:T(8,128)S(1)}, f32[128,1024]{1,0:T(8,128)S(1)}, u32[]{:S(2)}, u32[]{:S(2)}) collective-permute-start(f32[128,1024]{1,0:T(8,128)S(1)} %shard_map.205.a), channel_id=1, source_target_pairs={{0,2},{1,3},{2,0},{3,1},{4,6},{5,7},{6,4},{7,5},{8,10},{9,11},{10,... | collective-permute-start | bytes 1572872 | tf_op jit(solution)/shard_map/ppermute | solution.py:842
  97.7 41.1 %collective-permute-start.15 = (f32[256,1024]{1,0:T(8,128)S(1)}, f32[256,1024]{1,0:T(8,128)S(1)}, u32[]{:S(2)}, u32[]{:S(2)}) collective-permute-start(f32[256,1024]{1,0:T(8,128)S(1)} %copy-done.65), channel_id=1, source_target_pairs={{0,4},{1,5},{2,6},{3,7},{4,0},{5,1},{6,2},{7,3},{8,12},{9,13},{10,... | collective-permute-start | bytes 3145736 | tf_op jit(solution)/shard_map/ppermute | solution.py:842
  138.8 13.8 %collective-permute-start.16 = (f32[256,1024]{1,0:T(8,128)S(1)}, f32[256,1024]{1,0:T(8,128)}, u32[]{:S(2)}, u32[]{:S(2)}) collective-permute-start(f32[256,1024]{1,0:T(8,128)S(1)} %collective-permute-done.15.refs_1_), channel_id=1, source_target_pairs={{0,1},{1,0},{2,3},{3,2},{4,5},{5,4},{6,7},{7,6},{8,9},{9,8},{10,11... | collective-permute-start | bytes 3145736 | tf_op jit(solution)/shard_map/ppermute | solution.py:842
  139.0 25.7 %collective-permute-start.19 = (f32[256,1024]{1,0:T(8,128)}, f32[256,1024]{1,0:T(8,128)S(1)}, u32[]{:S(2)}, u32[]{:S(2)}) collective-permute-start(f32[256,1024]{1,0:T(8,128)} %get-tuple-element.305), channel_id=1, source_target_pairs={{0,4},{1,5},{2,6},{3,7},{4,0},{5,1},{6,2},{7,3},{8,12},{9,13},{10,... | collective-permute-start | bytes 3145736 | tf_op jit(solution)/shard_map/ppermute | solution.py:842
  149.5 16.7 %collective-permute-start.21 = (f32[256,1024]{1,0:T(8,128)S(1)}, f32[256,1024]{1,0:T(8,128)S(1)}, u32[]{:S(2)}, u32[]{:S(2)}) collective-permute-start(f32[256,1024]{1,0:T(8,128)S(1)} %collective-permute-done.10.refs_1_), channel_id=1, source_target_pairs={{0,1},{1,0},{2,3},{3,2},{4,5},{5,4},{6,7},{7,6},{8,9},{9,8},{10,11... | collective-permute-start | bytes 3145736 | tf_op jit(solution)/shard_map/ppermute | solution.py:842
  164.7 14.3 %collective-permute-start.23 = (f32[128,1024]{1,0:T(8,128)S(1)}, f32[128,1024]{1,0:T(8,128)S(1)}, u32[]{:S(2)}, u32[]{:S(2)}) collective-permute-start(f32[128,1024]{1,0:T(8,128)S(1)} %shard_map.212.a), channel_id=1, source_target_pairs={{0,2},{1,3},{2,0},{3,1},{4,6},{5,7},{6,4},{7,5},{8,10},{9,11},{10,... | collective-permute-start | bytes 1572872 | tf_op jit(solution)/shard_map/ppermute | solution.py:842
  179.2 23.3 %collective-permute-start.26 = (f32[128,1024]{1,0:T(8,128)S(1)}, f32[128,1024]{1,0:T(8,128)S(1)}, u32[]{:S(2)}, u32[]{:S(2)}) collective-permute-start(f32[128,1024]{1,0:T(8,128)S(1)} %shard_map.213.a), channel_id=1, source_target_pairs={{0,2},{1,3},{2,0},{3,1},{4,6},{5,7},{6,4},{7,5},{8,10},{9,11},{10,... | collective-permute-start | bytes 1572872 | tf_op jit(solution)/shard_map/ppermute | solution.py:842
  180.8 22.4 %collective-permute-start.28 = (f32[240,640]{1,0:T(8,128)S(1)}, f32[240,640]{1,0:T(8,128)}, u32[]{:S(2)}, u32[]{:S(2)}) collective-permute-start(f32[240,640]{1,0:T(8,128)S(1)} %copy-done.20), channel_id=1, source_target_pairs={{0,8},{1,9},{2,10},{3,11},{4,12},{5,13},{6,14},{7,15},{24,16},{25,... | collective-permute-start | bytes 1843208 | tf_op jit(solution)/shard_map/ppermute | solution.py:842
  185.3 43.2 %collective-permute-start.24 = (f32[240,640]{1,0:T(8,128)S(1)}, f32[240,640]{1,0:T(8,128)S(1)}, u32[]{:S(2)}, u32[]{:S(2)}) collective-permute-start(f32[240,640]{1,0:T(8,128)S(1)} %copy-done.19), channel_id=1, source_target_pairs={{0,8},{1,9},{2,10},{3,11},{4,12},{5,13},{6,14},{7,15},{24,16},{25,... | collective-permute-start | bytes 1843208 | tf_op jit(solution)/shard_map/ppermute | solution.py:842
  202.7 40.6 %collective-permute-start.20 = (f32[256,1024]{1,0:T(8,128)}, f32[256,1024]{1,0:T(8,128)S(1)}, u32[]{:S(2)}, u32[]{:S(2)}) collective-permute-start(f32[256,1024]{1,0:T(8,128)} %get-tuple-element.310), channel_id=1, source_target_pairs={{0,1},{1,0},{2,3},{3,2},{4,5},{5,4},{6,7},{7,6},{8,9},{9,8},{10,11... | collective-permute-start | bytes 3145736 | tf_op jit(solution)/shard_map/ppermute | solution.py:842
  204.3 25.7 %collective-permute-start.31 = (f32[240,640]{1,0:T(8,128)S(1)}, f32[240,640]{1,0:T(8,128)S(1)}, u32[]{:S(2)}, u32[]{:S(2)}) collective-permute-start(f32[240,640]{1,0:T(8,128)S(1)} %shard_map.219.a), channel_id=1, source_target_pairs={{8,16},{9,17},{10,18},{11,19},{12,20},{13,21},{14,22},{15,23},{16,... | collective-permute-start | bytes 1843208 | tf_op jit(solution)/shard_map/ppermute | solution.py:842
  205.0 37.3 %collective-permute-start.30 = (f32[240,640]{1,0:T(8,128)S(1)}, f32[240,640]{1,0:T(8,128)S(1)}, u32[]{:S(2)}, u32[]{:S(2)}) collective-permute-start(f32[240,640]{1,0:T(8,128)S(1)} %copy-done.18), channel_id=1, source_target_pairs={{0,8},{1,9},{2,10},{3,11},{4,12},{5,13},{6,14},{7,15},{24,16},{25,... | collective-permute-start | bytes 1843208 | tf_op jit(solution)/shard_map/ppermute | solution.py:842
  228.6 16.0 %collective-permute-start.29 = (f32[240,640]{1,0:T(8,128)S(1)}, f32[240,640]{1,0:T(8,128)S(1)}, u32[]{:S(2)}, u32[]{:S(2)}) collective-permute-start(f32[240,640]{1,0:T(8,128)S(1)} %shard_map.221.a), channel_id=1, source_target_pairs={{8,16},{9,17},{10,18},{11,19},{12,20},{13,21},{14,22},{15,23},{16,... | collective-permute-start | bytes 1843208 | tf_op jit(solution)/shard_map/ppermute | solution.py:842
  238.9 34.2 %collective-permute-start.37 = (f32[328,1024]{1,0:T(8,128)}, f32[328,1024]{1,0:T(8,128)}, u32[]{:S(2)}, u32[]{:S(2)}) collective-permute-start(f32[328,1024]{1,0:T(8,128)} %get-tuple-element.380), channel_id=1, source_target_pairs={{0,4},{1,5},{2,6},{3,7},{4,0},{5,1},{6,2},{7,3},{8,12},{9,13},{10,... | collective-permute-start | bytes 4030472 | tf_op jit(solution)/shard_map/ppermute | solution.py:842
  239.3 17.2 %collective-permute-start.34 = (f32[240,640]{1,0:T(8,128)S(1)}, f32[240,640]{1,0:T(8,128)S(1)}, u32[]{:S(2)}, u32[]{:S(2)}) collective-permute-start(f32[240,640]{1,0:T(8,128)S(1)} %copy-done.17), channel_id=1, source_target_pairs={{0,8},{1,9},{2,10},{3,11},{4,12},{5,13},{6,14},{7,15},{24,16},{25,... | collective-permute-start | bytes 1843208 | tf_op jit(solution)/shard_map/ppermute | solution.py:842
  242.4 15.7 %collective-permute-start.39 = (f32[240,640]{1,0:T(8,128)S(1)}, f32[240,640]{1,0:T(8,128)S(1)}, u32[]{:S(2)}, u32[]{:S(2)}) collective-permute-start(f32[240,640]{1,0:T(8,128)S(1)} %shard_map.224.a), channel_id=1, source_target_pairs={{8,16},{9,17},{10,18},{11,19},{12,20},{13,21},{14,22},{15,23},{16,... | collective-permute-start | bytes 1843208 | tf_op jit(solution)/shard_map/ppermute | solution.py:842
  243.3 18.2 %collective-permute-start.38 = (f32[240,640]{1,0:T(8,128)S(1)}, f32[240,640]{1,0:T(8,128)}, u32[]{:S(2)}, u32[]{:S(2)}) collective-permute-start(f32[240,640]{1,0:T(8,128)S(1)} %shard_map.222.a), channel_id=1, source_target_pairs={{8,0},{9,1},{10,2},{11,3},{12,4},{13,5},{14,6},{15,7},{16,24},{17,... | collective-permute-start | bytes 1843208 | tf_op jit(solution)/shard_map/ppermute | solution.py:842
  244.6 23.5 %collective-permute-start.36 = (f32[240,640]{1,0:T(8,128)}, f32[240,640]{1,0:T(8,128)}, u32[]{:S(2)}, u32[]{:S(2)}) collective-permute-start(f32[240,640]{1,0:T(8,128)} %get-tuple-element.377.a), channel_id=1, source_target_pairs={{0,8},{1,9},{2,10},{3,11},{4,12},{5,13},{6,14},{7,15},{24,16},{25,... | collective-permute-start | bytes 1843208 | tf_op jit(solution)/shard_map/ppermute | solution.py:842
  256.6 15.8 %collective-permute-start.35 = (f32[240,640]{1,0:T(8,128)S(1)}, f32[240,640]{1,0:T(8,128)}, u32[]{:S(2)}, u32[]{:S(2)}) collective-permute-start(f32[240,640]{1,0:T(8,128)S(1)} %shard_map.227.a), channel_id=1, source_target_pairs={{8,16},{9,17},{10,18},{11,19},{12,20},{13,21},{14,22},{15,23},{16,... | collective-permute-start | bytes 1843208 | tf_op jit(solution)/shard_map/ppermute | solution.py:842
  259.0 19.0 %collective-permute-start.33 = (f32[240,640]{1,0:T(8,128)S(1)}, f32[240,640]{1,0:T(8,128)}, u32[]{:S(2)}, u32[]{:S(2)}) collective-permute-start(f32[240,640]{1,0:T(8,128)S(1)} %shard_map.225.a), channel_id=1, source_target_pairs={{8,0},{9,1},{10,2},{11,3},{12,4},{13,5},{14,6},{15,7},{16,24},{17,... | collective-permute-start | bytes 1843208 | tf_op jit(solution)/shard_map/ppermute | solution.py:842
  262.7 20.5 %collective-permute-start.44 = (f32[240,640]{1,0:T(8,128)S(1)}, f32[240,640]{1,0:T(8,128)S(1)}, u32[]{:S(2)}, u32[]{:S(2)}) collective-permute-start(f32[240,640]{1,0:T(8,128)S(1)} %shard_map.229.refs_1_), channel_id=1, source_target_pairs={{0,4},{1,5},{2,6},{3,7},{4,0},{5,1},{6,2},{7,3},{8,12},{9,13},{10,... | collective-permute-start | bytes 1843208 | tf_op jit(solution)/shard_map/ppermute | solution.py:842
  268.0 16.0 %collective-permute-start.43 = (f32[240,640]{1,0:T(8,128)S(1)}, f32[240,640]{1,0:T(8,128)S(1)}, u32[]{:S(2)}, u32[]{:S(2)}) collective-permute-start(f32[240,640]{1,0:T(8,128)S(1)} %copy-done.16), channel_id=1, source_target_pairs={{0,8},{1,9},{2,10},{3,11},{4,12},{5,13},{6,14},{7,15},{24,16},{25,... | collective-permute-start | bytes 1843208 | tf_op jit(solution)/shard_map/ppermute | solution.py:842
  272.5 30.3 %collective-permute-start.32 = (f32[256,1024]{1,0:T(8,128)S(1)}, f32[256,1024]{1,0:T(8,128)S(1)}, u32[]{:S(2)}, u32[]{:S(2)}) collective-permute-start(f32[256,1024]{1,0:T(8,128)S(1)} %shard_map.226.a), channel_id=1, source_target_pairs={{0,2},{1,3},{2,0},{3,1},{4,6},{5,7},{6,4},{7,5},{8,10},{9,11},{10,... | collective-permute-start | bytes 3145736 | tf_op jit(solution)/shard_map/ppermute | solution.py:842
  273.0 15.5 %collective-permute-start.41 = (f32[240,640]{1,0:T(8,128)S(1)}, f32[240,640]{1,0:T(8,128)S(1)}, u32[]{:S(2)}, u32[]{:S(2)}) collective-permute-start(f32[240,640]{1,0:T(8,128)S(1)} %shard_map.228.a), channel_id=1, source_target_pairs={{8,0},{9,1},{10,2},{11,3},{12,4},{13,5},{14,6},{15,7},{16,24},{17,... | collective-permute-start | bytes 1843208 | tf_op jit(solution)/shard_map/ppermute | solution.py:842
  278.0 11.8 %collective-permute-start.42 = (f32[240,640]{1,0:T(8,128)S(1)}, f32[240,640]{1,0:T(8,128)S(1)}, u32[]{:S(2)}, u32[]{:S(2)}) collective-permute-start(f32[240,640]{1,0:T(8,128)S(1)} %shard_map.231.a), channel_id=1, source_target_pairs={{8,16},{9,17},{10,18},{11,19},{12,20},{13,21},{14,22},{15,23},{16,... | collective-permute-start | bytes 1843208 | tf_op jit(solution)/shard_map/ppermute | solution.py:842
  283.2 18.1 %collective-permute-start.40 = (f32[240,640]{1,0:T(8,128)S(1)}, f32[240,640]{1,0:T(8,128)S(1)}, u32[]{:S(2)}, u32[]{:S(2)}) collective-permute-start(f32[240,640]{1,0:T(8,128)S(1)} %shard_map.233.refs_2_), channel_id=1, source_target_pairs={{0,4},{1,5},{2,6},{3,7},{4,0},{5,1},{6,2},{7,3},{8,12},{9,13},{10,... | collective-permute-start | bytes 1843208 | tf_op jit(solution)/shard_map/ppermute | solution.py:842
  284.1 24.4 %collective-permute-start.47 = (f32[240,640]{1,0:T(8,128)S(1)}, f32[240,640]{1,0:T(8,128)S(1)}, u32[]{:S(2)}, u32[]{:S(2)}) collective-permute-start(f32[240,640]{1,0:T(8,128)S(1)} %shard_map.234.a), channel_id=1, source_target_pairs={{8,16},{9,17},{10,18},{11,19},{12,20},{13,21},{14,22},{15,23},{16,... | collective-permute-start | bytes 1843208 | tf_op jit(solution)/shard_map/ppermute | solution.py:842
  288.5 21.3 %collective-permute-start.46 = (f32[240,640]{1,0:T(8,128)S(1)}, f32[240,640]{1,0:T(8,128)S(1)}, u32[]{:S(2)}, u32[]{:S(2)}) collective-permute-start(f32[240,640]{1,0:T(8,128)S(1)} %shard_map.232.a), channel_id=1, source_target_pairs={{8,0},{9,1},{10,2},{11,3},{12,4},{13,5},{14,6},{15,7},{16,24},{17,... | collective-permute-start | bytes 1843208 | tf_op jit(solution)/shard_map/ppermute | solution.py:842
  289.8 17.1 %collective-permute-start.48 = (f32[72,1024]{1,0:T(8,128)S(1)}, f32[72,1024]{1,0:T(8,128)S(1)}, u32[]{:S(2)}, u32[]{:S(2)}) collective-permute-start(f32[72,1024]{1,0:T(8,128)S(1)} %get-tuple-element.396.a), channel_id=1, source_target_pairs={{0,8},{1,9},{2,10},{3,11},{4,12},{5,13},{6,14},{7,15},{24,16},{25,... | collective-permute-start | bytes 884744 | tf_op jit(solution)/shard_map/ppermute | solution.py:842
  302.9 37.2 %collective-permute-start.45 = (f32[256,1024]{1,0:T(8,128)S(1)}, f32[256,1024]{1,0:T(8,128)}, u32[]{:S(2)}, u32[]{:S(2)}) collective-permute-start(f32[256,1024]{1,0:T(8,128)S(1)} %shard_map.237.refs_3_), channel_id=1, source_target_pairs={{0,1},{1,0},{2,3},{3,2},{4,5},{5,4},{6,7},{7,6},{8,9},{9,8},{10,11... | collective-permute-start | bytes 3145736 | tf_op jit(solution)/shard_map/ppermute | solution.py:842
  306.9 16.8 %collective-permute-start.49 = (f32[240,640]{1,0:T(8,128)S(1)}, f32[240,640]{1,0:T(8,128)S(1)}, u32[]{:S(2)}, u32[]{:S(2)}) collective-permute-start(f32[240,640]{1,0:T(8,128)S(1)} %shard_map.236.refs_3_), channel_id=1, source_target_pairs={{0,4},{1,5},{2,6},{3,7},{4,0},{5,1},{6,2},{7,3},{8,12},{9,13},{10,... | collective-permute-start | bytes 1843208 | tf_op jit(solution)/shard_map/ppermute | solution.py:842
  308.5 17.4 %collective-permute-start.51 = (f32[240,640]{1,0:T(8,128)S(1)}, f32[240,640]{1,0:T(8,128)S(1)}, u32[]{:S(2)}, u32[]{:S(2)}) collective-permute-start(f32[240,640]{1,0:T(8,128)S(1)} %shard_map.235.a), channel_id=1, source_target_pairs={{8,0},{9,1},{10,2},{11,3},{12,4},{13,5},{14,6},{15,7},{16,24},{17,... | collective-permute-start | bytes 1843208 | tf_op jit(solution)/shard_map/ppermute | solution.py:842
  312.5 20.7 %collective-permute-start.50 = (f32[240,640]{1,0:T(8,128)S(1)}, f32[240,640]{1,0:T(8,128)S(1)}, u32[]{:S(2)}, u32[]{:S(2)}) collective-permute-start(f32[240,640]{1,0:T(8,128)S(1)} %shard_map.240.refs_4_), channel_id=1, source_target_pairs={{0,4},{1,5},{2,6},{3,7},{4,0},{5,1},{6,2},{7,3},{8,12},{9,13},{10,... | collective-permute-start | bytes 1843208 | tf_op jit(solution)/shard_map/ppermute | solution.py:842
  314.1 30.4 %collective-permute-start.55 = (f32[128,1024]{1,0:T(8,128)}, f32[128,1024]{1,0:T(8,128)S(1)}, u32[]{:S(2)}, u32[]{:S(2)}) collective-permute-start(f32[128,1024]{1,0:T(8,128)} %get-tuple-element.411.a), channel_id=1, source_target_pairs={{0,8},{1,9},{2,10},{3,11},{4,12},{5,13},{6,14},{7,15},{24,16},{25,... | collective-permute-start | bytes 1572872 | tf_op jit(solution)/shard_map/ppermute | solution.py:842
  324.6 21.8 %collective-permute-start.57 = (f32[240,640]{1,0:T(8,128)S(1)}, f32[240,640]{1,0:T(8,128)S(1)}, u32[]{:S(2)}, u32[]{:S(2)}) collective-permute-start(f32[240,640]{1,0:T(8,128)S(1)} %shard_map.239.a), channel_id=1, source_target_pairs={{8,0},{9,1},{10,2},{11,3},{12,4},{13,5},{14,6},{15,7},{16,24},{17,... | collective-permute-start | bytes 1843208 | tf_op jit(solution)/shard_map/ppermute | solution.py:842
  325.9 20.4 %collective-permute-start.54 = (f32[128,1024]{1,0:T(8,128)S(1)}, f32[128,1024]{1,0:T(8,128)S(1)}, u32[]{:S(2)}, u32[]{:S(2)}) collective-permute-start(f32[128,1024]{1,0:T(8,128)S(1)} %shard_map.241.a), channel_id=1, source_target_pairs={{8,16},{9,17},{10,18},{11,19},{12,20},{13,21},{14,22},{15,23},{16,... | collective-permute-start | bytes 1572872 | tf_op jit(solution)/shard_map/ppermute | solution.py:842
  334.1 15.5 %collective-permute-start.58 = (f32[240,640]{1,0:T(8,128)S(1)}, f32[240,640]{1,0:T(8,128)S(1)}, u32[]{:S(2)}, u32[]{:S(2)}) collective-permute-start(f32[240,640]{1,0:T(8,128)S(1)} %shard_map.243.refs_1_), channel_id=1, source_target_pairs={{0,4},{1,5},{2,6},{3,7},{4,0},{5,1},{6,2},{7,3},{8,12},{9,13},{10,... | collective-permute-start | bytes 1843208 | tf_op jit(solution)/shard_map/ppermute | solution.py:842
  346.5 17.4 %collective-permute-start.59 = (f32[240,640]{1,0:T(8,128)S(1)}, f32[240,640]{1,0:T(8,128)}, u32[]{:S(2)}, u32[]{:S(2)}) collective-permute-start(f32[240,640]{1,0:T(8,128)S(1)} %shard_map.248.refs_2_), channel_id=1, source_target_pairs={{0,4},{1,5},{2,6},{3,7},{4,0},{5,1},{6,2},{7,3},{8,12},{9,13},{10,... | collective-permute-start | bytes 1843208 | tf_op jit(solution)/shard_map/ppermute | solution.py:842
  347.0 13.5 %collective-permute-start.60 = (f32[72,1024]{1,0:T(8,128)S(1)}, f32[72,1024]{1,0:T(8,128)S(1)}, u32[]{:S(2)}, u32[]{:S(2)}) collective-permute-start(f32[72,1024]{1,0:T(8,128)S(1)} %shard_map.242.a), channel_id=1, source_target_pairs={{8,0},{9,1},{10,2},{11,3},{12,4},{13,5},{14,6},{15,7},{16,24},{17,... | collective-permute-start | bytes 884744 | tf_op jit(solution)/shard_map/ppermute | solution.py:842
  348.2 20.8 %collective-permute-start.56 = (f32[128,1024]{1,0:T(8,128)S(1)}, f32[128,1024]{1,0:T(8,128)S(1)}, u32[]{:S(2)}, u32[]{:S(2)}) collective-permute-start(f32[128,1024]{1,0:T(8,128)S(1)} %shard_map.247.a), channel_id=1, source_target_pairs={{8,0},{9,1},{10,2},{11,3},{12,4},{13,5},{14,6},{15,7},{16,24},{17,... | collective-permute-start | bytes 1572872 | tf_op jit(solution)/shard_map/ppermute | solution.py:842
  362.5 12.1 %collective-permute-start.62 = (f32[128,1024]{1,0:T(8,128)S(1)}, f32[128,1024]{1,0:T(8,128)S(1)}, u32[]{:S(2)}, u32[]{:S(2)}) collective-permute-start(f32[128,1024]{1,0:T(8,128)S(1)} %shard_map.249.a), channel_id=1, source_target_pairs={{8,0},{9,1},{10,2},{11,3},{12,4},{13,5},{14,6},{15,7},{16,24},{17,... | collective-permute-start | bytes 1572872 | tf_op jit(solution)/shard_map/ppermute | solution.py:842
  374.7 15.0 %collective-permute-start.65 = (f32[128,1024]{1,0:T(8,128)S(1)}, f32[128,1024]{1,0:T(8,128)S(1)}, u32[]{:S(2)}, u32[]{:S(2)}) collective-permute-start(f32[128,1024]{1,0:T(8,128)S(1)} %shard_map.253.refs_2_), channel_id=1, source_target_pairs={{0,4},{1,5},{2,6},{3,7},{4,0},{5,1},{6,2},{7,3},{8,12},{9,13},{10,... | collective-permute-start | bytes 1572872 | tf_op jit(solution)/shard_map/ppermute | solution.py:842
  376.4 13.4 %collective-permute-start.67 = (f32[128,1024]{1,0:T(8,128)S(1)}, f32[128,1024]{1,0:T(8,128)S(1)}, u32[]{:S(2)}, u32[]{:S(2)}) collective-permute-start(f32[128,1024]{1,0:T(8,128)S(1)} %slice.25.refs_5_), channel_id=1, source_target_pairs={{0,1},{1,0},{2,3},{3,2},{4,5},{5,4},{6,7},{7,6},{8,9},{9,8},{10,11... | collective-permute-start | bytes 1572872 | tf_op jit(solution)/shard_map/ppermute | solution.py:842
  (87 other events, 592.0 us)
